TPU v7x, 512 devices: a whole 4x8x8 slice. The times are simulated.
512 devices in a mesh: row: 8 (over y), col: 64 (over x, z, core).
Axes of the slice: x: 4, y: 8, z: 8, core: 2. Of those that a mesh axis runs over, the one named last changes fastest.
Arguments:
- integrals: float32 [2, 16384, 16384], P(None, 'row', 'col'), may hold values from -6 to 6
- coefs: float32 [16384, 1024], P('row', 'col'), may hold values from -0.125 to 0.125
- screen: int32 [128, 128], P('row', 'col'), may hold values from 0 to 1
- domains: int32 [8, 80], replicated, may hold values from 0 to 127, as said below
Outputs:
- pair_ints: float32 [2, 1024, 1024], P(None, 'row', 'col')
Inputs may be any that keep to these rules, and one draw needn't show every extreme that they name: `domains`: each row lists 80 distinct basis tiles, consecutive modulo 128.
All inputs are finite; a program needn't handle non-finite values.
Results may differ from a plain program's by a relative error of at most 0.000098.
Values sent between devices are 32-bit elements; how exact they have to be, the bound alone decides.
No kernel may reach another device: no remote copies, remote signals or barrier semaphores. Data moves between devices by JAX's collectives and lax.ppermute only.
A program may use at most 128 MiB of HBM per device.

v0:
```python
import jax
import jax.numpy as jnp
from jax import lax
from jax.sharding import PartitionSpec as P

TILE = 128


def from_root(value, axis, root):
    mine = lax.axis_index(axis) == root
    return lax.psum(jnp.where(mine, value, jnp.zeros_like(value)), axis)


def mask_block(coef_block, first_tile, domains):
    row_tiles = coef_block.shape[0] // TILE
    occ_tiles = coef_block.shape[1] // TILE
    tile_ids = first_tile + jnp.arange(row_tiles, dtype=jnp.int32)
    in_domain = jnp.any(domains[None, :, :] == tile_ids[:, None, None], axis=2).astype(jnp.float32)
    shaped = coef_block.reshape(row_tiles, TILE, occ_tiles, TILE) * in_domain[:, None, :, None]
    return shaped.reshape(coef_block.shape)


def shards(integrals, coefs, screen, domains):
    aux_count, row_len, col_len = integrals.shape
    row_count = lax.axis_size("row")
    col_count = lax.axis_size("col")
    row_idx = lax.axis_index("row")
    col_idx = lax.axis_index("col")
    pair_keep = screen.astype(jnp.float32)
    screened = (
        integrals.reshape(aux_count, row_len // TILE, TILE, col_len // TILE, TILE)
        * pair_keep[None, :, None, :, None]
    ).reshape(integrals.shape)
    gathered = lax.all_gather(coefs, "col", axis=1, tiled=True)
    gathered = mask_block(gathered, row_idx * (row_len // TILE), domains)
    partial_half = jnp.einsum(
        "pmn,mi->ipn",
        screened,
        gathered,
        precision=lax.Precision.HIGHEST,
        preferred_element_type=jnp.float32,
    )
    half_sum = lax.psum_scatter(partial_half, "row", scatter_dimension=0, tiled=True)
    col_ratio = col_count // row_count
    root_row = col_idx // col_ratio
    offset = col_idx % col_ratio * col_len
    rows_block = lax.dynamic_slice_in_dim(gathered, offset, col_len, 0)
    rows_block = from_root(rows_block, "row", root_row)
    partial_pairs = jnp.einsum(
        "ipn,nj->pij",
        half_sum,
        rows_block,
        precision=lax.Precision.HIGHEST,
        preferred_element_type=jnp.float32,
    )
    return lax.psum_scatter(partial_pairs, "col", scatter_dimension=2, tiled=True)


def solution(mesh):
    placed = (P(None, "row", "col"), P("row", "col"), P("row", "col"), P())
    return jax.shard_map(
        shards, mesh=mesh, in_specs=placed, out_specs=P(None, "row", "col"), check_vma=False
    )
```

profile of v0, /device:TPU:1, one launch (start us, length us, event | category | flops | bytes accessed | tf_op | source)
XLA Modules:
  0.0 403.2 jit_solution(5223739126120643194)
XLA Ops:
  6.5 0.0 all-gather.2.cloned.1.call-start
  6.5 0.7 all-gather.2.cloned.1.call-update
  7.3 0.0 all-reduce.2.cloned.1.call-start
  7.3 1.1 compare_reduce_fusion
  8.5 0.1 copy.8
  8.5 97.9 %all-gather.2.cloned.1.call-done = f32[2048,1024]{0,1:T(8,128)} async-done(((f32[2048,16]{0,1:T(8,128)}), f32[2048,1024]{0,1:T(8,128)}) %all-gather.2.cloned.1.call-update) | async-done | bytes 8388624 | tf_op jit(solution)/shard_map/all_gather | solution.py:34
  106.4 3.8 mul.31
  110.3 0.0 copy-start.1
  110.3 13.7 %bitcast_multiply_fusion = f32[2048,1024]{0,1:T(8,128)} fusion(f32[2048,1024]{0,1:T(8,128)} %all-gather.2.cloned.1.call-done, f32[128,8,16,128]{3,2,1,0:T(8,128)} %bitcast.20), kind=kLoop, calls=%fused_computation | loop fusion | flops 2097152 | bytes 25165824 | tf_op jit(solution)/shard_map/mul | solution.py:19
  124.0 2.3 dynamic-slice_select_fusion
  126.2 0.0 all-reduce.2.cloned.1.call-update
  126.3 0.2 reduce-scatter.3.cloned.1.call-start
  126.5 0.0 copy-done.1
  126.5 0.1 copy.9
  126.6 0.0 copy-start
  126.6 0.6 mul.35
  127.2 0.1 copy.14
  127.3 1.4 copy-done
  128.8 17.0 %fusion = f32[1024,2,256]{2,0,1:T(8,128)} fusion(f32[2048,1024]{0,1:T(8,128)} %bitcast_multiply_fusion, f32[2,2048,256]{2,1,0:T(8,128)S(1)} %copy-done, f32[2048,256]{1,0:T(8,128)S(1)} %bitcast.21), kind=kOutput, calls=%fused_computation.1 | convolution fusion | flops 12885950464 | bytes 16777216 | tf_op jit(solution)/shard_map/pmn,mi->ipn/dot_general | solution.py:36
  145.8 0.0 reduce-scatter.3.cloned.1.call-update
  145.8 0.0 reduce-scatter.5.cloned.1.call-start
  145.9 53.3 %all-reduce.2.cloned.1.call-done = f32[256,1024]{0,1:T(8,128)} async-done(((f32[256,1024]{0,1:T(8,128)}), f32[256,1024]{0,1:T(8,128)}) %all-reduce.2.cloned.1.call-update) | async-done | bytes 1048592 | tf_op jit(solution)/shard_map/psum | solution.py:11
  199.2 46.5 %reduce-scatter.3.cloned.1.call-done = f32[128,2,256]{2,0,1:T(8,128)} async-done(((f32[1024,2,256]{2,0,1:T(8,128)}), f32[128,2,256]{2,0,1:T(8,128)}) %reduce-scatter.3.cloned.1.call-update) | async-done | bytes 262160 | tf_op jit(solution)/shard_map/reduce_scatter | solution.py:43
  245.7 3.3 convolution_bitcast_fusion
  249.0 0.0 reduce-scatter.5.cloned.1.call-update
  249.0 147.7 %reduce-scatter.5.cloned.1.call-done = f32[2,128,16]{1,2,0:T(8,128)} async-done(((f32[2,128,1024]{1,2,0:T(8,128)}), f32[2,128,16]{1,2,0:T(8,128)}) %reduce-scatter.5.cloned.1.call-update) | async-done | bytes 16400 | tf_op jit(solution)/shard_map/reduce_scatter | solution.py:56
  (3 shorter events, 0.0 us)
Async XLA Ops:
  6.5 99.9 %all-gather.2.cloned.1.call-start = ((), (), s32[]{:S(2)}) async-start(), calls=%async_computation.2 | async-start | bytes 8519680 | tf_op jit(solution)/shard_map/all_gather | solution.py:34
  7.3 191.9 %all-reduce.2.cloned.1.call-start = ((), (), s32[]{:S(2)}) async-start(), calls=%async_computation.3 | async-start | bytes 2097152 | tf_op jit(solution)/shard_map/psum | solution.py:11
  110.3 16.2 %copy-start.1 = (s32[16,2]{0,1:T(2,128)S(1)}, s32[16,2]{0,1:T(2,128)}, u32[]{:S(2)}) copy-start(s32[16,2]{0,1:T(2,128)} %param.6) | copy-start | bytes 388
  126.3 119.5 %reduce-scatter.3.cloned.1.call-start = ((), (), s32[]{:S(2)}) async-start(), calls=%async_computation.4 | async-start | bytes 2359296 | tf_op jit(solution)/shard_map/reduce_scatter | solution.py:43
  126.6 2.2 copy-start
  145.8 250.9 %reduce-scatter.5.cloned.1.call-start = ((), (), s32[]{:S(2)}) async-start(), calls=%async_computation.5 | async-start | bytes 1064960 | tf_op jit(solution)/shard_map/reduce_scatter | solution.py:56
Sparse Core Ops, SparseCore 0:
  10.7 95.6 all-gather.1
  126.4 72.7 all-reduce.1
  202.0 43.6 reduce-scatter.2
  250.1 146.4 reduce-scatter.4
where the time goes:
time: 408 us; the launch traced here: 403 us
  waiting for transfers between devices  346 us (85%)
  matrix products  20.3 us (5%)
  other arithmetic  17.1 us (4%)
  between operations  13.2 us (3%)
  local copies, waits for them, and re-layouts  6.17 us (2%)
    reduce_scatter x1, waiting for transfers between devices, shards(): lax.psum_scatter(partial_pairs, 'col', scatter_dimension=2, tiled=True)  148 us
    all_gather x1, waiting for transfers between devices, shards(): gathered = lax.all_gather(coefs, 'col', axis=1, tiled=True)  97.9 us
    psum x1, waiting for transfers between devices, from_root(): return lax.psum(jnp.where(mine, value, jnp.zeros_like(value)), axis)  53.3 us
    reduce_scatter x1, waiting for transfers between devices, shards(): lax.psum_scatter(partial_half, 'row', scatter_dimension=0, tiled=True)  46.5 us
    dot_general x1, matrix products, shards(): jnp.einsum('pmn,mi->ipn', screened, gathered, precision=lax.Precision.HIG...  17 us
    mul x1, other arithmetic, mask_block(): coef_block.reshape(row_tiles, TILE, occ_tiles, TILE)  13.7 us
  transfers between devices with their start and end apart: 4, of which 4 were waited for; matrix products, arithmetic and copies ran while one was open for 5% of the time, Pallas kernels for 0%

commit v1 on v0

v1 whole, which is shorter than its diff:
```python
import jax
import jax.numpy as jnp
from jax import lax
from jax.experimental import pallas as pl
from jax.experimental.pallas import tpu as pltpu
from jax.sharding import Mesh, PartitionSpec as P

TILE = 128
NX, NZ = 4, 8
BF16 = jnp.bfloat16
F32 = jnp.float32


def split(value):
    high = value.astype(BF16)
    return high, (value - high.astype(F32)).astype(BF16)


def swap(value):
    return lax.ppermute(value, "core", [(0, 1), (1, 0)])


def gather(value, axis):
    copies = jnp.broadcast_to(value[None], (lax.axis_size(axis),) + value.shape)
    return lax.all_to_all(copies, axis, 0, 0, tiled=True)


def pieces_kernel(core_ref, own_ref, other_ref, high_ref, low_ref):
    first = core_ref[0] == 0
    own, other = own_ref[0], other_ref[0]
    width = own.shape[1]
    for place, value in enumerate((jnp.where(first, own, other), jnp.where(first, other, own))):
        high, low = split(value)
        high_ref[:, place * width : (place + 1) * width] = high
        low_ref[:, place * width : (place + 1) * width] = low


def pieces(core, own, other):
    aux, rows, width = own.shape
    step = 512
    block = pl.BlockSpec((1, step, width), lambda p, m, core: (p, m, 0))
    out = pl.BlockSpec((step, 2 * width), lambda p, m, core: (m, p))
    shape = jax.ShapeDtypeStruct((rows, aux * 2 * width), BF16)
    return pl.pallas_call(
        pieces_kernel,
        out_shape=(shape, shape),
        grid_spec=pltpu.PrefetchScalarGridSpec(
            num_scalar_prefetch=1,
            grid=(aux, rows // step),
            in_specs=[block, block],
            out_specs=(out, out),
        ),
        compiler_params=pltpu.CompilerParams(vmem_limit_bytes=32 * 2**20),
    )(core, own, other)


def first_kernel(coef_ref, high_ref, low_ref, out_ref, coef_high, coef_low):
    @pl.when(pl.program_id(0) == 0)
    def _():
        high, low = split(coef_ref[...])
        coef_high[...] = high
        coef_low[...] = low

    total = jnp.dot(coef_high[...], low_ref[...], preferred_element_type=F32)
    total += jnp.dot(coef_low[...], high_ref[...], preferred_element_type=F32)
    total += jnp.dot(coef_high[...], high_ref[...], preferred_element_type=F32)
    for z in range(NZ):
        for x in range(NX):
            start = (z * NX + x) * 16
            out_ref[x, z // 4, z % 4] = total[start : start + 16]


def first(coef, high, low):
    occ, depth = coef.shape
    width = high.shape[1]
    step = 256
    piece = pl.BlockSpec((depth, step), lambda n: (0, n))
    return pl.pallas_call(
        first_kernel,
        out_shape=jax.ShapeDtypeStruct((NX, 2, 4, 16, width), F32),
        grid=(width // step,),
        in_specs=[pl.BlockSpec((occ, depth), lambda n: (0, 0)), piece, piece],
        out_specs=pl.BlockSpec((NX, 2, 4, 16, step), lambda n: (0, 0, 0, 0, n)),
        scratch_shapes=[pltpu.VMEM((occ, depth), BF16), pltpu.VMEM((occ, depth), BF16)],
        compiler_params=pltpu.CompilerParams(vmem_limit_bytes=56 * 2**20),
        cost_estimate=pl.CostEstimate(
            flops=6 * occ * depth * width, bytes_accessed=14 * 2**20, transcendentals=0
        ),
    )(coef, high, low)


def second_kernel(rows_ref, half_ref, out_ref):
    half = half_ref[...]
    width = half.shape[1] // 2
    half = jnp.concatenate([half[:, :width], half[:, width:]], axis=0)
    half_high, half_low = split(half)
    rows_high, rows_low = split(rows_ref[...])

    def dot(a, b):
        return lax.dot_general(a, b, (((1,), (1,)), ((), ())), preferred_element_type=F32)

    out_ref[...] = (dot(rows_high, half_low) + dot(rows_low, half_high)) + dot(rows_high, half_high)


def second(rows, half):
    occ = rows.shape[0]
    return pl.pallas_call(
        second_kernel,
        out_shape=jax.ShapeDtypeStruct((occ, 2 * half.shape[0]), F32),
        compiler_params=pltpu.CompilerParams(vmem_limit_bytes=32 * 2**20),
    )(rows, half)


def shards(integrals, coefs, screen, domains):
    aux, row_len, col_len = integrals.shape
    occ = coefs.shape[1]
    row, core = lax.axis_index("y"), lax.axis_index("core")
    col = lax.axis_index(("x", "z", "core"))
    row_tiles = row_len // TILE

    tile_ids = row * row_tiles + jnp.arange(row_tiles, dtype=jnp.int32)
    listed = lax.dynamic_index_in_dim(domains, col * occ // TILE, 0, keepdims=False)
    in_domain = jnp.any(listed[None, :] == tile_ids[:, None], axis=1).astype(F32)
    coef = coefs.T * jnp.repeat(in_domain, TILE)[None, :]

    along_x = gather(coef, "x").reshape(NX * occ, row_len)
    gathered = lax.all_gather(along_x, "z", axis=0, tiled=True)

    keep = screen.astype(F32)
    screened = (
        integrals.reshape(aux, row_tiles, TILE, col_len // TILE, TILE) * keep[None, :, None, :, None]
    ).reshape(integrals.shape)
    high, low = pieces(core[None], screened, swap(screened))

    chip_len = 2 * col_len
    part = lax.all_to_all(coef.reshape(8, occ // 8, row_len), "y", 0, 0, tiled=True)
    part = part.reshape(8, occ // 8, row_len // chip_len, chip_len).transpose(0, 2, 1, 3)
    part = part.reshape(NX * NZ, occ // 8, chip_len)
    part = lax.all_to_all(part, ("x", "z"), 0, 0, tiled=True)
    part = gather(part, "y")
    both = jnp.stack([part, swap(part)])
    both = jnp.where(core == 0, both, both[::-1])
    rows = both.transpose(2, 0, 1, 3, 4).reshape(NX * NZ * 2 * occ, chip_len)

    half = first(gathered, high, low).reshape(NX * NZ * occ, 2 * aux * col_len)
    half = lax.psum_scatter(half, "y", scatter_dimension=0, tiled=True)
    pairs = second(rows, half)
    pairs = pairs.reshape(NX * NZ * 2, occ, pairs.shape[1])
    pairs = lax.all_to_all(pairs, ("x", "z", "core"), 0, 0, tiled=True)
    pairs = pairs.reshape(NX * NZ, 2, occ, aux, 4, occ).sum(axis=0)
    return pairs.transpose(2, 3, 0, 4, 1).reshape(aux, 8 * occ, occ)


def solution(mesh):
    devices = mesh.devices.reshape(8, NX, NZ, 2)
    split_mesh = Mesh(devices, ("y", "x", "z", "core"))
    col = ("x", "z", "core")
    placed = (P(None, "y", col), P("y", col), P("y", col), P())
    return jax.shard_map(
        shards, mesh=split_mesh, in_specs=placed, out_specs=P(None, "y", col), check_vma=False
    )
```

time: 408 us -> 212 us (0.52)
  waiting for transfers between devices: 346 us -> 37.6 us
  blocking collectives: 0 us -> 95.3 us
  matrix products: 20.3 us -> 0 us
  Pallas kernels: 0 us -> 19.5 us
  starting transfers between devices: 0.31 us -> 16.2 us
  local copies, waits for them, and re-layouts: 6.17 us -> 19.9 us
  other arithmetic: 17.1 us -> 8.9 us
    reduce_scatter x2 -> x1, waiting for transfers between devices: 194 us -> 0.02 us  [shards(): half = lax.psum_scatter(half, 'y', scatter_dimension=0, tiled=True)]
    all_to_all x0 -> x4, blocking collectives: none -> 95.3 us  [the longest x2 55.8 us: gather(): return lax.all_to_all(copies, axis, 0, 0, tiled=True)]
    all_gather x1, waiting for transfers between devices: 97.9 us -> 32.9 us  [shards(): gathered = lax.all_gather(along_x, 'z', axis=0, tiled=True)]
    psum x1 -> x0, waiting for transfers between devices: 53.3 us -> none  [from_root(): return lax.psum(jnp.where(mine, value, jnp.zeros_like(value)), axis)]
    dot_general x2 -> x0, matrix products: 20.3 us -> none  [the longest x1 17 us: shards(): jnp.einsum('pmn,mi->ipn', screened, gathered, precision=lax.Precision.HIG...]
    pallas_call x0 -> x3, Pallas kernels: none -> 19.5 us  [the longest x1 12 us: first(): pl.pallas_call(first_kernel, out_shape=jax.ShapeDtypeStruct((NX, 2, 4, 16...]
    ppermute x0 -> x2, starting transfers between devices: none -> 12.2 us  [swap(): return lax.ppermute(value, 'core', [(0, 1), (1, 0)])]
    mul x1 -> x2, other arithmetic: 13.7 us -> 3.3 us  [the longest x1 2.38 us: shards(): integrals.reshape(aux, row_tiles, TILE, col_len // TILE, TILE)]
  transfers between devices with their start and end apart: 4 -> 5, of which waited for: 4 -> 3; matrix products, arithmetic and copies ran while one was open for 5% -> 6% of each run, Pallas kernels for 0% -> 9%
where the time goes in v1:
time: 212 us; the launch traced here: 211 us
  blocking collectives  95.3 us (45%)
  waiting for transfers between devices  37.6 us (18%)
  local copies, waits for them, and re-layouts  19.9 us (9%)
  Pallas kernels  19.5 us (9%)
  starting transfers between devices  16.2 us (8%)
  between operations  13.6 us (6%)
  other arithmetic  8.9 us (4%)
    all_to_all x2, blocking collectives, gather(): return lax.all_to_all(copies, axis, 0, 0, tiled=True)  55.8 us
    all_gather x1, waiting for transfers between devices, shards(): gathered = lax.all_gather(along_x, 'z', axis=0, tiled=True)  32.9 us
    all_to_all x1, blocking collectives, shards(): pairs = lax.all_to_all(pairs, ('x', 'z', 'core'), 0, 0, tiled=True)  23.9 us
    all_to_all x1, blocking collectives, shards(): part = lax.all_to_all(part, ('x', 'z'), 0, 0, tiled=True)  15.6 us
    ppermute x2, starting transfers between devices, swap(): return lax.ppermute(value, 'core', [(0, 1), (1, 0)])  12.2 us
    pallas_call x1, Pallas kernels, first(): pl.pallas_call(first_kernel, out_shape=jax.ShapeDtypeStruct((NX, 2, 4, 16...  12 us
    unnamed x13, local copies, waits for them, and re-layouts  7.73 us
    pallas_call x1, Pallas kernels, pieces(): pl.pallas_call(pieces_kernel, out_shape=(shape, shape), grid_spec=pltpu.P...  6.51 us
  transfers between devices with their start and end apart: 5, of which 3 were waited for; matrix products, arithmetic and copies ran while one was open for 6% of the time, Pallas kernels for 9%

profile of v1, /device:TPU:1, one launch (start us, length us, event | category | flops | bytes accessed | tf_op | source)
XLA Modules:
  0.0 210.9 jit_solution(16416871586169017944)
XLA Ops:
  6.5 0.0 copy-start
  6.5 0.0 copy-start.5
  6.5 0.0 all-gather.2.cloned.1.call-start
  6.6 0.7 copy-done
  7.2 0.2 compare_reduce_fusion
  7.4 0.1 broadcast_bitcast_fusion
  7.5 0.9 multiply_bitcast_fusion
  8.5 11.7 %all_to_all.25 = f32[4,16,2048]{2,1,0:T(8,128)} all-to-all(f32[4,16,2048]{2,1,0:T(8,128)S(1)} %broadcast_in_dim.10), channel_id=1, replica_groups=mesh['y'=8,'x'=4,'z'=8,'core'=2] {'x'}, dimensions={0} | all-to-all | bytes 1048576 | tf_op jit(solution)/shard_map/all_to_all | solution.py:25
  20.1 0.0 all-gather.2.cloned.1.call-update
  20.2 0.0 copy-done.5
  20.2 0.1 copy.15
  20.3 0.6 mul.46
  20.9 0.0 copy-start.4
  20.9 0.1 copy.19
  21.0 2.0 copy-done.4
  23.1 2.4 %broadcast_multiply_fusion.own_ref = f32[2,2048,256]{2,1,0:T(8,128)} fusion(f32[2,2048,256]{2,1,0:T(8,128)S(1)} %copy-done.4, f32[2048,256]{1,0:T(8,128)S(1)} %bitcast.23), kind=kLoop, calls=%fused_computation.4 | loop fusion | flops 1048576 | bytes 10485760 | tf_op jit(solution)/shard_map/mul | solution.py:131
  25.5 8.3 %collective-permute-start.1 = (f32[2,2048,256]{2,1,0:T(8,128)}, f32[2,2048,256]{2,1,0:T(8,128)}, u32[]{:S(2)}, u32[]{:S(2)}) collective-permute-start(f32[2,2048,256]{2,1,0:T(8,128)} %broadcast_multiply_fusion.own_ref), channel_id=1, source_target_pairs={{0,1},{1,0},{2,3},{3,2},{4,5},{5,4},{6,7},{7,6},{8,9},{9,8},{10,11... | collective-permute-start | bytes 12582920 | tf_op jit(solution)/shard_map/ppermute | solution.py:20
  33.7 0.7 reshape.36
  34.5 4.0 %all-to-all-start = ((f32[8,2,2048]{2,1,0:T(2,128)}), f32[8,2,2048]{2,1,0:T(2,128)S(1)}, u32[]{:S(2)}, u32[]{:S(2)}) async-start(f32[8,2,2048]{2,1,0:T(2,128)} %reshape.36), calls=%async_computation | async-start | bytes 262144 | tf_op jit(solution)/shard_map/all_to_all | solution.py:136
  38.4 0.0 reduce-scatter.2.cloned.1.call-start
  38.5 2.4 %collective-permute-done.1.other_ref = f32[2,2048,256]{2,1,0:T(8,128)} collective-permute-done((f32[2,2048,256]{2,1,0:T(8,128)}, f32[2,2048,256]{2,1,0:T(8,128)}, u32[]{:S(2)}, u32[]{:S(2)}) %collective-permute-start.1) | collective-permute-done | bytes 4194336 | tf_op jit(solution)/shard_map/ppermute | solution.py:20
  40.8 6.5 %shard_map.46 = (bf16[2048,1024]{1,0:T(8,128)(2,1)S(1)}, bf16[2048,1024]{1,0:T(8,128)(2,1)S(1)}) custom-call(s32[1]{0:T(128)} %bitcast.7.core_ref, f32[2,2048,256]{2,1,0:T(8,128)} %broadcast_multiply_fusion.own_ref, f32[2,2048,256]{2,1,0:T(8,128)} %collective-permute-done.1.other_ref), custom_call_target="tpu_custom_call" | custom-call | tf_op jit(solution)/shard_map/pallas_call | solution.py:44
  47.3 0.0 copy-start.2
  47.4 2.0 copy-done.2
  49.3 0.0 copy-start.3
  49.3 2.0 copy-done.3
  51.3 32.9 %all-gather.2.cloned.1.call-done.coef_ref = f32[512,2048]{1,0:T(8,128)} async-done(((f32[64,2048]{1,0:T(8,128)}), f32[512,2048]{1,0:T(8,128)}) %all-gather.2.cloned.1.call-update) | async-done | bytes 4194320 | tf_op jit(solution)/shard_map/all_gather | solution.py:127
  84.2 12.0 %shard_map.47 = f32[4,2,4,16,1024]{4,3,2,1,0:T(8,128)} custom-call(f32[512,2048]{1,0:T(8,128)} %all-gather.2.cloned.1.call-done.coef_ref, bf16[2048,1024]{1,0:T(8,128)(2,1)} %copy-done.2, bf16[2048,1024]{1,0:T(8,128)(2,1)} %copy-done.3), custom_call_target="tpu_custom_call" | custom-call | flops 6442450944 | bytes 14680064 | tf_op jit(solution)/shard_map/pallas_call | solution.py:78
  96.2 0.0 reduce-scatter.2.cloned.1.call-update
  96.2 0.0 all-to-all-done
  96.2 0.1 pad_maximum_fusion.1
  96.3 0.1 reshape.37
  96.4 15.6 %all_to_all.26 = f32[32,2,512]{2,1,0:T(2,128)S(1)} all-to-all(f32[32,2,512]{2,1,0:T(2,128)S(1)} %reshape.37), channel_id=1, replica_groups=mesh['y'=8,'x'=4,'z'=8,'core'=2] {'x','z'}, dimensions={0} | all-to-all | bytes 262144 | tf_op jit(solution)/shard_map/all_to_all | solution.py:139
  112.0 0.3 broadcast_in_dim.9
  112.3 44.1 %all_to_all.27 = f32[8,32,2,512]{3,2,1,0:T(2,128)S(1)} all-to-all(f32[8,32,2,512]{3,2,1,0:T(2,128)S(1)} %broadcast_in_dim.9), channel_id=1, replica_groups=mesh['y'=8,'x'=4,'z'=8,'core'=2] {'y'}, dimensions={0} | all-to-all | bytes 2097152 | tf_op jit(solution)/shard_map/all_to_all | solution.py:25
  156.4 3.9 %collective-permute-start = (f32[8,32,2,512]{3,2,1,0:T(2,128)S(1)}, f32[8,32,2,512]{3,2,1,0:T(2,128)S(1)}, u32[]{:S(2)}, u32[]{:S(2)}) collective-permute-start(f32[8,32,2,512]{3,2,1,0:T(2,128)S(1)} %all_to_all.27), channel_id=1, source_target_pairs={{0,1},{1,0},{2,3},{3,2},{4,5},{5,4},{6,7},{7,6},{8,9},{9,8},{10,11... | collective-permute-start | bytes 3145736 | tf_op jit(solution)/shard_map/ppermute | solution.py:20
  160.3 2.3 %collective-permute-done = f32[8,32,2,512]{3,2,1,0:T(2,128)S(1)} collective-permute-done((f32[8,32,2,512]{3,2,1,0:T(2,128)S(1)}, f32[8,32,2,512]{3,2,1,0:T(2,128)S(1)}, u32[]{:S(2)}, u32[]{:S(2)}) %collective-permute-start) | collective-permute-done | bytes 1048608 | tf_op jit(solution)/shard_map/ppermute | solution.py:20
  162.6 1.3 pad_maximum_fusion
  163.9 0.9 fusion
  164.8 2.6 %copy.14 = f32[32,2,8,2,512]{4,3,2,1,0:T(2,128)} copy(f32[32,2,8,2,512]{4,3,0,2,1:T(2,128)S(1)} %fusion) | data formatting | bytes 4194304 | tf_op jit(solution)/shard_map/transpose | solution.py:143
  167.4 2.7 %reshape.38.rows_ref = f32[1024,512]{1,0:T(8,128)S(1)} reshape(f32[32,2,8,2,512]{4,3,2,1,0:T(2,128)} %copy.14) | data formatting | bytes 4194304 | tf_op jit(solution)/shard_map/reshape | solution.py:143
  170.1 0.0 reduce-scatter.2.cloned.1.call-done.half_ref
  170.1 0.0 copy-start.1
  170.1 0.9 copy-done.1
  171.1 1.0 shard_map.48
  172.1 23.9 %all_to_all.28 = f32[64,16,128]{2,1,0:T(8,128)S(1)} all-to-all(f32[64,16,128]{2,1,0:T(8,128)S(1)} %bitcast.22), channel_id=1, replica_groups=mesh['y'=8,'x'=4,'z'=8,'core'=2] {'x','z','core'}, dimensions={0} | all-to-all | bytes 1048576 | tf_op jit(solution)/shard_map/all_to_all | solution.py:149
  195.9 4.1 %reshape.42 = f32[32,2,16,2,4,16]{5,4,3,2,1,0:T(4,128)} reshape(f32[64,16,128]{2,1,0:T(8,128)S(1)} %all_to_all.28) | data formatting | bytes 1048576 | tf_op jit(solution)/shard_map/reshape | solution.py:150
  200.1 3.1 %reduce_sum.9 = f32[2,16,2,4,16]{4,3,2,1,0:T(4,128)S(1)} reduce(f32[32,2,16,2,4,16]{5,4,3,2,1,0:T(4,128)} %reshape.42, f32[]{:T(128)} %constant.47.clone.1), dimensions={0}, to_apply=%region_2.3 | reduce | flops 126976 | bytes 540676 | tf_op jit(solution)/shard_map/reduce_sum | solution.py:150
  203.2 0.1 copy.16
  203.3 0.8 reshape.43
  (6 shorter events, 0.1 us)
Async XLA Ops:
  6.5 0.7 copy-start
  6.5 13.6 %copy-start.5 = (s32[16,2]{0,1:T(2,128)S(1)}, s32[16,2]{0,1:T(2,128)}, u32[]{:S(2)}) copy-start(s32[16,2]{0,1:T(2,128)} %param.6) | copy-start | bytes 388
  6.5 77.7 %all-gather.2.cloned.1.call-start = ((), (), s32[]{:S(2)}) async-start(), calls=%async_computation.6 | async-start | bytes 4718592 | tf_op jit(solution)/shard_map/all_gather | solution.py:127
  20.9 2.2 %copy-start.4 = (f32[2,2048,256]{2,1,0:T(8,128)S(1)}, f32[2,2048,256]{2,1,0:T(8,128)}, u32[]{:S(2)}) copy-start(f32[2,2048,256]{2,1,0:T(8,128)} %param.4) | copy-start | bytes 12582916
  25.5 15.4 %collective-permute-start.1 = (f32[2,2048,256]{2,1,0:T(8,128)}, f32[2,2048,256]{2,1,0:T(8,128)}, u32[]{:S(2)}, u32[]{:S(2)}) collective-permute-start(f32[2,2048,256]{2,1,0:T(8,128)} %broadcast_multiply_fusion.own_ref), channel_id=1, source_target_pairs={{0,1},{1,0},{2,3},{3,2},{4,5},{5,4},{6,7},{7,6},{8,9},{9,8},{10,11... | collective-permute-start | bytes 12582920 | tf_op jit(solution)/shard_map/ppermute | solution.py:20
  34.5 61.8 %all-to-all-start = ((f32[8,2,2048]{2,1,0:T(2,128)}), f32[8,2,2048]{2,1,0:T(2,128)S(1)}, u32[]{:S(2)}, u32[]{:S(2)}) async-start(f32[8,2,2048]{2,1,0:T(2,128)} %reshape.36), calls=%async_computation | async-start | bytes 262144 | tf_op jit(solution)/shard_map/all_to_all | solution.py:136
  38.4 131.7 %reduce-scatter.2.cloned.1.call-start = ((), (), s32[]{:S(2)}) async-start(), calls=%async_computation.7 | async-start | bytes 2359296 | tf_op jit(solution)/shard_map/reduce_scatter | solution.py:146
  47.3 2.0 copy-start.2
  49.3 2.0 copy-start.3
  156.4 6.2 %collective-permute-start = (f32[8,32,2,512]{3,2,1,0:T(2,128)S(1)}, f32[8,32,2,512]{3,2,1,0:T(2,128)S(1)}, u32[]{:S(2)}, u32[]{:S(2)}) collective-permute-start(f32[8,32,2,512]{3,2,1,0:T(2,128)S(1)} %all_to_all.27), channel_id=1, source_target_pairs={{0,1},{1,0},{2,3},{3,2},{4,5},{5,4},{6,7},{7,6},{8,9},{9,8},{10,11... | collective-permute-start | bytes 3145736 | tf_op jit(solution)/shard_map/ppermute | solution.py:20
  170.1 1.0 copy-start.1
Sparse Core Ops, SparseCore 0:
  20.3 63.8 all-gather.1
  96.3 56.7 reduce-scatter.1

commit v2 on v1

--- a/solution.py
+++ b/solution.py
@@ -54,7 +54,8 @@
     )(core, own, other)
 
 
-def first_kernel(coef_ref, high_ref, low_ref, out_ref, coef_high, coef_low):
+def first_kernel(coef_ref, high_ref, low_ref, after_ref, out_ref, coef_high, coef_low):
+    del after_ref
     @pl.when(pl.program_id(0) == 0)
     def _():
         high, low = split(coef_ref[...])
@@ -70,7 +71,7 @@
             out_ref[x, z // 4, z % 4] = total[start : start + 16]
 
 
-def first(coef, high, low):
+def first(coef, high, low, after):
     occ, depth = coef.shape
     width = high.shape[1]
     step = 256
@@ -79,14 +80,19 @@
         first_kernel,
         out_shape=jax.ShapeDtypeStruct((NX, 2, 4, 16, width), F32),
         grid=(width // step,),
-        in_specs=[pl.BlockSpec((occ, depth), lambda n: (0, 0)), piece, piece],
+        in_specs=[
+            pl.BlockSpec((occ, depth), lambda n: (0, 0)),
+            piece,
+            piece,
+            pl.BlockSpec(memory_space=pl.ANY),
+        ],
         out_specs=pl.BlockSpec((NX, 2, 4, 16, step), lambda n: (0, 0, 0, 0, n)),
         scratch_shapes=[pltpu.VMEM((occ, depth), BF16), pltpu.VMEM((occ, depth), BF16)],
         compiler_params=pltpu.CompilerParams(vmem_limit_bytes=56 * 2**20),
         cost_estimate=pl.CostEstimate(
             flops=6 * occ * depth * width, bytes_accessed=14 * 2**20, transcendentals=0
         ),
-    )(coef, high, low)
+    )(coef, high, low, after)
 
 
 def second_kernel(rows_ref, half_ref, out_ref):
@@ -109,6 +115,24 @@
         out_shape=jax.ShapeDtypeStruct((occ, 2 * half.shape[0]), F32),
         compiler_params=pltpu.CompilerParams(vmem_limit_bytes=32 * 2**20),
     )(rows, half)
+
+
+def last_kernel(parts_ref, out_ref):
+    count = parts_ref.shape[0] // 2
+    sums = [parts_ref[core] for core in range(2)]
+    for place in range(1, count):
+        for core in range(2):
+            sums[core] += parts_ref[2 * place + core]
+    for aux in range(2):
+        runs = [sums[core][:, aux * 64 + z * 16 :][:, :16] for z in range(4) for core in range(2)]
+        out_ref[aux] = jnp.concatenate(runs, axis=1)
+
+
+def last(parts):
+    return pl.pallas_call(
+        last_kernel,
+        out_shape=jax.ShapeDtypeStruct((2, parts.shape[1], parts.shape[2]), F32),
+    )(parts)
 
 
 def shards(integrals, coefs, screen, domains):
@@ -137,18 +161,20 @@
     part = part.reshape(8, occ // 8, row_len // chip_len, chip_len).transpose(0, 2, 1, 3)
     part = part.reshape(NX * NZ, occ // 8, chip_len)
     part = lax.all_to_all(part, ("x", "z"), 0, 0, tiled=True)
-    part = gather(part, "y")
-    both = jnp.stack([part, swap(part)])
+    occ_part = occ // 8
+    part = part.reshape(NX * NZ * occ_part, chip_len)
+    mine = lax.all_gather(part, "y", axis=0, tiled=True)
+    both = jnp.stack([mine, swap(mine)])
     both = jnp.where(core == 0, both, both[::-1])
-    rows = both.transpose(2, 0, 1, 3, 4).reshape(NX * NZ * 2 * occ, chip_len)
+    rows = both.reshape(2, 8, NX * NZ, occ_part, chip_len).transpose(2, 0, 1, 3, 4)
+    rows = rows.reshape(NX * NZ * 2 * occ, chip_len)
 
-    half = first(gathered, high, low).reshape(NX * NZ * occ, 2 * aux * col_len)
+    half = first(gathered, high, low, part).reshape(NX * NZ * occ, 2 * aux * col_len)
     half = lax.psum_scatter(half, "y", scatter_dimension=0, tiled=True)
     pairs = second(rows, half)
     pairs = pairs.reshape(NX * NZ * 2, occ, pairs.shape[1])
     pairs = lax.all_to_all(pairs, ("x", "z", "core"), 0, 0, tiled=True)
-    pairs = pairs.reshape(NX * NZ, 2, occ, aux, 4, occ).sum(axis=0)
-    return pairs.transpose(2, 3, 0, 4, 1).reshape(aux, 8 * occ, occ)
+    return last(pairs).transpose(0, 2, 1)
 
 
 def solution(mesh):

time: 212 us -> 213 us (level)
  waiting for transfers between devices: 37.6 us -> 61 us
  blocking collectives: 95.3 us -> 77.5 us
  other arithmetic: 8.9 us -> 5.3 us
    all_to_all x2 -> x1, blocking collectives: 55.8 us -> 11.7 us  [gather(): return lax.all_to_all(copies, axis, 0, 0, tiled=True)]
    reduce_scatter x1, waiting for transfers between devices: 0.02 us -> 25.5 us  [shards(): half = lax.psum_scatter(half, 'y', scatter_dimension=0, tiled=True)]
    all_gather x0 -> x1, waiting for transfers between devices: none -> 24.3 us  [shards(): mine = lax.all_gather(part, 'y', axis=0, tiled=True)]
    all_gather x1, waiting for transfers between devices: 32.9 us -> 8.62 us  [shards(): gathered = lax.all_gather(along_x, 'z', axis=0, tiled=True)]
    all_to_all x0 -> x1, blocking collectives: none -> 12.3 us  [shards(): lax.all_to_all(coef.reshape(8, occ // 8, row_len), 'y', 0, 0, tiled=True)]
    all_to_all x1, blocking collectives: 23.9 us -> 32.8 us  [shards(): pairs = lax.all_to_all(pairs, ('x', 'z', 'core'), 0, 0, tiled=True)]
    all_to_all x1, blocking collectives: 15.6 us -> 20.8 us  [shards(): part = lax.all_to_all(part, ('x', 'z'), 0, 0, tiled=True)]
    all_to_all x1 -> x0, starting transfers between devices: 3.96 us -> none  [shards(): lax.all_to_all(coef.reshape(8, occ // 8, row_len), 'y', 0, 0, tiled=True)]
  transfers between devices with their start and end apart: 5 -> 5, of which waited for: 3 -> 4; matrix products, arithmetic and copies ran while one was open for 6% -> 7% of each run, Pallas kernels for 9% -> 9%
where the time goes in v2:
time: 213 us
  blocking collectives  77.5 us (36%)
  waiting for transfers between devices  61 us (29%)
  Pallas kernels  21.3 us (10%)
  local copies, waits for them, and re-layouts  18.5 us (9%)
  starting transfers between devices  15.7 us (7%)
  between operations  13.3 us (6%)
  other arithmetic  5.3 us (2%)
    all_to_all x1, blocking collectives, shards(): pairs = lax.all_to_all(pairs, ('x', 'z', 'core'), 0, 0, tiled=True)  32.8 us
    reduce_scatter x1, waiting for transfers between devices, shards(): half = lax.psum_scatter(half, 'y', scatter_dimension=0, tiled=True)  25.5 us
    all_gather x1, waiting for transfers between devices, shards(): mine = lax.all_gather(part, 'y', axis=0, tiled=True)  24.3 us
    all_to_all x1, blocking collectives, shards(): part = lax.all_to_all(part, ('x', 'z'), 0, 0, tiled=True)  20.8 us
    ppermute x2, starting transfers between devices, swap(): return lax.ppermute(value, 'core', [(0, 1), (1, 0)])  15.6 us
    all_to_all x1, blocking collectives, shards(): lax.all_to_all(coef.reshape(8, occ // 8, row_len), 'y', 0, 0, tiled=True)  12.3 us
    pallas_call x1, Pallas kernels, first(): pl.pallas_call(first_kernel, out_shape=jax.ShapeDtypeStruct((NX, 2, 4, 16...  12 us
    all_to_all x1, blocking collectives, gather(): return lax.all_to_all(copies, axis, 0, 0, tiled=True)  11.7 us
  transfers between devices with their start and end apart: 5, of which 4 were waited for; matrix products, arithmetic and copies ran while one was open for 7% of the time, Pallas kernels for 9%

profile of v2, /device:TPU:1, one launch (start us, length us, event | category | flops | bytes accessed | tf_op | source)
XLA Modules:
  0.0 212.6 jit_solution(5937136703469079401)
XLA Ops:
  6.5 0.0 copy-start
  6.5 0.0 copy-start.5
  6.5 0.0 all-gather.5.cloned.1.call-start
  6.6 0.7 copy-done
  7.2 0.2 compare_reduce_fusion
  7.4 0.1 broadcast_bitcast_fusion
  7.5 0.9 multiply_bitcast_fusion
  8.5 11.7 %all_to_all.20 = f32[4,16,2048]{2,1,0:T(8,128)} all-to-all(f32[4,16,2048]{2,1,0:T(8,128)S(1)} %broadcast_in_dim.7), channel_id=1, replica_groups=mesh['y'=8,'x'=4,'z'=8,'core'=2] {'x'}, dimensions={0} | all-to-all | bytes 1048576 | tf_op jit(solution)/shard_map/all_to_all | solution.py:25
  20.1 0.0 all-gather.5.cloned.1.call-update
  20.2 0.0 all-gather.3.cloned.1.call-start
  20.2 0.0 copy-done.5
  20.2 0.1 copy.8
  20.3 0.6 mul.46
  20.9 0.0 copy-start.4
  21.0 0.1 copy.12
  21.1 2.0 copy-done.4
  23.1 2.4 %broadcast_multiply_fusion.own_ref = f32[2,2048,256]{2,1,0:T(8,128)} fusion(f32[2,2048,256]{2,1,0:T(8,128)S(1)} %copy-done.4, f32[2048,256]{1,0:T(8,128)S(1)} %bitcast.22), kind=kLoop, calls=%fused_computation.4 | loop fusion | flops 1048576 | bytes 10485760 | tf_op jit(solution)/shard_map/mul | solution.py:155
  25.5 8.3 %collective-permute-start.1 = (f32[2,2048,256]{2,1,0:T(8,128)}, f32[2,2048,256]{2,1,0:T(8,128)}, u32[]{:S(2)}, u32[]{:S(2)}) collective-permute-start(f32[2,2048,256]{2,1,0:T(8,128)} %broadcast_multiply_fusion.own_ref), channel_id=1, source_target_pairs={{0,1},{1,0},{2,3},{3,2},{4,5},{5,4},{6,7},{7,6},{8,9},{9,8},{10,11... | collective-permute-start | bytes 12582920 | tf_op jit(solution)/shard_map/ppermute | solution.py:20
  33.8 0.1 reshape.35
  33.9 12.3 %all_to_all.21 = f32[8,2,2048]{2,1,0:T(2,128)S(1)} all-to-all(f32[8,2,2048]{2,1,0:T(2,128)S(1)} %reshape.35), channel_id=1, replica_groups=mesh['y'=8,'x'=4,'z'=8,'core'=2] {'y'}, dimensions={0} | all-to-all | bytes 262144 | tf_op jit(solution)/shard_map/all_to_all | solution.py:160
  46.1 0.1 pad_maximum_fusion.1
  46.2 0.1 reshape.36
  46.3 20.8 %all_to_all.22 = f32[32,2,512]{2,1,0:T(2,128)S(1)} all-to-all(f32[32,2,512]{2,1,0:T(2,128)S(1)} %reshape.36), channel_id=1, replica_groups=mesh['y'=8,'x'=4,'z'=8,'core'=2] {'x','z'}, dimensions={0} | all-to-all | bytes 262144 | tf_op jit(solution)/shard_map/all_to_all | solution.py:163
  67.1 0.7 reshape.37.after_ref
  67.8 0.0 all-gather.3.cloned.1.call-update
  67.8 0.0 reduce-scatter.2.cloned.1.call-start
  67.9 0.0 collective-permute-done.1.other_ref
  67.9 6.6 %shard_map.46 = (bf16[2048,1024]{1,0:T(8,128)(2,1)S(1)}, bf16[2048,1024]{1,0:T(8,128)(2,1)S(1)}) custom-call(s32[1]{0:T(128)} %bitcast.7.core_ref, f32[2,2048,256]{2,1,0:T(8,128)} %broadcast_multiply_fusion.own_ref, f32[2,2048,256]{2,1,0:T(8,128)} %collective-permute-done.1.other_ref), custom_call_target="tpu_custom_call" | custom-call | tf_op jit(solution)/shard_map/pallas_call | solution.py:44
  74.4 0.0 copy-start.2
  74.5 2.0 copy-done.2
  76.4 0.0 copy-start.3
  76.4 2.0 copy-done.3
  78.4 8.6 %all-gather.5.cloned.1.call-done.coef_ref = f32[512,2048]{1,0:T(8,128)} async-done(((f32[64,2048]{1,0:T(8,128)}), f32[512,2048]{1,0:T(8,128)}) %all-gather.5.cloned.1.call-update) | async-done | bytes 4194320 | tf_op jit(solution)/shard_map/all_gather | solution.py:151
  87.0 12.0 %shard_map.47 = f32[4,2,4,16,1024]{4,3,2,1,0:T(8,128)} custom-call(f32[512,2048]{1,0:T(8,128)} %all-gather.5.cloned.1.call-done.coef_ref, bf16[2048,1024]{1,0:T(8,128)(2,1)} %copy-done.2, bf16[2048,1024]{1,0:T(8,128)(2,1)} %copy-done.3, f32[64,512]{1,0:T(8,128)} %reshape.37.after_ref), custom_call_target="tpu_custom_call" | custom-call | flops 6442450944 | bytes 14680064 | tf_op jit(solution)/shard_map/pallas_call | solution.py:79
  99.0 0.0 reduce-scatter.2.cloned.1.call-update
  99.0 24.3 %all-gather.3.cloned.1.call-done = f32[512,512]{1,0:T(8,128)} async-done(((f32[64,512]{1,0:T(8,128)}), f32[512,512]{1,0:T(8,128)}) %all-gather.3.cloned.1.call-update) | async-done | bytes 1048592 | tf_op jit(solution)/shard_map/all_gather | solution.py:166
  123.3 7.3 %collective-permute-start = (f32[512,512]{1,0:T(8,128)}, f32[512,512]{1,0:T(8,128)S(1)}, u32[]{:S(2)}, u32[]{:S(2)}) collective-permute-start(f32[512,512]{1,0:T(8,128)} %all-gather.3.cloned.1.call-done), channel_id=1, source_target_pairs={{0,1},{1,0},{2,3},{3,2},{4,5},{5,4},{6,7},{7,6},{8,9},{9,8},{10,11... | collective-permute-start | bytes 3145736 | tf_op jit(solution)/shard_map/ppermute | solution.py:20
  130.7 2.5 %collective-permute-done = f32[512,512]{1,0:T(8,128)S(1)} collective-permute-done((f32[512,512]{1,0:T(8,128)}, f32[512,512]{1,0:T(8,128)S(1)}, u32[]{:S(2)}, u32[]{:S(2)}) %collective-permute-start) | collective-permute-done | bytes 1048608 | tf_op jit(solution)/shard_map/ppermute | solution.py:20
  133.1 1.5 pad_maximum_fusion
  134.6 0.2 reverse_select_fusion
  134.9 2.3 %reshape.38 = f32[2,8,32,2,512]{4,3,2,1,0:T(2,128)} reshape(f32[2,512,512]{2,1,0:T(8,128)S(1)} %reverse_select_fusion) | data formatting | bytes 4194304 | tf_op jit(solution)/shard_map/reshape | solution.py:169
  137.2 4.1 %copy.13 = f32[2,8,32,2,512]{4,3,1,0,2:T(2,128)} copy(f32[2,8,32,2,512]{4,3,2,1,0:T(2,128)} %reshape.38) | data formatting | bytes 4194304 | tf_op jit(solution)/shard_map/reshape | solution.py:169
  141.3 2.7 %reshape.39.rows_ref = f32[1024,512]{1,0:T(8,128)S(1)} reshape(f32[32,2,8,2,512]{4,3,2,1,0:T(2,128)} %bitcast.24) | data formatting | bytes 4194304 | tf_op jit(solution)/shard_map/reshape | solution.py:170
  144.0 25.5 %reduce-scatter.2.cloned.1.call-done.half_ref = f32[64,1024]{1,0:T(8,128)} async-done(((f32[512,1024]{1,0:T(8,128)}), f32[64,1024]{1,0:T(8,128)}) %reduce-scatter.2.cloned.1.call-update) | async-done | bytes 262160 | tf_op jit(solution)/shard_map/reduce_scatter | solution.py:173
  169.5 0.0 copy-start.1
  169.5 0.9 copy-done.1
  170.5 1.0 shard_map.48
  171.4 32.8 %all_to_all.23.parts_ref = f32[64,16,128]{2,1,0:T(8,128)} all-to-all(f32[64,16,128]{2,1,0:T(8,128)S(1)} %bitcast.21), channel_id=1, replica_groups=mesh['y'=8,'x'=4,'z'=8,'core'=2] {'x','z','core'}, dimensions={0} | all-to-all | bytes 1048576 | tf_op jit(solution)/shard_map/all_to_all | solution.py:176
  204.3 1.8 shard_map.49
  (6 shorter events, 0.1 us)
Async XLA Ops:
  6.5 0.7 copy-start
  6.5 13.7 %copy-start.5 = (s32[16,2]{0,1:T(2,128)S(1)}, s32[16,2]{0,1:T(2,128)}, u32[]{:S(2)}) copy-start(s32[16,2]{0,1:T(2,128)} %param.6) | copy-start | bytes 388
  6.5 80.5 %all-gather.5.cloned.1.call-start = ((), (), s32[]{:S(2)}) async-start(), calls=%async_computation.6 | async-start | bytes 4718592 | tf_op jit(solution)/shard_map/all_gather | solution.py:151
  20.2 103.2 %all-gather.3.cloned.1.call-start = ((), (), s32[]{:S(2)}) async-start(), calls=%async_computation.5 | async-start | bytes 1179648 | tf_op jit(solution)/shard_map/all_gather | solution.py:166
  20.9 2.2 %copy-start.4 = (f32[2,2048,256]{2,1,0:T(8,128)S(1)}, f32[2,2048,256]{2,1,0:T(8,128)}, u32[]{:S(2)}) copy-start(f32[2,2048,256]{2,1,0:T(8,128)} %param.4) | copy-start | bytes 12582916
  25.5 42.4 %collective-permute-start.1 = (f32[2,2048,256]{2,1,0:T(8,128)}, f32[2,2048,256]{2,1,0:T(8,128)}, u32[]{:S(2)}, u32[]{:S(2)}) collective-permute-start(f32[2,2048,256]{2,1,0:T(8,128)} %broadcast_multiply_fusion.own_ref), channel_id=1, source_target_pairs={{0,1},{1,0},{2,3},{3,2},{4,5},{5,4},{6,7},{7,6},{8,9},{9,8},{10,11... | collective-permute-start | bytes 12582920 | tf_op jit(solution)/shard_map/ppermute | solution.py:20
  67.8 101.7 %reduce-scatter.2.cloned.1.call-start = ((), (), s32[]{:S(2)}) async-start(), calls=%async_computation.7 | async-start | bytes 2359296 | tf_op jit(solution)/shard_map/reduce_scatter | solution.py:173
  74.4 2.0 copy-start.2
  76.4 2.0 copy-start.3
  123.3 9.8 %collective-permute-start = (f32[512,512]{1,0:T(8,128)}, f32[512,512]{1,0:T(8,128)S(1)}, u32[]{:S(2)}, u32[]{:S(2)}) collective-permute-start(f32[512,512]{1,0:T(8,128)} %all-gather.3.cloned.1.call-done), channel_id=1, source_target_pairs={{0,1},{1,0},{2,3},{3,2},{4,5},{5,4},{6,7},{7,6},{8,9},{9,8},{10,11... | collective-permute-start | bytes 3145736 | tf_op jit(solution)/shard_map/ppermute | solution.py:20
  169.5 0.9 copy-start.1
Sparse Core Ops, SparseCore 0:
  20.3 66.6 all-gather.4
  89.1 34.2 all-gather.2
  126.2 43.2 reduce-scatter.1

commit v3 on v2

--- a/solution.py
+++ b/solution.py
@@ -23,6 +23,46 @@
 def gather(value, axis):
     copies = jnp.broadcast_to(value[None], (lax.axis_size(axis),) + value.shape)
     return lax.all_to_all(copies, axis, 0, 0, tiled=True)
+
+
+def around(value, axis):
+    count = lax.axis_size(axis)
+    found = [value] * count
+    for step in range(1, count // 2 + 1):
+        found[step] = lax.ppermute(found[step - 1], axis, [(i, (i - 1) % count) for i in range(count)])
+        if 2 * step < count:
+            back = found[(1 - step) % count]
+            found[-step] = lax.ppermute(back, axis, [(i, (i + 1) % count) for i in range(count)])
+    return found
+
+
+def assemble_kernel(place_ref, own_ref, other_ref, out_ref):
+    row, core = place_ref[0], place_ref[1]
+    count, length, _ = own_ref.shape
+    places = length // 2
+    for source, ref in enumerate((own_ref, other_ref)):
+        which = core if source == 0 else 1 - core
+        for step in range(count):
+            line = lax.rem(row + step, count)
+            for pair in range(2):
+                start = which * 2 * count + line * 2 + pair
+                out_ref[pl.ds(start, places, stride=4 * count), :] = ref[step, pl.ds(pair, places, stride=2), :]
+
+
+def assemble(place, own, other):
+    count, length, width = own.shape
+    block = pl.BlockSpec((count, length, TILE), lambda n, place: (0, 0, n))
+    return pl.pallas_call(
+        assemble_kernel,
+        out_shape=jax.ShapeDtypeStruct((2 * count * length, width), F32),
+        grid_spec=pltpu.PrefetchScalarGridSpec(
+            num_scalar_prefetch=1,
+            grid=(width // TILE,),
+            in_specs=[block, block],
+            out_specs=pl.BlockSpec((2 * count * length, TILE), lambda n, place: (0, n)),
+        ),
+        compiler_params=pltpu.CompilerParams(vmem_limit_bytes=32 * 2**20),
+    )(place, own, other)
 
 
 def pieces_kernel(core_ref, own_ref, other_ref, high_ref, low_ref):
@@ -163,11 +203,8 @@
     part = lax.all_to_all(part, ("x", "z"), 0, 0, tiled=True)
     occ_part = occ // 8
     part = part.reshape(NX * NZ * occ_part, chip_len)
-    mine = lax.all_gather(part, "y", axis=0, tiled=True)
-    both = jnp.stack([mine, swap(mine)])
-    both = jnp.where(core == 0, both, both[::-1])
-    rows = both.reshape(2, 8, NX * NZ, occ_part, chip_len).transpose(2, 0, 1, 3, 4)
-    rows = rows.reshape(NX * NZ * 2 * occ, chip_len)
+    ring = jnp.stack(around(part, "y"))
+    rows = assemble(jnp.stack([row, core]), ring, swap(ring))
 
     half = first(gathered, high, low, part).reshape(NX * NZ * occ, 2 * aux * col_len)
     half = lax.psum_scatter(half, "y", scatter_dimension=0, tiled=True)

time: 213 us -> 183 us (0.86)
  waiting for transfers between devices: 61 us -> 18.6 us
  starting transfers between devices: 15.7 us -> 42.9 us
  local copies, waits for them, and re-layouts: 18.5 us -> 9.02 us
  blocking collectives: 77.5 us -> 69.4 us
  Pallas kernels: 21.3 us -> 24.4 us
    ppermute x0 -> x7, starting transfers between devices: none -> 26.4 us  [the longest x4 20.6 us: around(): lax.ppermute(found[step - 1], axis, [(i, (i - 1) % count) for i in range(...]
    reduce_scatter x1, waiting for transfers between devices: 25.5 us -> 0.02 us  [shards(): half = lax.psum_scatter(half, 'y', scatter_dimension=0, tiled=True)]
    all_gather x1 -> x0, waiting for transfers between devices: 24.3 us -> none  [shards(): mine = lax.all_gather(part, 'y', axis=0, tiled=True)]
    reshape x3 -> x0, local copies, waits for them, and re-layouts: 9.08 us -> none  [the longest x2 6.39 us: shards(): both.reshape(2, 8, NX * NZ, occ_part, chip_len).transpose(2, 0, 1, 3, 4)]
    all_to_all x1, blocking collectives: 32.8 us -> 24.7 us  [shards(): pairs = lax.all_to_all(pairs, ('x', 'z', 'core'), 0, 0, tiled=True)]
    ppermute x0 -> x7, waiting for transfers between devices: none -> 7.67 us  [the longest x4 7.66 us: around(): lax.ppermute(found[step - 1], axis, [(i, (i - 1) % count) for i in range(...]
    pallas_call x0 -> x1, Pallas kernels: none -> 3.13 us  [assemble(): pl.pallas_call(assemble_kernel, out_shape=jax.ShapeDtypeStruct((2 * count...]
    unnamed x13 -> x20, local copies, waits for them, and re-layouts: 7.74 us -> 7.21 us
  transfers between devices with their start and end apart: 5 -> 11, of which waited for: 4 -> 6; matrix products, arithmetic and copies ran while one was open for 7% -> 3% of each run, Pallas kernels for 9% -> 5%
where the time goes in v3:
time: 183 us; the launch traced here: 182 us
  blocking collectives  69.4 us (38%)
  starting transfers between devices  42.9 us (23%)
  Pallas kernels  24.4 us (13%)
  waiting for transfers between devices  18.6 us (10%)
  between operations  13.7 us (7%)
  local copies, waits for them, and re-layouts  9.02 us (5%)
  other arithmetic  4.33 us (2%)
    all_to_all x1, blocking collectives, shards(): pairs = lax.all_to_all(pairs, ('x', 'z', 'core'), 0, 0, tiled=True)  24.7 us
    all_to_all x1, blocking collectives, shards(): part = lax.all_to_all(part, ('x', 'z'), 0, 0, tiled=True)  20.8 us
    ppermute x4, starting transfers between devices, around(): lax.ppermute(found[step - 1], axis, [(i, (i - 1) % count) for i in range(...  20.6 us
    ppermute x2, starting transfers between devices, swap(): return lax.ppermute(value, 'core', [(0, 1), (1, 0)])  16.4 us
    all_to_all x1, blocking collectives, shards(): lax.all_to_all(coef.reshape(8, occ // 8, row_len), 'y', 0, 0, tiled=True)  12.3 us
    pallas_call x1, Pallas kernels, first(): pl.pallas_call(first_kernel, out_shape=jax.ShapeDtypeStruct((NX, 2, 4, 16...  12 us
    all_to_all x1, blocking collectives, gather(): return lax.all_to_all(copies, axis, 0, 0, tiled=True)  11.7 us
    all_gather x1, waiting for transfers between devices, shards(): gathered = lax.all_gather(along_x, 'z', axis=0, tiled=True)  8.72 us
  transfers between devices with their start and end apart: 11, of which 6 were waited for; matrix products, arithmetic and copies ran while one was open for 3% of the time, Pallas kernels for 5%

profile of v3, /device:TPU:1, one launch (start us, length us, event | category | flops | bytes accessed | tf_op | source)
XLA Modules:
  0.0 182.4 jit_solution(4654124992775401401)
XLA Ops:
  6.5 0.0 copy-start
  6.5 0.0 all-gather.2.cloned.1.call-start
  6.5 0.7 copy-done
  7.2 0.2 compare_reduce_fusion
  7.4 0.1 broadcast_bitcast_fusion
  7.5 0.9 multiply_bitcast_fusion
  8.5 11.7 %all_to_all.20 = f32[4,16,2048]{2,1,0:T(8,128)} all-to-all(f32[4,16,2048]{2,1,0:T(8,128)S(1)} %broadcast_in_dim.5), channel_id=1, replica_groups=mesh['y'=8,'x'=4,'z'=8,'core'=2] {'x'}, dimensions={0} | all-to-all | bytes 1048576 | tf_op jit(solution)/shard_map/all_to_all | solution.py:25
  20.1 0.0 all-gather.2.cloned.1.call-update
  20.2 0.0 reduce-scatter.2.cloned.1.call-start
  20.2 0.7 convert_element_type.7
  20.9 0.1 copy.6
  21.0 0.0 copy-start.4
  21.0 0.6 mul.46
  21.6 0.1 copy.9
  21.7 1.4 copy-done.4
  23.2 2.4 %broadcast_multiply_fusion.own_ref = f32[2,2048,256]{2,1,0:T(8,128)} fusion(f32[2,2048,256]{2,1,0:T(8,128)S(1)} %copy-done.4, f32[2048,256]{1,0:T(8,128)S(1)} %bitcast.32), kind=kLoop, calls=%fused_computation.1 | loop fusion | flops 1048576 | bytes 10485760 | tf_op jit(solution)/shard_map/mul | solution.py:195
  25.6 8.3 %collective-permute-start.8 = (f32[2,2048,256]{2,1,0:T(8,128)}, f32[2,2048,256]{2,1,0:T(8,128)}, u32[]{:S(2)}, u32[]{:S(2)}) collective-permute-start(f32[2,2048,256]{2,1,0:T(8,128)} %broadcast_multiply_fusion.own_ref), channel_id=1, source_target_pairs={{0,1},{1,0},{2,3},{3,2},{4,5},{5,4},{6,7},{7,6},{8,9},{9,8},{10,11... | collective-permute-start | bytes 12582920 | tf_op jit(solution)/shard_map/ppermute | solution.py:20
  33.8 0.1 reshape.29
  33.9 12.3 %all_to_all.21 = f32[8,2,2048]{2,1,0:T(2,128)S(1)} all-to-all(f32[8,2,2048]{2,1,0:T(2,128)S(1)} %reshape.29), channel_id=1, replica_groups=mesh['y'=8,'x'=4,'z'=8,'core'=2] {'y'}, dimensions={0} | all-to-all | bytes 262144 | tf_op jit(solution)/shard_map/all_to_all | solution.py:200
  46.2 0.1 pad_maximum_fusion
  46.3 0.1 reshape.30
  46.3 20.8 %all_to_all.22 = f32[32,2,512]{2,1,0:T(2,128)S(1)} all-to-all(f32[32,2,512]{2,1,0:T(2,128)S(1)} %reshape.30), channel_id=1, replica_groups=mesh['y'=8,'x'=4,'z'=8,'core'=2] {'x','z'}, dimensions={0} | all-to-all | bytes 262144 | tf_op jit(solution)/shard_map/all_to_all | solution.py:203
  67.1 0.7 reshape.31.after_ref
  67.8 0.0 collective-permute-done.8.other_ref
  67.8 6.5 %shard_map.47 = (bf16[2048,1024]{1,0:T(8,128)(2,1)S(1)}, bf16[2048,1024]{1,0:T(8,128)(2,1)S(1)}) custom-call(s32[1]{0:T(128)} %bitcast.1.core_ref, f32[2,2048,256]{2,1,0:T(8,128)} %broadcast_multiply_fusion.own_ref, f32[2,2048,256]{2,1,0:T(8,128)} %collective-permute-done.8.other_ref), custom_call_target="tpu_custom_call" | custom-call | tf_op jit(solution)/shard_map/pallas_call | solution.py:84
  74.4 0.0 copy-start.2
  74.4 2.0 %copy-done.2 = bf16[2048,1024]{1,0:T(8,128)(2,1)} copy-done((bf16[2048,1024]{1,0:T(8,128)(2,1)}, bf16[2048,1024]{1,0:T(8,128)(2,1)S(1)}, u32[]{:S(2)}) %copy-start.2) | copy-done | bytes 4194328
  76.4 0.0 copy-start.3
  76.4 2.0 %copy-done.3 = bf16[2048,1024]{1,0:T(8,128)(2,1)} copy-done((bf16[2048,1024]{1,0:T(8,128)(2,1)}, bf16[2048,1024]{1,0:T(8,128)(2,1)S(1)}, u32[]{:S(2)}) %copy-start.3) | copy-done | bytes 4194328
  78.3 8.7 %all-gather.2.cloned.1.call-done.coef_ref = f32[512,2048]{1,0:T(8,128)} async-done(((f32[64,2048]{1,0:T(8,128)}), f32[512,2048]{1,0:T(8,128)}) %all-gather.2.cloned.1.call-update) | async-done | bytes 4194320 | tf_op jit(solution)/shard_map/all_gather | solution.py:191
  87.1 0.0 copy-start.5
  87.1 12.0 %shard_map.48 = f32[4,2,4,16,1024]{4,3,2,1,0:T(8,128)} custom-call(f32[512,2048]{1,0:T(8,128)} %all-gather.2.cloned.1.call-done.coef_ref, bf16[2048,1024]{1,0:T(8,128)(2,1)} %copy-done.2, bf16[2048,1024]{1,0:T(8,128)(2,1)} %copy-done.3, f32[64,512]{1,0:T(8,128)} %reshape.31.after_ref), custom_call_target="tpu_custom_call" | custom-call | flops 6442450944 | bytes 14680064 | tf_op jit(solution)/shard_map/pallas_call | solution.py:119
  99.1 0.0 reduce-scatter.2.cloned.1.call-update
  99.1 0.0 copy-done.5
  99.1 4.5 %collective-permute-start = (f32[64,512]{1,0:T(8,128)S(1)}, f32[64,512]{1,0:T(8,128)S(1)}, u32[]{:S(2)}, u32[]{:S(2)}) collective-permute-start(f32[64,512]{1,0:T(8,128)S(1)} %copy-done.5), channel_id=1, source_target_pairs={{0,448},{64,0},{128,64},{192,128},{256,192},{320,256},{384,320},{4... | collective-permute-start | bytes 393224 | tf_op jit(solution)/shard_map/ppermute | solution.py:32
  103.6 1.9 %collective-permute-start.4 = (f32[64,512]{1,0:T(8,128)S(1)}, f32[64,512]{1,0:T(8,128)S(1)}, u32[]{:S(2)}, u32[]{:S(2)}) collective-permute-start(f32[64,512]{1,0:T(8,128)S(1)} %copy-done.5), channel_id=1, source_target_pairs={{0,64},{64,128},{128,192},{192,256},{256,320},{320,384},{384,448},... | collective-permute-start | bytes 393224 | tf_op jit(solution)/shard_map/ppermute | solution.py:35
  105.5 0.1 stack_reshape.3
  105.6 0.1 collective-permute-done
  105.8 5.3 %collective-permute-start.1 = (f32[64,512]{1,0:T(8,128)S(1)}, f32[64,512]{1,0:T(8,128)S(1)}, u32[]{:S(2)}, u32[]{:S(2)}) collective-permute-start(f32[64,512]{1,0:T(8,128)S(1)} %collective-permute-done), channel_id=1, source_target_pairs={{0,448},{64,0},{128,64},{192,128},{256,192},{320,256},{384,320},{4... | collective-permute-start | bytes 393224 | tf_op jit(solution)/shard_map/ppermute | solution.py:32
  111.1 0.0 collective-permute-done.4
  111.1 1.9 %collective-permute-start.5 = (f32[64,512]{1,0:T(8,128)S(1)}, f32[64,512]{1,0:T(8,128)S(1)}, u32[]{:S(2)}, u32[]{:S(2)}) collective-permute-start(f32[64,512]{1,0:T(8,128)S(1)} %collective-permute-done.4), channel_id=1, source_target_pairs={{0,64},{64,128},{128,192},{192,256},{256,320},{320,384},{384,448},... | collective-permute-start | bytes 393224 | tf_op jit(solution)/shard_map/ppermute | solution.py:35
  113.0 2.3 %collective-permute-done.1 = f32[64,512]{1,0:T(8,128)S(1)} collective-permute-done((f32[64,512]{1,0:T(8,128)S(1)}, f32[64,512]{1,0:T(8,128)S(1)}, u32[]{:S(2)}, u32[]{:S(2)}) %collective-permute-start.1) | collective-permute-done | bytes 131104 | tf_op jit(solution)/shard_map/ppermute | solution.py:32
  115.3 5.4 %collective-permute-start.2 = (f32[64,512]{1,0:T(8,128)S(1)}, f32[64,512]{1,0:T(8,128)S(1)}, u32[]{:S(2)}, u32[]{:S(2)}) collective-permute-start(f32[64,512]{1,0:T(8,128)S(1)} %collective-permute-done.1), channel_id=1, source_target_pairs={{0,448},{64,0},{128,64},{192,128},{256,192},{320,256},{384,320},{4... | collective-permute-start | bytes 393224 | tf_op jit(solution)/shard_map/ppermute | solution.py:32
  120.7 0.0 collective-permute-done.5
  120.7 1.9 %collective-permute-start.6 = (f32[64,512]{1,0:T(8,128)S(1)}, f32[64,512]{1,0:T(8,128)S(1)}, u32[]{:S(2)}, u32[]{:S(2)}) collective-permute-start(f32[64,512]{1,0:T(8,128)S(1)} %collective-permute-done.5), channel_id=1, source_target_pairs={{0,64},{64,128},{128,192},{192,256},{256,320},{320,384},{384,448},... | collective-permute-start | bytes 393224 | tf_op jit(solution)/shard_map/ppermute | solution.py:35
  122.7 1.7 collective-permute-done.2
  124.3 5.4 %collective-permute-start.3 = (f32[64,512]{1,0:T(8,128)S(1)}, f32[64,512]{1,0:T(8,128)S(1)}, u32[]{:S(2)}, u32[]{:S(2)}) collective-permute-start(f32[64,512]{1,0:T(8,128)S(1)} %collective-permute-done.2), channel_id=1, source_target_pairs={{0,448},{64,0},{128,64},{192,128},{256,192},{320,256},{384,320},{4... | collective-permute-start | bytes 393224 | tf_op jit(solution)/shard_map/ppermute | solution.py:32
  129.8 3.6 %collective-permute-done.3 = f32[64,512]{1,0:T(8,128)S(1)} collective-permute-done((f32[64,512]{1,0:T(8,128)S(1)}, f32[64,512]{1,0:T(8,128)S(1)}, u32[]{:S(2)}, u32[]{:S(2)}) %collective-permute-start.3) | collective-permute-done | bytes 131104 | tf_op jit(solution)/shard_map/ppermute | solution.py:32
  133.4 0.0 collective-permute-done.6
  133.5 8.1 %collective-permute-start.7 = (f32[8,64,512]{2,1,0:T(8,128)S(1)}, f32[8,64,512]{2,1,0:T(8,128)S(1)}, u32[]{:S(2)}, u32[]{:S(2)}) collective-permute-start(f32[8,64,512]{2,1,0:T(8,128)S(1)} %bitcast_dynamic-update-slice_fusion.own_ref), channel_id=1, source_target_pairs={{0,1},{1,0},{2,3},{3,2},{4,5},{5,4},{6,7},{7,6},{8,9},{9,8},{10,11... | collective-permute-start | bytes 3145736 | tf_op jit(solution)/shard_map/ppermute | solution.py:20
  141.6 0.1 pad_add_fusion.place_ref
  141.7 2.2 %collective-permute-done.7.other_ref = f32[8,64,512]{2,1,0:T(8,128)S(1)} collective-permute-done((f32[8,64,512]{2,1,0:T(8,128)S(1)}, f32[8,64,512]{2,1,0:T(8,128)S(1)}, u32[]{:S(2)}, u32[]{:S(2)}) %collective-permute-start.7) | collective-permute-done | bytes 1048608 | tf_op jit(solution)/shard_map/ppermute | solution.py:20
  143.9 3.1 %shard_map.46.rows_ref = f32[1024,512]{1,0:T(8,128)S(1)} custom-call(s32[2]{0:T(128)S(1)} %pad_add_fusion.place_ref, f32[8,64,512]{2,1,0:T(8,128)S(1)} %bitcast_dynamic-update-slice_fusion.own_ref, f32[8,64,512]{2,1,0:T(8,128)S(1)} %collective-permute-done.7.other_ref), custom_call_target="tpu_custom_call" | custom-call | tf_op jit(solution)/shard_map/pallas_call | solution.py:55
  147.0 0.0 reduce-scatter.2.cloned.1.call-done.half_ref
  147.1 0.0 copy-start.1
  147.1 0.9 copy-done.1
  148.0 1.0 shard_map.49
  149.0 24.7 %all_to_all.23.parts_ref = f32[64,16,128]{2,1,0:T(8,128)} all-to-all(f32[64,16,128]{2,1,0:T(8,128)S(1)} %bitcast.31), channel_id=1, replica_groups=mesh['y'=8,'x'=4,'z'=8,'core'=2] {'x','z','core'}, dimensions={0} | all-to-all | bytes 1048576 | tf_op jit(solution)/shard_map/all_to_all | solution.py:213
  173.8 1.8 shard_map.50
  (13 shorter events, 0.2 us)
Async XLA Ops:
  6.5 0.7 copy-start
  6.5 80.5 %all-gather.2.cloned.1.call-start = ((), (), s32[]{:S(2)}) async-start(), calls=%async_computation.5 | async-start | bytes 4718592 | tf_op jit(solution)/shard_map/all_gather | solution.py:191
  20.2 126.9 %reduce-scatter.2.cloned.1.call-start = ((), (), s32[]{:S(2)}) async-start(), calls=%async_computation.6 | async-start | bytes 2359296 | tf_op jit(solution)/shard_map/reduce_scatter | solution.py:210
  21.0 2.2 %copy-start.4 = (f32[2,2048,256]{2,1,0:T(8,128)S(1)}, f32[2,2048,256]{2,1,0:T(8,128)}, u32[]{:S(2)}) copy-start(f32[2,2048,256]{2,1,0:T(8,128)} %param.4) | copy-start | bytes 12582916
  25.6 42.3 %collective-permute-start.8 = (f32[2,2048,256]{2,1,0:T(8,128)}, f32[2,2048,256]{2,1,0:T(8,128)}, u32[]{:S(2)}, u32[]{:S(2)}) collective-permute-start(f32[2,2048,256]{2,1,0:T(8,128)} %broadcast_multiply_fusion.own_ref), channel_id=1, source_target_pairs={{0,1},{1,0},{2,3},{3,2},{4,5},{5,4},{6,7},{7,6},{8,9},{9,8},{10,11... | collective-permute-start | bytes 12582920 | tf_op jit(solution)/shard_map/ppermute | solution.py:20
  74.4 2.0 %copy-start.2 = (bf16[2048,1024]{1,0:T(8,128)(2,1)}, bf16[2048,1024]{1,0:T(8,128)(2,1)S(1)}, u32[]{:S(2)}) copy-start(bf16[2048,1024]{1,0:T(8,128)(2,1)S(1)} %get-tuple-element.7.high_ref) | copy-start | bytes 12582916
  76.4 2.0 %copy-start.3 = (bf16[2048,1024]{1,0:T(8,128)(2,1)}, bf16[2048,1024]{1,0:T(8,128)(2,1)S(1)}, u32[]{:S(2)}) copy-start(bf16[2048,1024]{1,0:T(8,128)(2,1)S(1)} %get-tuple-element.8.low_ref) | copy-start | bytes 12582916
  87.1 12.0 %copy-start.5 = (f32[64,512]{1,0:T(8,128)S(1)}, f32[64,512]{1,0:T(8,128)}, u32[]{:S(2)}) copy-start(f32[64,512]{1,0:T(8,128)} %reshape.31.after_ref) | copy-start | bytes 393220
  99.1 6.7 %collective-permute-start = (f32[64,512]{1,0:T(8,128)S(1)}, f32[64,512]{1,0:T(8,128)S(1)}, u32[]{:S(2)}, u32[]{:S(2)}) collective-permute-start(f32[64,512]{1,0:T(8,128)S(1)} %copy-done.5), channel_id=1, source_target_pairs={{0,448},{64,0},{128,64},{192,128},{256,192},{320,256},{384,320},{4... | collective-permute-start | bytes 393224 | tf_op jit(solution)/shard_map/ppermute | solution.py:32
  103.6 7.5 %collective-permute-start.4 = (f32[64,512]{1,0:T(8,128)S(1)}, f32[64,512]{1,0:T(8,128)S(1)}, u32[]{:S(2)}, u32[]{:S(2)}) collective-permute-start(f32[64,512]{1,0:T(8,128)S(1)} %copy-done.5), channel_id=1, source_target_pairs={{0,64},{64,128},{128,192},{192,256},{256,320},{320,384},{384,448},... | collective-permute-start | bytes 393224 | tf_op jit(solution)/shard_map/ppermute | solution.py:35
  105.8 9.5 %collective-permute-start.1 = (f32[64,512]{1,0:T(8,128)S(1)}, f32[64,512]{1,0:T(8,128)S(1)}, u32[]{:S(2)}, u32[]{:S(2)}) collective-permute-start(f32[64,512]{1,0:T(8,128)S(1)} %collective-permute-done), channel_id=1, source_target_pairs={{0,448},{64,0},{128,64},{192,128},{256,192},{320,256},{384,320},{4... | collective-permute-start | bytes 393224 | tf_op jit(solution)/shard_map/ppermute | solution.py:32
  111.1 9.6 %collective-permute-start.5 = (f32[64,512]{1,0:T(8,128)S(1)}, f32[64,512]{1,0:T(8,128)S(1)}, u32[]{:S(2)}, u32[]{:S(2)}) collective-permute-start(f32[64,512]{1,0:T(8,128)S(1)} %collective-permute-done.4), channel_id=1, source_target_pairs={{0,64},{64,128},{128,192},{192,256},{256,320},{320,384},{384,448},... | collective-permute-start | bytes 393224 | tf_op jit(solution)/shard_map/ppermute | solution.py:35
  115.3 9.0 %collective-permute-start.2 = (f32[64,512]{1,0:T(8,128)S(1)}, f32[64,512]{1,0:T(8,128)S(1)}, u32[]{:S(2)}, u32[]{:S(2)}) collective-permute-start(f32[64,512]{1,0:T(8,128)S(1)} %collective-permute-done.1), channel_id=1, source_target_pairs={{0,448},{64,0},{128,64},{192,128},{256,192},{320,256},{384,320},{4... | collective-permute-start | bytes 393224 | tf_op jit(solution)/shard_map/ppermute | solution.py:32
  120.7 12.7 %collective-permute-start.6 = (f32[64,512]{1,0:T(8,128)S(1)}, f32[64,512]{1,0:T(8,128)S(1)}, u32[]{:S(2)}, u32[]{:S(2)}) collective-permute-start(f32[64,512]{1,0:T(8,128)S(1)} %collective-permute-done.5), channel_id=1, source_target_pairs={{0,64},{64,128},{128,192},{192,256},{256,320},{320,384},{384,448},... | collective-permute-start | bytes 393224 | tf_op jit(solution)/shard_map/ppermute | solution.py:35
  124.3 9.1 %collective-permute-start.3 = (f32[64,512]{1,0:T(8,128)S(1)}, f32[64,512]{1,0:T(8,128)S(1)}, u32[]{:S(2)}, u32[]{:S(2)}) collective-permute-start(f32[64,512]{1,0:T(8,128)S(1)} %collective-permute-done.2), channel_id=1, source_target_pairs={{0,448},{64,0},{128,64},{192,128},{256,192},{320,256},{384,320},{4... | collective-permute-start | bytes 393224 | tf_op jit(solution)/shard_map/ppermute | solution.py:32
  133.5 10.4 %collective-permute-start.7 = (f32[8,64,512]{2,1,0:T(8,128)S(1)}, f32[8,64,512]{2,1,0:T(8,128)S(1)}, u32[]{:S(2)}, u32[]{:S(2)}) collective-permute-start(f32[8,64,512]{2,1,0:T(8,128)S(1)} %bitcast_dynamic-update-slice_fusion.own_ref), channel_id=1, source_target_pairs={{0,1},{1,0},{2,3},{3,2},{4,5},{5,4},{6,7},{7,6},{8,9},{9,8},{10,11... | collective-permute-start | bytes 3145736 | tf_op jit(solution)/shard_map/ppermute | solution.py:20
  147.1 1.0 copy-start.1
Sparse Core Ops, SparseCore 0:
  20.3 66.7 all-gather.1
  99.2 43.1 reduce-scatter.1

commit v4 on v2

--- a/solution.py
+++ b/solution.py
@@ -50,71 +50,89 @@
             in_specs=[block, block],
             out_specs=(out, out),
         ),
-        compiler_params=pltpu.CompilerParams(vmem_limit_bytes=32 * 2**20),
+        compiler_params=pltpu.CompilerParams(vmem_limit_bytes=56 * 2**20),
     )(core, own, other)
 
 
-def first_kernel(coef_ref, high_ref, low_ref, after_ref, out_ref, coef_high, coef_low):
-    del after_ref
-    @pl.when(pl.program_id(0) == 0)
+def first_kernel(coef_ref, high_ref, low_ref, passed_ref, out_ref, passed_out_ref, total):
+    del passed_ref, passed_out_ref
+    step = pl.program_id(0)
+    coef_high, coef_low = split(coef_ref[...])
+    part = jnp.dot(coef_high, low_ref[...], preferred_element_type=F32)
+    part += jnp.dot(coef_low, high_ref[...], preferred_element_type=F32)
+    part += jnp.dot(coef_high, high_ref[...], preferred_element_type=F32)
+
+    @pl.when(step == 0)
     def _():
-        high, low = split(coef_ref[...])
-        coef_high[...] = high
-        coef_low[...] = low
-
-    total = jnp.dot(coef_high[...], low_ref[...], preferred_element_type=F32)
-    total += jnp.dot(coef_low[...], high_ref[...], preferred_element_type=F32)
-    total += jnp.dot(coef_high[...], high_ref[...], preferred_element_type=F32)
-    for z in range(NZ):
-        for x in range(NX):
-            start = (z * NX + x) * 16
-            out_ref[x, z // 4, z % 4] = total[start : start + 16]
-
-
-def first(coef, high, low, after):
+        total[...] = part
+
+    @pl.when(step > 0)
+    def _():
+        total[...] += part
+
+    @pl.when(step == pl.num_programs(0) - 1)
+    def _():
+        for z in range(NZ):
+            for x in range(NX):
+                start = (z * NX + x) * 16
+                out_ref[x, z // 4, z % 4] = total[start : start + 16]
+
+
+def first(coef, high, low, passed):
     occ, depth = coef.shape
     width = high.shape[1]
-    step = 256
-    piece = pl.BlockSpec((depth, step), lambda n: (0, n))
+    step = 512
+    piece = pl.BlockSpec((step, width), lambda k: (k, 0))
     return pl.pallas_call(
         first_kernel,
-        out_shape=jax.ShapeDtypeStruct((NX, 2, 4, 16, width), F32),
-        grid=(width // step,),
+        out_shape=(
+            jax.ShapeDtypeStruct((NX, 2, 4, 16, width), F32),
+            jax.ShapeDtypeStruct(passed.shape, passed.dtype),
+        ),
+        grid=(depth // step,),
         in_specs=[
-            pl.BlockSpec((occ, depth), lambda n: (0, 0)),
+            pl.BlockSpec((occ, step), lambda k: (0, k)),
             piece,
             piece,
             pl.BlockSpec(memory_space=pl.ANY),
         ],
-        out_specs=pl.BlockSpec((NX, 2, 4, 16, step), lambda n: (0, 0, 0, 0, n)),
-        scratch_shapes=[pltpu.VMEM((occ, depth), BF16), pltpu.VMEM((occ, depth), BF16)],
+        out_specs=(
+            pl.BlockSpec((NX, 2, 4, 16, width), lambda k: (0, 0, 0, 0, 0)),
+            pl.BlockSpec(memory_space=pl.ANY),
+        ),
+        input_output_aliases={3: 1},
+        scratch_shapes=[pltpu.VMEM((occ, width), F32)],
         compiler_params=pltpu.CompilerParams(vmem_limit_bytes=56 * 2**20),
         cost_estimate=pl.CostEstimate(
             flops=6 * occ * depth * width, bytes_accessed=14 * 2**20, transcendentals=0
         ),
-    )(coef, high, low, after)
-
-
-def second_kernel(rows_ref, half_ref, out_ref):
+    )(coef, high, low, passed)
+
+
+def second_kernel(core_ref, own_ref, other_ref, half_ref, out_ref):
+    core = core_ref[0]
     half = half_ref[...]
     width = half.shape[1] // 2
     half = jnp.concatenate([half[:, :width], half[:, width:]], axis=0)
     half_high, half_low = split(half)
-    rows_high, rows_low = split(rows_ref[...])
 
     def dot(a, b):
         return lax.dot_general(a, b, (((1,), (1,)), ((), ())), preferred_element_type=F32)
 
-    out_ref[...] = (dot(rows_high, half_low) + dot(rows_low, half_high)) + dot(rows_high, half_high)
-
-
-def second(rows, half):
-    occ = rows.shape[0]
+    for which, ref in ((core, own_ref), (1 - core, other_ref)):
+        high, low = split(ref[...])
+        part = (dot(high, half_low) + dot(low, half_high)) + dot(high, half_high)
+        out_ref[:, pl.ds(which, 1)] = part.reshape(NX * NZ, 1, 16, part.shape[1])
+
+
+def second(core, own, other, half):
+    vmem = pl.BlockSpec(memory_space=pltpu.VMEM)
     return pl.pallas_call(
         second_kernel,
-        out_shape=jax.ShapeDtypeStruct((occ, 2 * half.shape[0]), F32),
+        out_shape=jax.ShapeDtypeStruct((NX * NZ, 2, 16, 2 * half.shape[0]), F32),
+        in_specs=[pl.BlockSpec(memory_space=pltpu.SMEM), vmem, vmem, vmem],
         compiler_params=pltpu.CompilerParams(vmem_limit_bytes=32 * 2**20),
-    )(rows, half)
+    )(core, own, other, half)
 
 
 def last_kernel(parts_ref, out_ref):
@@ -147,8 +165,8 @@
     in_domain = jnp.any(listed[None, :] == tile_ids[:, None], axis=1).astype(F32)
     coef = coefs.T * jnp.repeat(in_domain, TILE)[None, :]
 
-    along_x = gather(coef, "x").reshape(NX * occ, row_len)
-    gathered = lax.all_gather(along_x, "z", axis=0, tiled=True)
+    along_x = gather(coef, "x")
+    gathered = lax.all_gather(along_x.reshape(NX * occ, row_len), "z", axis=0, tiled=True)
 
     keep = screen.astype(F32)
     screened = (
@@ -157,22 +175,17 @@
     high, low = pieces(core[None], screened, swap(screened))
 
     chip_len = 2 * col_len
-    part = lax.all_to_all(coef.reshape(8, occ // 8, row_len), "y", 0, 0, tiled=True)
-    part = part.reshape(8, occ // 8, row_len // chip_len, chip_len).transpose(0, 2, 1, 3)
-    part = part.reshape(NX * NZ, occ // 8, chip_len)
-    part = lax.all_to_all(part, ("x", "z"), 0, 0, tiled=True)
-    occ_part = occ // 8
-    part = part.reshape(NX * NZ * occ_part, chip_len)
-    mine = lax.all_gather(part, "y", axis=0, tiled=True)
-    both = jnp.stack([mine, swap(mine)])
-    both = jnp.where(core == 0, both, both[::-1])
-    rows = both.reshape(2, 8, NX * NZ, occ_part, chip_len).transpose(2, 0, 1, 3, 4)
-    rows = rows.reshape(NX * NZ * 2 * occ, chip_len)
-
-    half = first(gathered, high, low, part).reshape(NX * NZ * occ, 2 * aux * col_len)
+    mine = lax.dynamic_index_in_dim(along_x, lax.axis_index("x"), 0, keepdims=False)
+    along_y = gather(mine, "y").reshape(8, occ, row_len // chip_len, chip_len)
+    along_y = along_y.transpose(0, 2, 1, 3).reshape(NX * NZ, occ, chip_len)
+
+    half, along_y = first(gathered, high, low, along_y)
+    half = half.reshape(NX * NZ * occ, 2 * aux * col_len)
     half = lax.psum_scatter(half, "y", scatter_dimension=0, tiled=True)
-    pairs = second(rows, half)
-    pairs = pairs.reshape(NX * NZ * 2, occ, pairs.shape[1])
+
+    rows = lax.all_to_all(along_y, ("x", "z"), 0, 0, tiled=True).reshape(NX * NZ * occ, chip_len)
+    pairs = second(core[None], rows, swap(rows), half)
+    pairs = pairs.reshape(NX * NZ * 2, occ, pairs.shape[3])
     pairs = lax.all_to_all(pairs, ("x", "z", "core"), 0, 0, tiled=True)
     return last(pairs).transpose(0, 2, 1)
 

time: 213 us -> 178 us (0.84)
  waiting for transfers between devices: 61 us -> 8.31 us
  blocking collectives: 77.5 us -> 107 us
  local copies, waits for them, and re-layouts: 18.5 us -> 5.1 us
    all_to_all x1 -> x2, blocking collectives: 11.7 us -> 44.6 us  [gather(): return lax.all_to_all(copies, axis, 0, 0, tiled=True)]
    all_gather x2 -> x1, waiting for transfers between devices: 33 us -> 6.01 us  [shards(): lax.all_gather(along_x.reshape(NX * occ, row_len), 'z', axis=0, tiled=True)]
    reduce_scatter x1, waiting for transfers between devices: 25.5 us -> 0.01 us  [shards(): half = lax.psum_scatter(half, 'y', scatter_dimension=0, tiled=True)]
    reshape x6 -> x0, local copies, waits for them, and re-layouts: 9.97 us -> none  [the longest x2 6.39 us: shards(): both.reshape(2, 8, NX * NZ, occ_part, chip_len).transpose(2, 0, 1, 3, 4)]
    unnamed x13 -> x7, local copies, waits for them, and re-layouts: 7.74 us -> 3.2 us
    pallas_call x1, Pallas kernels: 6.57 us -> 9.32 us  [pieces(): pl.pallas_call(pieces_kernel, out_shape=(shape, shape), grid_spec=pltpu.P...]
    all_to_all x2 -> x1, blocking collectives: 33 us -> 31.3 us  [shards(): lax.all_to_all(along_y, ('x', 'z'), 0, 0, tiled=True)]
  transfers between devices with their start and end apart: 5 -> 4, of which waited for: 4 -> 2; matrix products, arithmetic and copies ran while one was open for 7% -> 3% of each run, Pallas kernels for 9% -> 5%
where the time goes in v4:
time: 178 us; the launch traced here: 177 us
  blocking collectives  107 us (60%)
  Pallas kernels  23.4 us (13%)
  starting transfers between devices  15.2 us (9%)
  between operations  13.5 us (8%)
  waiting for transfers between devices  8.31 us (5%)
  other arithmetic  5.17 us (3%)
  local copies, waits for them, and re-layouts  5.1 us (3%)
    all_to_all x2, blocking collectives, gather(): return lax.all_to_all(copies, axis, 0, 0, tiled=True)  44.6 us
    all_to_all x1, blocking collectives, shards(): lax.all_to_all(along_y, ('x', 'z'), 0, 0, tiled=True)  31.3 us
    all_to_all x1, blocking collectives, shards(): pairs = lax.all_to_all(pairs, ('x', 'z', 'core'), 0, 0, tiled=True)  30.7 us
    ppermute x2, starting transfers between devices, swap(): return lax.ppermute(value, 'core', [(0, 1), (1, 0)])  15.2 us
    pallas_call x1, Pallas kernels, first(): pl.pallas_call(first_kernel, out_shape=(jax.ShapeDtypeStruct((NX, 2, 4, 1...  11.3 us
    pallas_call x1, Pallas kernels, pieces(): pl.pallas_call(pieces_kernel, out_shape=(shape, shape), grid_spec=pltpu.P...  9.32 us
    all_gather x1, waiting for transfers between devices, shards(): lax.all_gather(along_x.reshape(NX * occ, row_len), 'z', axis=0, tiled=True)  6.01 us
  transfers between devices with their start and end apart: 4, of which 2 were waited for; matrix products, arithmetic and copies ran while one was open for 3% of the time, Pallas kernels for 5%

profile of v4, /device:TPU:1, one launch (start us, length us, event | category | flops | bytes accessed | tf_op | source)
XLA Modules:
  0.0 177.4 jit_solution(17726952642758155352)
XLA Ops:
  6.5 0.0 copy-start
  6.5 0.0 all-gather.2.cloned.1.call-start
  6.5 0.7 copy-done
  7.2 0.2 compare_reduce_fusion
  7.4 0.1 broadcast_bitcast_fusion
  7.5 0.9 multiply_bitcast_fusion
  8.5 11.7 %all_to_all.20 = f32[4,16,2048]{2,1,0:T(8,128)} all-to-all(f32[4,16,2048]{2,1,0:T(8,128)S(1)} %broadcast_in_dim.12), channel_id=1, replica_groups=mesh['y'=8,'x'=4,'z'=8,'core'=2] {'x'}, dimensions={0} | all-to-all | bytes 1048576 | tf_op jit(solution)/shard_map/all_to_all | solution.py:25
  20.1 0.0 all-gather.2.cloned.1.call-update
  20.2 0.0 reduce-scatter.2.cloned.1.call-start
  20.2 0.7 convert_element_type.7
  20.9 0.1 copy.7
  21.0 0.0 copy-start.2
  21.0 0.6 mul.46
  21.6 0.1 copy.10
  21.7 1.4 copy-done.2
  23.2 2.3 %broadcast_multiply_fusion.own_ref = f32[2,2048,256]{2,1,0:T(8,128)} fusion(f32[2,2048,256]{2,1,0:T(8,128)S(1)} %copy-done.2, f32[2048,256]{1,0:T(8,128)S(1)} %bitcast.23), kind=kLoop, calls=%fused_computation.1 | loop fusion | flops 1048576 | bytes 10485760 | tf_op jit(solution)/shard_map/mul | solution.py:173
  25.5 8.3 %collective-permute-start = (f32[2,2048,256]{2,1,0:T(8,128)}, f32[2,2048,256]{2,1,0:T(8,128)}, u32[]{:S(2)}, u32[]{:S(2)}) collective-permute-start(f32[2,2048,256]{2,1,0:T(8,128)} %broadcast_multiply_fusion.own_ref), channel_id=1, source_target_pairs={{0,1},{1,0},{2,3},{3,2},{4,5},{5,4},{6,7},{7,6},{8,9},{9,8},{10,11... | collective-permute-start | bytes 12582920 | tf_op jit(solution)/shard_map/ppermute | solution.py:20
  33.8 0.9 dynamic-slice_bitcast_fusion
  34.7 0.1 broadcast_in_dim.28
  34.8 32.9 %all_to_all.21 = f32[8,16,2048]{2,1,0:T(8,128)S(1)} all-to-all(f32[8,16,2048]{2,1,0:T(8,128)S(1)} %broadcast_in_dim.28), channel_id=1, replica_groups=mesh['y'=8,'x'=4,'z'=8,'core'=2] {'y'}, dimensions={0} | all-to-all | bytes 2097152 | tf_op jit(solution)/shard_map/all_to_all | solution.py:25
  67.8 0.1 fusion
  67.9 1.0 pad_maximum_fusion
  68.9 0.0 collective-permute-done.other_ref
  68.9 9.3 %shard_map.46 = (bf16[2048,1024]{1,0:T(8,128)(2,1)}, bf16[2048,1024]{1,0:T(8,128)(2,1)}) custom-call(s32[1]{0:T(128)} %bitcast.core_ref, f32[2,2048,256]{2,1,0:T(8,128)} %broadcast_multiply_fusion.own_ref, f32[2,2048,256]{2,1,0:T(8,128)} %collective-permute-done.other_ref), custom_call_target="tpu_custom_call" | custom-call | tf_op jit(solution)/shard_map/pallas_call | solution.py:44
  78.2 6.0 %all-gather.2.cloned.1.call-done.coef_ref = f32[512,2048]{1,0:T(8,128)} async-done(((f32[64,2048]{1,0:T(8,128)}), f32[512,2048]{1,0:T(8,128)}) %all-gather.2.cloned.1.call-update) | async-done | bytes 4194320 | tf_op jit(solution)/shard_map/all_gather | solution.py:169
  84.2 11.3 %shard_map.47 = (f32[4,2,4,16,1024]{4,3,2,1,0:T(8,128)}, f32[32,16,512]{2,1,0:T(8,128)}) custom-call(f32[512,2048]{1,0:T(8,128)} %all-gather.2.cloned.1.call-done.coef_ref, bf16[2048,1024]{1,0:T(8,128)(2,1)} %get-tuple-element.9.high_ref, bf16[2048,1024]{1,0:T(8,128)(2,1)} %get-tuple-element.10.low_ref, ...), custom_call_target="tpu_custom_call", output_to_operand_aliasing={{1}: (3, {})} | custom-call | flops 6442450944 | bytes 14680064 | tf_op jit(solution)/shard_map/pallas_call | solution.py:86
  95.6 0.0 reduce-scatter.2.cloned.1.call-update
  95.6 31.3 %all_to_all.22 = f32[32,16,512]{2,1,0:T(8,128)S(1)} all-to-all(f32[32,16,512]{2,1,0:T(8,128)} %get-tuple-element.11), channel_id=1, replica_groups=mesh['y'=8,'x'=4,'z'=8,'core'=2] {'x','z'}, dimensions={0} | all-to-all | bytes 2097152 | tf_op jit(solution)/shard_map/all_to_all | solution.py:186
  126.9 6.9 %collective-permute-start.1 = (f32[512,512]{1,0:T(8,128)S(1)}, f32[512,512]{1,0:T(8,128)S(1)}, u32[]{:S(2)}, u32[]{:S(2)}) collective-permute-start(f32[512,512]{1,0:T(8,128)S(1)} %bitcast.20), channel_id=1, source_target_pairs={{0,1},{1,0},{2,3},{3,2},{4,5},{5,4},{6,7},{7,6},{8,9},{9,8},{10,11... | collective-permute-start | bytes 3145736 | tf_op jit(solution)/shard_map/ppermute | solution.py:20
  133.8 2.3 %collective-permute-done.1.other_ref = f32[512,512]{1,0:T(8,128)S(1)} collective-permute-done((f32[512,512]{1,0:T(8,128)S(1)}, f32[512,512]{1,0:T(8,128)S(1)}, u32[]{:S(2)}, u32[]{:S(2)}) %collective-permute-start.1) | collective-permute-done | bytes 1048608 | tf_op jit(solution)/shard_map/ppermute | solution.py:20
  136.0 0.0 reduce-scatter.2.cloned.1.call-done.half_ref
  136.0 0.0 copy-start.1
  136.0 0.9 copy-done.1
  137.0 1.0 shard_map.48
  138.0 30.7 %all_to_all.23.parts_ref = f32[64,16,128]{2,1,0:T(8,128)} all-to-all(f32[64,16,128]{2,1,0:T(8,128)S(1)} %bitcast.22), channel_id=1, replica_groups=mesh['y'=8,'x'=4,'z'=8,'core'=2] {'x','z','core'}, dimensions={0} | all-to-all | bytes 1048576 | tf_op jit(solution)/shard_map/all_to_all | solution.py:189
  168.7 1.8 %shard_map.49 = f32[2,16,128]{2,1,0:T(8,128)} custom-call(f32[64,16,128]{2,1,0:T(8,128)} %all_to_all.23.parts_ref), custom_call_target="tpu_custom_call" | custom-call | tf_op jit(solution)/shard_map/pallas_call | solution.py:150
  (4 shorter events, 0.1 us)
Async XLA Ops:
  6.5 0.7 copy-start
  6.5 77.7 %all-gather.2.cloned.1.call-start = ((), (), s32[]{:S(2)}) async-start(), calls=%async_computation.5 | async-start | bytes 4718592 | tf_op jit(solution)/shard_map/all_gather | solution.py:169
  20.2 115.9 %reduce-scatter.2.cloned.1.call-start = ((), (), s32[]{:S(2)}) async-start(), calls=%async_computation.6 | async-start | bytes 2359296 | tf_op jit(solution)/shard_map/reduce_scatter | solution.py:184
  21.0 2.2 %copy-start.2 = (f32[2,2048,256]{2,1,0:T(8,128)S(1)}, f32[2,2048,256]{2,1,0:T(8,128)}, u32[]{:S(2)}) copy-start(f32[2,2048,256]{2,1,0:T(8,128)} %param.4) | copy-start | bytes 12582916
  25.5 43.4 %collective-permute-start = (f32[2,2048,256]{2,1,0:T(8,128)}, f32[2,2048,256]{2,1,0:T(8,128)}, u32[]{:S(2)}, u32[]{:S(2)}) collective-permute-start(f32[2,2048,256]{2,1,0:T(8,128)} %broadcast_multiply_fusion.own_ref), channel_id=1, source_target_pairs={{0,1},{1,0},{2,3},{3,2},{4,5},{5,4},{6,7},{7,6},{8,9},{9,8},{10,11... | collective-permute-start | bytes 12582920 | tf_op jit(solution)/shard_map/ppermute | solution.py:20
  126.9 9.1 %collective-permute-start.1 = (f32[512,512]{1,0:T(8,128)S(1)}, f32[512,512]{1,0:T(8,128)S(1)}, u32[]{:S(2)}, u32[]{:S(2)}) collective-permute-start(f32[512,512]{1,0:T(8,128)S(1)} %bitcast.20), channel_id=1, source_target_pairs={{0,1},{1,0},{2,3},{3,2},{4,5},{5,4},{6,7},{7,6},{8,9},{9,8},{10,11... | collective-permute-start | bytes 3145736 | tf_op jit(solution)/shard_map/ppermute | solution.py:20
  136.0 1.0 copy-start.1
Sparse Core Ops, SparseCore 0:
  20.3 63.9 all-gather.1
  95.7 38.5 reduce-scatter.1

commit v5 on v4

--- a/solution.py
+++ b/solution.py
@@ -25,50 +25,24 @@
     return lax.all_to_all(copies, axis, 0, 0, tiled=True)
 
 
-def pieces_kernel(core_ref, own_ref, other_ref, high_ref, low_ref):
-    first = core_ref[0] == 0
-    own, other = own_ref[0], other_ref[0]
-    width = own.shape[1]
-    for place, value in enumerate((jnp.where(first, own, other), jnp.where(first, other, own))):
-        high, low = split(value)
-        high_ref[:, place * width : (place + 1) * width] = high
-        low_ref[:, place * width : (place + 1) * width] = low
-
-
-def pieces(core, own, other):
-    aux, rows, width = own.shape
-    step = 512
-    block = pl.BlockSpec((1, step, width), lambda p, m, core: (p, m, 0))
-    out = pl.BlockSpec((step, 2 * width), lambda p, m, core: (m, p))
-    shape = jax.ShapeDtypeStruct((rows, aux * 2 * width), BF16)
-    return pl.pallas_call(
-        pieces_kernel,
-        out_shape=(shape, shape),
-        grid_spec=pltpu.PrefetchScalarGridSpec(
-            num_scalar_prefetch=1,
-            grid=(aux, rows // step),
-            in_specs=[block, block],
-            out_specs=(out, out),
-        ),
-        compiler_params=pltpu.CompilerParams(vmem_limit_bytes=56 * 2**20),
-    )(core, own, other)
-
-
-def first_kernel(coef_ref, high_ref, low_ref, passed_ref, out_ref, passed_out_ref, total):
+def first_kernel(coef_ref, own_ref, other_ref, passed_ref, out_ref, passed_out_ref, total):
     del passed_ref, passed_out_ref
     step = pl.program_id(0)
+    aux, _, width = own_ref.shape
     coef_high, coef_low = split(coef_ref[...])
-    part = jnp.dot(coef_high, low_ref[...], preferred_element_type=F32)
-    part += jnp.dot(coef_low, high_ref[...], preferred_element_type=F32)
-    part += jnp.dot(coef_high, high_ref[...], preferred_element_type=F32)
 
     @pl.when(step == 0)
     def _():
-        total[...] = part
+        total[...] = jnp.zeros_like(total)
 
-    @pl.when(step > 0)
-    def _():
-        total[...] += part
+    for p in range(aux):
+        for place, ref in enumerate((own_ref, other_ref)):
+            high, low = split(ref[p])
+            part = jnp.dot(coef_high, low, preferred_element_type=F32)
+            part += jnp.dot(coef_low, high, preferred_element_type=F32)
+            part += jnp.dot(coef_high, high, preferred_element_type=F32)
+            start = (2 * p + place) * width
+            total[:, start : start + width] += part
 
     @pl.when(step == pl.num_programs(0) - 1)
     def _():
@@ -78,11 +52,12 @@
                 out_ref[x, z // 4, z % 4] = total[start : start + 16]
 
 
-def first(coef, high, low, passed):
+def first(coef, own, other, passed):
     occ, depth = coef.shape
-    width = high.shape[1]
+    aux, _, half_width = own.shape
+    width = 2 * aux * half_width
     step = 512
-    piece = pl.BlockSpec((step, width), lambda k: (k, 0))
+    block = pl.BlockSpec((aux, step, half_width), lambda k: (0, k, 0))
     return pl.pallas_call(
         first_kernel,
         out_shape=(
@@ -92,8 +67,8 @@
         grid=(depth // step,),
         in_specs=[
             pl.BlockSpec((occ, step), lambda k: (0, k)),
-            piece,
-            piece,
+            block,
+            block,
             pl.BlockSpec(memory_space=pl.ANY),
         ],
         out_specs=(
@@ -106,14 +81,18 @@
         cost_estimate=pl.CostEstimate(
             flops=6 * occ * depth * width, bytes_accessed=14 * 2**20, transcendentals=0
         ),
-    )(coef, high, low, passed)
+    )(coef, own, other, passed)
 
 
 def second_kernel(core_ref, own_ref, other_ref, half_ref, out_ref):
     core = core_ref[0]
     half = half_ref[...]
-    width = half.shape[1] // 2
-    half = jnp.concatenate([half[:, :width], half[:, width:]], axis=0)
+    width = half.shape[1] // 4
+    own, other = (
+        jnp.concatenate([half[:, n * width : (n + 1) * width] for n in (place, place + 2)], axis=0)
+        for place in range(2)
+    )
+    half = jnp.concatenate([jnp.where(core == 0, own, other), jnp.where(core == 0, other, own)], axis=1)
     half_high, half_low = split(half)
 
     def dot(a, b):
@@ -172,21 +151,22 @@
     screened = (
         integrals.reshape(aux, row_tiles, TILE, col_len // TILE, TILE) * keep[None, :, None, :, None]
     ).reshape(integrals.shape)
-    high, low = pieces(core[None], screened, swap(screened))
+    other = swap(screened)
 
     chip_len = 2 * col_len
     mine = lax.dynamic_index_in_dim(along_x, lax.axis_index("x"), 0, keepdims=False)
     along_y = gather(mine, "y").reshape(8, occ, row_len // chip_len, chip_len)
     along_y = along_y.transpose(0, 2, 1, 3).reshape(NX * NZ, occ, chip_len)
 
-    half, along_y = first(gathered, high, low, along_y)
+    half, along_y = first(gathered, screened, other, along_y)
     half = half.reshape(NX * NZ * occ, 2 * aux * col_len)
     half = lax.psum_scatter(half, "y", scatter_dimension=0, tiled=True)
 
     rows = lax.all_to_all(along_y, ("x", "z"), 0, 0, tiled=True).reshape(NX * NZ * occ, chip_len)
     pairs = second(core[None], rows, swap(rows), half)
-    pairs = pairs.reshape(NX * NZ * 2, occ, pairs.shape[3])
-    pairs = lax.all_to_all(pairs, ("x", "z", "core"), 0, 0, tiled=True)
+    pairs = pairs.reshape(NX, NZ * 2, occ, pairs.shape[3])
+    pairs = lax.all_to_all(pairs, "x", 0, 0, tiled=True).sum(axis=0)
+    pairs = lax.all_to_all(pairs, ("z", "core"), 0, 0, tiled=True)
     return last(pairs).transpose(0, 2, 1)
 
 

time: 178 us -> 179 us (level)
  waiting for transfers between devices: 8.31 us -> 17.6 us
  Pallas kernels: 23.4 us -> 14.2 us
    pallas_call x1 -> x0, Pallas kernels: 9.32 us -> none  [pieces(): pl.pallas_call(pieces_kernel, out_shape=(shape, shape), grid_spec=pltpu.P...]
    all_gather x1, waiting for transfers between devices: 6.01 us -> 15.3 us  [shards(): lax.all_gather(along_x.reshape(NX * occ, row_len), 'z', axis=0, tiled=True)]
    all_to_all x1 -> x2, blocking collectives: 30.7 us -> 31.5 us  [the longest x1 22.2 us: shards(): pairs = lax.all_to_all(pairs, ('z', 'core'), 0, 0, tiled=True)]
  transfers between devices with their start and end apart: 4 -> 4, of which waited for: 2 -> 2; matrix products, arithmetic and copies ran while one was open for 3% -> 3% of each run, Pallas kernels for 5% -> 0%
where the time goes in v5:
time: 179 us; the launch traced here: 178 us
  blocking collectives  107 us (60%)
  waiting for transfers between devices  17.6 us (10%)
  starting transfers between devices  15.2 us (8%)
  Pallas kernels  14.2 us (8%)
  between operations  13.5 us (8%)
  other arithmetic  5.27 us (3%)
  local copies, waits for them, and re-layouts  5.1 us (3%)
    all_to_all x2, blocking collectives, gather(): return lax.all_to_all(copies, axis, 0, 0, tiled=True)  44.7 us
    all_to_all x1, blocking collectives, shards(): lax.all_to_all(along_y, ('x', 'z'), 0, 0, tiled=True)  31.3 us
    all_to_all x1, blocking collectives, shards(): pairs = lax.all_to_all(pairs, ('z', 'core'), 0, 0, tiled=True)  22.2 us
    all_gather x1, waiting for transfers between devices, shards(): lax.all_gather(along_x.reshape(NX * occ, row_len), 'z', axis=0, tiled=True)  15.3 us
    ppermute x2, starting transfers between devices, swap(): return lax.ppermute(value, 'core', [(0, 1), (1, 0)])  15.1 us
    pallas_call x1, Pallas kernels, first(): pl.pallas_call(first_kernel, out_shape=(jax.ShapeDtypeStruct((NX, 2, 4, 1...  11.6 us
    all_to_all x1, blocking collectives, shards(): pairs = lax.all_to_all(pairs, 'x', 0, 0, tiled=True).sum(axis=0)  9.33 us
  transfers between devices with their start and end apart: 4, of which 2 were waited for; matrix products, arithmetic and copies ran while one was open for 3% of the time, Pallas kernels for 0%

profile of v5, /device:TPU:1, one launch (start us, length us, event | category | flops | bytes accessed | tf_op | source)
XLA Modules:
  0.0 178.3 jit_solution(1959163798303209597)
XLA Ops:
  6.5 0.0 copy-start
  6.5 0.0 all-gather.2.cloned.1.call-start
  6.5 0.7 copy-done
  7.2 0.2 compare_reduce_fusion
  7.4 0.1 broadcast_bitcast_fusion
  7.5 0.9 multiply_bitcast_fusion
  8.5 11.7 %all_to_all.25 = f32[4,16,2048]{2,1,0:T(8,128)} all-to-all(f32[4,16,2048]{2,1,0:T(8,128)S(1)} %broadcast_in_dim.12), channel_id=1, replica_groups=mesh['y'=8,'x'=4,'z'=8,'core'=2] {'x'}, dimensions={0} | all-to-all | bytes 1048576 | tf_op jit(solution)/shard_map/all_to_all | solution.py:25
  20.1 0.0 all-gather.2.cloned.1.call-update
  20.2 0.0 reduce-scatter.2.cloned.1.call-start
  20.2 0.7 convert_element_type.7
  20.9 0.1 copy.7
  21.0 0.0 copy-start.2
  21.0 0.6 mul.46
  21.6 0.1 copy.10
  21.7 1.4 copy-done.2
  23.2 2.4 %broadcast_multiply_fusion.own_ref = f32[2,2048,256]{2,1,0:T(8,128)} fusion(f32[2,2048,256]{2,1,0:T(8,128)S(1)} %copy-done.2, f32[2048,256]{1,0:T(8,128)S(1)} %bitcast.23), kind=kLoop, calls=%fused_computation.1 | loop fusion | flops 1048576 | bytes 10485760 | tf_op jit(solution)/shard_map/mul | solution.py:152
  25.5 8.3 %collective-permute-start = (f32[2,2048,256]{2,1,0:T(8,128)}, f32[2,2048,256]{2,1,0:T(8,128)}, u32[]{:S(2)}, u32[]{:S(2)}) collective-permute-start(f32[2,2048,256]{2,1,0:T(8,128)} %broadcast_multiply_fusion.own_ref), channel_id=1, source_target_pairs={{0,1},{1,0},{2,3},{3,2},{4,5},{5,4},{6,7},{7,6},{8,9},{9,8},{10,11... | collective-permute-start | bytes 12582920 | tf_op jit(solution)/shard_map/ppermute | solution.py:20
  33.8 0.9 dynamic-slice_bitcast_fusion
  34.7 0.1 broadcast_in_dim.27
  34.8 33.0 %all_to_all.26 = f32[8,16,2048]{2,1,0:T(8,128)S(1)} all-to-all(f32[8,16,2048]{2,1,0:T(8,128)S(1)} %broadcast_in_dim.27), channel_id=1, replica_groups=mesh['y'=8,'x'=4,'z'=8,'core'=2] {'y'}, dimensions={0} | all-to-all | bytes 2097152 | tf_op jit(solution)/shard_map/all_to_all | solution.py:25
  67.8 0.1 fusion
  67.9 1.1 pad_maximum_fusion
  69.0 0.0 collective-permute-done.other_ref
  69.0 15.3 %all-gather.2.cloned.1.call-done.coef_ref = f32[512,2048]{1,0:T(8,128)} async-done(((f32[64,2048]{1,0:T(8,128)}), f32[512,2048]{1,0:T(8,128)}) %all-gather.2.cloned.1.call-update) | async-done | bytes 4194320 | tf_op jit(solution)/shard_map/all_gather | solution.py:148
  84.2 11.6 %shard_map.46 = (f32[4,2,4,16,1024]{4,3,2,1,0:T(8,128)}, f32[32,16,512]{2,1,0:T(8,128)}) custom-call(f32[512,2048]{1,0:T(8,128)} %all-gather.2.cloned.1.call-done.coef_ref, f32[2,2048,256]{2,1,0:T(8,128)} %broadcast_multiply_fusion.own_ref, f32[2,2048,256]{2,1,0:T(8,128)} %collective-permute-done.other_ref, ...), custom_call_target="tpu_custom_call", output_to_operand_aliasing={{1}: (3, {})} | custom-call | flops 6442450944 | bytes 14680064 | tf_op jit(solution)/shard_map/pallas_call | solution.py:61
  95.9 0.0 reduce-scatter.2.cloned.1.call-update
  95.9 31.3 %all_to_all.27 = f32[32,16,512]{2,1,0:T(8,128)S(1)} all-to-all(f32[32,16,512]{2,1,0:T(8,128)} %get-tuple-element.7), channel_id=1, replica_groups=mesh['y'=8,'x'=4,'z'=8,'core'=2] {'x','z'}, dimensions={0} | all-to-all | bytes 2097152 | tf_op jit(solution)/shard_map/all_to_all | solution.py:165
  127.2 6.9 %collective-permute-start.1 = (f32[512,512]{1,0:T(8,128)S(1)}, f32[512,512]{1,0:T(8,128)S(1)}, u32[]{:S(2)}, u32[]{:S(2)}) collective-permute-start(f32[512,512]{1,0:T(8,128)S(1)} %bitcast.20), channel_id=1, source_target_pairs={{0,1},{1,0},{2,3},{3,2},{4,5},{5,4},{6,7},{7,6},{8,9},{9,8},{10,11... | collective-permute-start | bytes 3145736 | tf_op jit(solution)/shard_map/ppermute | solution.py:20
  134.1 2.3 %collective-permute-done.1.other_ref = f32[512,512]{1,0:T(8,128)S(1)} collective-permute-done((f32[512,512]{1,0:T(8,128)S(1)}, f32[512,512]{1,0:T(8,128)S(1)}, u32[]{:S(2)}, u32[]{:S(2)}) %collective-permute-start.1) | collective-permute-done | bytes 1048608 | tf_op jit(solution)/shard_map/ppermute | solution.py:20
  136.3 0.0 reduce-scatter.2.cloned.1.call-done.half_ref
  136.3 0.0 copy-start.1
  136.3 0.9 copy-done.1
  137.3 1.0 shard_map.47
  138.3 9.3 %all_to_all.28 = f32[4,16,16,128]{3,2,1,0:T(8,128)S(1)} all-to-all(f32[4,16,16,128]{3,2,1,0:T(8,128)S(1)} %bitcast.22), channel_id=1, replica_groups=mesh['y'=8,'x'=4,'z'=8,'core'=2] {'x'}, dimensions={0} | all-to-all | bytes 1048576 | tf_op jit(solution)/shard_map/all_to_all | solution.py:168
  147.7 22.2 %all_to_all.29.parts_ref = f32[16,16,128]{2,1,0:T(8,128)} all-to-all(f32[16,16,128]{2,1,0:T(8,128)S(1)} %reduce_sum.9), channel_id=1, replica_groups=mesh['y'=8,'x'=4,'z'=8,'core'=2] {'z','core'}, dimensions={0} | all-to-all | bytes 262144 | tf_op jit(solution)/shard_map/all_to_all | solution.py:169
  169.9 1.6 shard_map.48
  (5 shorter events, 0.1 us)
Async XLA Ops:
  6.5 0.7 copy-start
  6.5 77.7 %all-gather.2.cloned.1.call-start = ((), (), s32[]{:S(2)}) async-start(), calls=%async_computation.6 | async-start | bytes 4718592 | tf_op jit(solution)/shard_map/all_gather | solution.py:148
  20.2 116.1 %reduce-scatter.2.cloned.1.call-start = ((), (), s32[]{:S(2)}) async-start(), calls=%async_computation.7 | async-start | bytes 2359296 | tf_op jit(solution)/shard_map/reduce_scatter | solution.py:163
  21.0 2.2 %copy-start.2 = (f32[2,2048,256]{2,1,0:T(8,128)S(1)}, f32[2,2048,256]{2,1,0:T(8,128)}, u32[]{:S(2)}) copy-start(f32[2,2048,256]{2,1,0:T(8,128)} %param.4) | copy-start | bytes 12582916
  25.5 43.4 %collective-permute-start = (f32[2,2048,256]{2,1,0:T(8,128)}, f32[2,2048,256]{2,1,0:T(8,128)}, u32[]{:S(2)}, u32[]{:S(2)}) collective-permute-start(f32[2,2048,256]{2,1,0:T(8,128)} %broadcast_multiply_fusion.own_ref), channel_id=1, source_target_pairs={{0,1},{1,0},{2,3},{3,2},{4,5},{5,4},{6,7},{7,6},{8,9},{9,8},{10,11... | collective-permute-start | bytes 12582920 | tf_op jit(solution)/shard_map/ppermute | solution.py:20
  127.2 9.1 %collective-permute-start.1 = (f32[512,512]{1,0:T(8,128)S(1)}, f32[512,512]{1,0:T(8,128)S(1)}, u32[]{:S(2)}, u32[]{:S(2)}) collective-permute-start(f32[512,512]{1,0:T(8,128)S(1)} %bitcast.20), channel_id=1, source_target_pairs={{0,1},{1,0},{2,3},{3,2},{4,5},{5,4},{6,7},{7,6},{8,9},{9,8},{10,11... | collective-permute-start | bytes 3145736 | tf_op jit(solution)/shard_map/ppermute | solution.py:20
  136.3 1.0 copy-start.1
Sparse Core Ops, SparseCore 0:
  20.3 63.9 all-gather.1
  96.0 38.6 reduce-scatter.1

commit v6 on v5

--- a/solution.py
+++ b/solution.py
@@ -84,58 +84,53 @@
     )(coef, own, other, passed)
 
 
-def second_kernel(core_ref, own_ref, other_ref, half_ref, out_ref):
-    core = core_ref[0]
-    half = half_ref[...]
-    width = half.shape[1] // 4
-    own, other = (
-        jnp.concatenate([half[:, n * width : (n + 1) * width] for n in (place, place + 2)], axis=0)
-        for place in range(2)
-    )
-    half = jnp.concatenate([jnp.where(core == 0, own, other), jnp.where(core == 0, other, own)], axis=1)
+def second_kernel(rows_ref, halves_ref, out_ref):
+    width = halves_ref.shape[2] // 4
+
+    def nus(p, z, source):
+        pair = halves_ref[source, z * 16 : z * 16 + 16, 2 * p * width : 2 * (p + 1) * width]
+        return pair if source == 0 else jnp.concatenate([pair[:, width:], pair[:, :width]], axis=1)
+
+    half = jnp.concatenate([nus(p, z, c) for p in range(2) for z in range(4) for c in range(2)], axis=0)
     half_high, half_low = split(half)
+    rows_high, rows_low = split(rows_ref[...])
 
     def dot(a, b):
         return lax.dot_general(a, b, (((1,), (1,)), ((), ())), preferred_element_type=F32)
 
-    for which, ref in ((core, own_ref), (1 - core, other_ref)):
-        high, low = split(ref[...])
-        part = (dot(high, half_low) + dot(low, half_high)) + dot(high, half_high)
-        out_ref[:, pl.ds(which, 1)] = part.reshape(NX * NZ, 1, 16, part.shape[1])
+    out_ref[...] = (dot(rows_high, half_low) + dot(rows_low, half_high)) + dot(rows_high, half_high)
 
 
-def second(core, own, other, half):
+def second(rows, halves):
     vmem = pl.BlockSpec(memory_space=pltpu.VMEM)
     return pl.pallas_call(
         second_kernel,
-        out_shape=jax.ShapeDtypeStruct((NX * NZ, 2, 16, 2 * half.shape[0]), F32),
-        in_specs=[pl.BlockSpec(memory_space=pltpu.SMEM), vmem, vmem, vmem],
+        out_shape=jax.ShapeDtypeStruct((rows.shape[0], 4 * halves.shape[1]), F32),
+        in_specs=[vmem, vmem],
         compiler_params=pltpu.CompilerParams(vmem_limit_bytes=32 * 2**20),
-    )(core, own, other, half)
+    )(rows, halves)
 
 
 def last_kernel(parts_ref, out_ref):
-    count = parts_ref.shape[0] // 2
-    sums = [parts_ref[core] for core in range(2)]
-    for place in range(1, count):
-        for core in range(2):
-            sums[core] += parts_ref[2 * place + core]
+    total = parts_ref[0]
+    for place in range(1, parts_ref.shape[0]):
+        total += parts_ref[place]
+    width = out_ref.shape[2]
     for aux in range(2):
-        runs = [sums[core][:, aux * 64 + z * 16 :][:, :16] for z in range(4) for core in range(2)]
-        out_ref[aux] = jnp.concatenate(runs, axis=1)
+        out_ref[aux] = total[:, aux * width : (aux + 1) * width]
 
 
 def last(parts):
     return pl.pallas_call(
         last_kernel,
-        out_shape=jax.ShapeDtypeStruct((2, parts.shape[1], parts.shape[2]), F32),
+        out_shape=jax.ShapeDtypeStruct((2, parts.shape[1], parts.shape[2] // 2), F32),
     )(parts)
 
 
 def shards(integrals, coefs, screen, domains):
     aux, row_len, col_len = integrals.shape
     occ = coefs.shape[1]
-    row, core = lax.axis_index("y"), lax.axis_index("core")
+    row = lax.axis_index("y")
     col = lax.axis_index(("x", "z", "core"))
     row_tiles = row_len // TILE
 
@@ -163,10 +158,9 @@
     half = lax.psum_scatter(half, "y", scatter_dimension=0, tiled=True)
 
     rows = lax.all_to_all(along_y, ("x", "z"), 0, 0, tiled=True).reshape(NX * NZ * occ, chip_len)
-    pairs = second(core[None], rows, swap(rows), half)
-    pairs = pairs.reshape(NX, NZ * 2, occ, pairs.shape[3])
-    pairs = lax.all_to_all(pairs, "x", 0, 0, tiled=True).sum(axis=0)
-    pairs = lax.all_to_all(pairs, ("z", "core"), 0, 0, tiled=True)
+    pairs = second(rows, lax.all_gather(half, "core"))
+    pairs = pairs.reshape(NX * NZ, occ, pairs.shape[1])
+    pairs = lax.all_to_all(pairs, ("x", "z"), 0, 0, tiled=True)
     return last(pairs).transpose(0, 2, 1)
 
 

time: 179 us -> 177 us (0.989); the launches traced: 178 us -> 175 us
  blocking collectives: 107 us -> 75.4 us
  waiting for transfers between devices: 17.6 us -> 47.3 us
    all_to_all x3 -> x1, blocking collectives: 62.8 us -> 24.3 us  [shards(): pairs = lax.all_to_all(pairs, ('x', 'z'), 0, 0, tiled=True)]
    reduce_scatter x1, waiting for transfers between devices: 0.01 us -> 32 us  [shards(): half = lax.psum_scatter(half, 'y', scatter_dimension=0, tiled=True)]
    ppermute x2 -> x1, starting transfers between devices: 15.1 us -> 8.26 us  [swap(): return lax.ppermute(value, 'core', [(0, 1), (1, 0)])]
    all_to_all x0 -> x1, starting transfers between devices: none -> 6.67 us  [shards(): lax.all_to_all(along_y, ('x', 'z'), 0, 0, tiled=True)]
    all_gather x0 -> x1, blocking collectives: none -> 6.49 us  [shards(): pairs = second(rows, lax.all_gather(half, 'core'))]
    ppermute x2 -> x1, waiting for transfers between devices: 2.27 us -> 0.01 us  [swap(): return lax.ppermute(value, 'core', [(0, 1), (1, 0)])]
where the time goes in v6:
time: 177 us; the launch traced here: 175 us
  blocking collectives  75.4 us (43%)
  waiting for transfers between devices  47.3 us (27%)
  starting transfers between devices  15 us (8%)
  Pallas kernels  13.9 us (8%)
  between operations  13.5 us (8%)
  other arithmetic  5.26 us (3%)
  local copies, waits for them, and re-layouts  4.15 us (2%)
    all_to_all x2, blocking collectives, gather(): return lax.all_to_all(copies, axis, 0, 0, tiled=True)  44.7 us
    reduce_scatter x1, waiting for transfers between devices, shards(): half = lax.psum_scatter(half, 'y', scatter_dimension=0, tiled=True)  32 us
    all_to_all x1, blocking collectives, shards(): pairs = lax.all_to_all(pairs, ('x', 'z'), 0, 0, tiled=True)  24.3 us
    all_gather x1, waiting for transfers between devices, shards(): lax.all_gather(along_x.reshape(NX * occ, row_len), 'z', axis=0, tiled=True)  15.2 us
    pallas_call x1, Pallas kernels, first(): pl.pallas_call(first_kernel, out_shape=(jax.ShapeDtypeStruct((NX, 2, 4, 1...  11.6 us
    ppermute x1, starting transfers between devices, swap(): return lax.ppermute(value, 'core', [(0, 1), (1, 0)])  8.26 us
    all_to_all x1, starting transfers between devices, shards(): lax.all_to_all(along_y, ('x', 'z'), 0, 0, tiled=True)  6.67 us
    all_gather x1, blocking collectives, shards(): pairs = second(rows, lax.all_gather(half, 'core'))  6.49 us
  transfers between devices with their start and end apart: 4, of which 2 were waited for; matrix products, arithmetic and copies ran while one was open for 3% of the time, Pallas kernels for 0%

profile of v6, /device:TPU:1, one launch (start us, length us, event | category | flops | bytes accessed | tf_op | source)
XLA Modules:
  0.0 174.5 jit_solution(2665238725436552717)
XLA Ops:
  6.5 0.0 copy-start
  6.5 0.0 all-gather.3.cloned.1.call-start
  6.5 0.7 copy-done
  7.2 0.2 compare_reduce_fusion
  7.4 0.1 broadcast_bitcast_fusion
  7.5 0.9 multiply_bitcast_fusion
  8.5 11.7 %all_to_all.20 = f32[4,16,2048]{2,1,0:T(8,128)} all-to-all(f32[4,16,2048]{2,1,0:T(8,128)S(1)} %broadcast_in_dim.9), channel_id=1, replica_groups=mesh['y'=8,'x'=4,'z'=8,'core'=2] {'x'}, dimensions={0} | all-to-all | bytes 1048576 | tf_op jit(solution)/shard_map/all_to_all | solution.py:25
  20.1 0.0 all-gather.3.cloned.1.call-update
  20.2 0.0 reduce-scatter.2.cloned.1.call-start
  20.2 0.7 convert_element_type.7
  20.9 0.1 copy.7
  21.0 0.0 copy-start.1
  21.0 0.6 mul.46
  21.6 0.1 copy.10
  21.7 1.4 copy-done.1
  23.2 2.4 %broadcast_multiply_fusion.own_ref = f32[2,2048,256]{2,1,0:T(8,128)} fusion(f32[2,2048,256]{2,1,0:T(8,128)S(1)} %copy-done.1, f32[2048,256]{1,0:T(8,128)S(1)} %bitcast.23), kind=kLoop, calls=%fused_computation.1 | loop fusion | flops 1048576 | bytes 10485760 | tf_op jit(solution)/shard_map/mul | solution.py:147
  25.6 8.3 %collective-permute-start = (f32[2,2048,256]{2,1,0:T(8,128)}, f32[2,2048,256]{2,1,0:T(8,128)}, u32[]{:S(2)}, u32[]{:S(2)}) collective-permute-start(f32[2,2048,256]{2,1,0:T(8,128)} %broadcast_multiply_fusion.own_ref), channel_id=1, source_target_pairs={{0,1},{1,0},{2,3},{3,2},{4,5},{5,4},{6,7},{7,6},{8,9},{9,8},{10,11... | collective-permute-start | bytes 12582920 | tf_op jit(solution)/shard_map/ppermute | solution.py:20
  33.8 0.9 dynamic-slice_bitcast_fusion
  34.8 0.1 broadcast_in_dim.11
  34.9 33.0 %all_to_all.21 = f32[8,16,2048]{2,1,0:T(8,128)S(1)} all-to-all(f32[8,16,2048]{2,1,0:T(8,128)S(1)} %broadcast_in_dim.11), channel_id=1, replica_groups=mesh['y'=8,'x'=4,'z'=8,'core'=2] {'y'}, dimensions={0} | all-to-all | bytes 2097152 | tf_op jit(solution)/shard_map/all_to_all | solution.py:25
  67.8 0.1 fusion
  67.9 1.1 pad_maximum_fusion
  69.0 0.0 collective-permute-done.other_ref
  69.0 15.2 %all-gather.3.cloned.1.call-done.coef_ref = f32[512,2048]{1,0:T(8,128)} async-done(((f32[64,2048]{1,0:T(8,128)}), f32[512,2048]{1,0:T(8,128)}) %all-gather.3.cloned.1.call-update) | async-done | bytes 4194320 | tf_op jit(solution)/shard_map/all_gather | solution.py:143
  84.2 11.6 %shard_map.46 = (f32[4,2,4,16,1024]{4,3,2,1,0:T(8,128)}, f32[32,16,512]{2,1,0:T(8,128)}) custom-call(f32[512,2048]{1,0:T(8,128)} %all-gather.3.cloned.1.call-done.coef_ref, f32[2,2048,256]{2,1,0:T(8,128)} %broadcast_multiply_fusion.own_ref, f32[2,2048,256]{2,1,0:T(8,128)} %collective-permute-done.other_ref, ...), custom_call_target="tpu_custom_call", output_to_operand_aliasing={{1}: (3, {})} | custom-call | flops 6442450944 | bytes 14680064 | tf_op jit(solution)/shard_map/pallas_call | solution.py:61
  95.8 0.0 reduce-scatter.2.cloned.1.call-update
  95.9 6.7 %all-to-all-start.2 = ((f32[32,16,512]{2,1,0:T(8,128)}), f32[32,16,512]{2,1,0:T(8,128)S(1)}, u32[]{:S(2)}, u32[]{:S(2)}) async-start(f32[32,16,512]{2,1,0:T(8,128)} %get-tuple-element.7), calls=%async_computation.2 | async-start | bytes 2097152 | tf_op jit(solution)/shard_map/all_to_all | solution.py:160
  102.6 32.0 %reduce-scatter.2.cloned.1.call-done = f32[64,1024]{1,0:T(8,128)} async-done(((f32[512,1024]{1,0:T(8,128)}), f32[64,1024]{1,0:T(8,128)}) %reduce-scatter.2.cloned.1.call-update) | async-done | bytes 262160 | tf_op jit(solution)/shard_map/reduce_scatter | solution.py:158
  134.6 6.5 %all-gather = f32[128,1024]{1,0:T(8,128)S(1)} all-gather(f32[64,1024]{1,0:T(8,128)} %reduce-scatter.2.cloned.1.call-done), channel_id=2, replica_groups=mesh['y'=8,'x'=4,'z'=8,'core'=2] {'core'}, dimensions={0}, use_global_device_ids=true | all-gather | bytes 786432 | tf_op jit(solution)/shard_map/all_gather | solution.py:161
  141.1 0.0 all-to-all-done.2
  141.1 0.6 shard_map.47
  141.7 24.3 %all_to_all.22.parts_ref = f32[32,16,256]{2,1,0:T(8,128)} all-to-all(f32[32,16,256]{2,1,0:T(8,128)S(1)} %bitcast.22), channel_id=1, replica_groups=mesh['y'=8,'x'=4,'z'=8,'core'=2] {'x','z'}, dimensions={0} | all-to-all | bytes 1048576 | tf_op jit(solution)/shard_map/all_to_all | solution.py:163
  166.0 1.7 shard_map.48
  (4 shorter events, 0.1 us)
Async XLA Ops:
  6.5 0.7 copy-start
  6.5 77.7 %all-gather.3.cloned.1.call-start = ((), (), s32[]{:S(2)}) async-start(), calls=%async_computation.5 | async-start | bytes 4718592 | tf_op jit(solution)/shard_map/all_gather | solution.py:143
  20.2 114.4 %reduce-scatter.2.cloned.1.call-start = ((), (), s32[]{:S(2)}) async-start(), calls=%async_computation.6 | async-start | bytes 2359296 | tf_op jit(solution)/shard_map/reduce_scatter | solution.py:158
  21.0 2.2 %copy-start.1 = (f32[2,2048,256]{2,1,0:T(8,128)S(1)}, f32[2,2048,256]{2,1,0:T(8,128)}, u32[]{:S(2)}) copy-start(f32[2,2048,256]{2,1,0:T(8,128)} %param.4) | copy-start | bytes 12582916
  25.6 43.4 %collective-permute-start = (f32[2,2048,256]{2,1,0:T(8,128)}, f32[2,2048,256]{2,1,0:T(8,128)}, u32[]{:S(2)}, u32[]{:S(2)}) collective-permute-start(f32[2,2048,256]{2,1,0:T(8,128)} %broadcast_multiply_fusion.own_ref), channel_id=1, source_target_pairs={{0,1},{1,0},{2,3},{3,2},{4,5},{5,4},{6,7},{7,6},{8,9},{9,8},{10,11... | collective-permute-start | bytes 12582920 | tf_op jit(solution)/shard_map/ppermute | solution.py:20
  95.9 45.2 %all-to-all-start.2 = ((f32[32,16,512]{2,1,0:T(8,128)}), f32[32,16,512]{2,1,0:T(8,128)S(1)}, u32[]{:S(2)}, u32[]{:S(2)}) async-start(f32[32,16,512]{2,1,0:T(8,128)} %get-tuple-element.7), calls=%async_computation.2 | async-start | bytes 2097152 | tf_op jit(solution)/shard_map/all_to_all | solution.py:160
Sparse Core Ops, SparseCore 0:
  20.3 63.9 all-gather.2
  96.0 38.5 reduce-scatter.1

commit v7 on v6

v7 whole, which is shorter than its diff:
```python
import jax
import jax.numpy as jnp
from jax import lax
from jax.experimental import pallas as pl
from jax.experimental.pallas import tpu as pltpu
from jax.sharding import Mesh, PartitionSpec as P

TILE = 128
NX, NZ = 4, 8
REST = 256
BF16 = jnp.bfloat16
F32 = jnp.float32


def split(value):
    high = value.astype(BF16)
    return high, (value - high.astype(F32)).astype(BF16)


def swap(value):
    return lax.ppermute(value, "core", [(0, 1), (1, 0)])


def gather(value, axis):
    copies = jnp.broadcast_to(value[None], (lax.axis_size(axis),) + value.shape)
    return lax.all_to_all(copies, axis, 0, 0, tiled=True)


def around(value, axis):
    count = lax.axis_size(axis)
    found = [value] * count
    for step in range(1, count // 2 + 1):
        found[step] = lax.ppermute(found[step - 1], axis, [(i, (i - 1) % count) for i in range(count)])
        if 2 * step < count:
            back = found[(1 - step) % count]
            found[-step] = lax.ppermute(back, axis, [(i, (i + 1) % count) for i in range(count)])
    return jnp.stack(found)


def first_kernel(
    coef_hbm, rest_hbm, own_hbm, other_hbm, passed_hbm, out_hbm, passed_out_hbm,
    coef, rest, own, other, total, sums, coef_sem, rest_sem, own_sem, other_sem, out_sem,
):
    del passed_hbm, passed_out_hbm
    steps, aux, depth, width = own.shape

    def copies(step):
        rows = pl.ds(step * depth, depth)
        if step < steps - 1:
            columns = pltpu.make_async_copy(coef_hbm.at[:, rows], coef.at[step], coef_sem.at[step])
        else:
            columns = pltpu.make_async_copy(rest_hbm, rest, rest_sem)
        return (
            columns,
            pltpu.make_async_copy(own_hbm.at[:, rows, :], own.at[step], own_sem.at[step]),
            pltpu.make_async_copy(other_hbm.at[:, rows, :], other.at[step], other_sem.at[step]),
        )

    for step in range(steps):
        for copy in copies(step):
            copy.start()
    for step in range(steps):
        for copy in copies(step):
            copy.wait()
        coef_high, coef_low = split(coef[step] if step < steps - 1 else rest[...])
        for p in range(aux):
            for place, integrals in enumerate((own, other)):
                high, low = split(integrals[step, p])
                part = jnp.dot(coef_high, low, preferred_element_type=F32)
                part += jnp.dot(coef_low, high, preferred_element_type=F32)
                part += jnp.dot(coef_high, high, preferred_element_type=F32)
                columns = slice((2 * p + place) * width, (2 * p + place + 1) * width)
                if step == 0:
                    total[:, columns] = part
                elif step < steps - 1:
                    total[:, columns] += part
                else:
                    for z in range(NZ):
                        for x in range(NX):
                            start, end = (z * NX + x) * 16, (x * NZ + z) * 16
                            sums[end : end + 16, columns] = total[start : start + 16, columns] + part[end : end + 16]
    copy = pltpu.make_async_copy(sums, out_hbm, out_sem)
    copy.start()
    copy.wait()


def first(coef, rest, own, other, passed):
    occ = coef.shape[0]
    aux, full_depth, half_width = own.shape
    depth = rest.shape[1]
    steps = full_depth // depth
    width = 2 * aux * half_width
    away = pl.BlockSpec(memory_space=pl.ANY)
    block = pltpu.VMEM((steps, aux, depth, half_width), F32)
    sems = pltpu.SemaphoreType.DMA((steps,))
    return pl.pallas_call(
        first_kernel,
        out_shape=(
            jax.ShapeDtypeStruct((occ, width), F32),
            jax.ShapeDtypeStruct(passed.shape, passed.dtype),
        ),
        in_specs=[away] * 5,
        out_specs=(away, away),
        input_output_aliases={4: 1},
        scratch_shapes=[
            pltpu.VMEM((steps - 1, occ, depth), F32),
            pltpu.VMEM((occ, depth), F32),
            block,
            block,
            pltpu.VMEM((occ, width), F32),
            pltpu.VMEM((occ, width), F32),
            pltpu.SemaphoreType.DMA((steps - 1,)),
            pltpu.SemaphoreType.DMA,
            sems,
            sems,
            pltpu.SemaphoreType.DMA,
        ],
        compiler_params=pltpu.CompilerParams(vmem_limit_bytes=56 * 2**20),
        cost_estimate=pl.CostEstimate(
            flops=6 * occ * full_depth * width, bytes_accessed=14 * 2**20, transcendentals=0
        ),
    )(coef, rest, own, other, passed)


def second_kernel(rows_ref, halves_ref, out_ref):
    width = halves_ref.shape[2] // 4

    def nus(p, z, source):
        pair = halves_ref[source, z * 16 : z * 16 + 16, 2 * p * width : 2 * (p + 1) * width]
        return pair if source == 0 else jnp.concatenate([pair[:, width:], pair[:, :width]], axis=1)

    half = jnp.concatenate([nus(p, z, c) for p in range(2) for z in range(4) for c in range(2)], axis=0)
    half_high, half_low = split(half)
    rows_high, rows_low = split(rows_ref[...])

    def dot(a, b):
        return lax.dot_general(a, b, (((1,), (1,)), ((), ())), preferred_element_type=F32)

    out_ref[...] = (dot(rows_high, half_low) + dot(rows_low, half_high)) + dot(rows_high, half_high)


def second(rows, halves):
    vmem = pl.BlockSpec(memory_space=pltpu.VMEM)
    return pl.pallas_call(
        second_kernel,
        out_shape=jax.ShapeDtypeStruct((rows.shape[0], 4 * halves.shape[1]), F32),
        in_specs=[vmem, vmem],
        compiler_params=pltpu.CompilerParams(vmem_limit_bytes=32 * 2**20),
    )(rows, halves)


def last_kernel(parts_ref, out_ref):
    total = parts_ref[0]
    for place in range(1, parts_ref.shape[0]):
        total += parts_ref[place]
    width = out_ref.shape[2]
    for aux in range(2):
        out_ref[aux] = total[:, aux * width : (aux + 1) * width]


def last(parts):
    return pl.pallas_call(
        last_kernel,
        out_shape=jax.ShapeDtypeStruct((2, parts.shape[1], parts.shape[2] // 2), F32),
    )(parts)


def shards(integrals, coefs, screen, domains):
    aux, row_len, col_len = integrals.shape
    occ = coefs.shape[1]
    row = lax.axis_index("y")
    col = lax.axis_index(("x", "z", "core"))
    row_tiles = row_len // TILE

    tile_ids = row * row_tiles + jnp.arange(row_tiles, dtype=jnp.int32)
    listed = lax.dynamic_index_in_dim(domains, col * occ // TILE, 0, keepdims=False)
    in_domain = jnp.any(listed[None, :] == tile_ids[:, None], axis=1).astype(F32)
    coef = coefs.T * jnp.repeat(in_domain, TILE)[None, :]

    most = row_len - REST
    along_x = gather(coef[:, :most], "x")
    gathered = lax.all_gather(along_x.reshape(NX * occ, most), "z", axis=0, tiled=True)

    keep = screen.astype(F32)
    screened = (
        integrals.reshape(aux, row_tiles, TILE, col_len // TILE, TILE) * keep[None, :, None, :, None]
    ).reshape(integrals.shape)
    other = swap(screened)

    after = 0.0 * (along_x[0, 0, 0] + screened[0, 0, 0])
    rest = gather(gather(coef[:, most:] + after, "z"), "x").reshape(NX * NZ * occ, REST)

    along_y = around(coef + 0.0 * along_x[0, 0, 0], "y")

    half, along_y = first(gathered, rest, screened, other, along_y)
    half = lax.psum_scatter(half, "y", scatter_dimension=0, tiled=True)

    chip_len = 2 * col_len
    along_y = lax.dynamic_slice_in_dim(jnp.concatenate([along_y, along_y]), lax.rem(8 - row, 8), 8, 0)
    along_y = along_y.reshape(8, occ, row_len // chip_len, chip_len).transpose(0, 2, 1, 3)
    rows = lax.all_to_all(along_y.reshape(NX * NZ, occ, chip_len), ("x", "z"), 0, 0, tiled=True)
    pairs = second(rows.reshape(NX * NZ * occ, chip_len), lax.all_gather(half, "core"))
    pairs = pairs.reshape(NX * NZ, occ, pairs.shape[1])
    pairs = lax.all_to_all(pairs, ("x", "z"), 0, 0, tiled=True)
    return last(pairs).transpose(0, 2, 1)


def solution(mesh):
    devices = mesh.devices.reshape(8, NX, NZ, 2)
    split_mesh = Mesh(devices, ("y", "x", "z", "core"))
    col = ("x", "z", "core")
    placed = (P(None, "y", col), P("y", col), P("y", col), P())
    return jax.shard_map(
        shards, mesh=split_mesh, in_specs=placed, out_specs=P(None, "y", col), check_vma=False
    )
```

time: 177 us -> 174 us (0.983)
  starting transfers between devices: 15 us -> 50 us
  blocking collectives: 75.4 us -> 41.8 us
  waiting for transfers between devices: 47.3 us -> 36.9 us
  local copies, waits for them, and re-layouts: 4.15 us -> 7.72 us
  between operations: 13.5 us -> 15.6 us
    all_to_all x2 -> x1, blocking collectives: 44.7 us -> 11.3 us  [gather(): return lax.all_to_all(copies, axis, 0, 0, tiled=True)]
    ppermute x0 -> x7, starting transfers between devices: none -> 23.5 us  [the longest x4 16.3 us: around(): lax.ppermute(found[step - 1], axis, [(i, (i - 1) % count) for i in range(...]
    all_gather x1, waiting for transfers between devices: 15.2 us -> 0.57 us  [shards(): lax.all_gather(along_x.reshape(NX * occ, most), 'z', axis=0, tiled=True)]
    all_to_all x1 -> x3, starting transfers between devices: 6.67 us -> 18.1 us  [the longest x2 12 us: gather(): return lax.all_to_all(copies, axis, 0, 0, tiled=True)]
    all_to_all x1 -> x3, waiting for transfers between devices: 0.01 us -> 3.77 us  [the longest x2 3.76 us: gather(): return lax.all_to_all(copies, axis, 0, 0, tiled=True)]
    slice x1 -> x4, local copies, waits for them, and re-layouts: 0.08 us -> 2.47 us  [the longest x2 2.38 us: shards(): after = 0.0 * (along_x[0, 0, 0] + screened[0, 0, 0])]
    ppermute x0 -> x7, waiting for transfers between devices: none -> 1.92 us  [the longest x4 1.91 us: around(): lax.ppermute(found[step - 1], axis, [(i, (i - 1) % count) for i in range(...]
  transfers between devices with their start and end apart: 4 -> 13, of which waited for: 2 -> 4; matrix products, arithmetic and copies ran while one was open for 3% -> 6% of each run, Pallas kernels for 0% -> 0%
where the time goes in v7:
time: 174 us; the launch traced here: 171 us
  starting transfers between devices  50 us (29%)
  blocking collectives  41.8 us (24%)
  waiting for transfers between devices  36.9 us (21%)
  between operations  15.6 us (9%)
  Pallas kernels  12.4 us (7%)
  local copies, waits for them, and re-layouts  7.72 us (4%)
  other arithmetic  6.61 us (4%)
    reduce_scatter x1, waiting for transfers between devices, shards(): half = lax.psum_scatter(half, 'y', scatter_dimension=0, tiled=True)  30.6 us
    all_to_all x1, blocking collectives, shards(): pairs = lax.all_to_all(pairs, ('x', 'z'), 0, 0, tiled=True)  23.9 us
    ppermute x4, starting transfers between devices, around(): lax.ppermute(found[step - 1], axis, [(i, (i - 1) % count) for i in range(...  16.3 us
    all_to_all x2, starting transfers between devices, gather(): return lax.all_to_all(copies, axis, 0, 0, tiled=True)  12 us
    all_to_all x1, blocking collectives, gather(): return lax.all_to_all(copies, axis, 0, 0, tiled=True)  11.3 us
    pallas_call x1, Pallas kernels, first(): pl.pallas_call(first_kernel, out_shape=(jax.ShapeDtypeStruct((occ, width)...  10.1 us
    ppermute x1, starting transfers between devices, swap(): return lax.ppermute(value, 'core', [(0, 1), (1, 0)])  8.27 us
    ppermute x3, starting transfers between devices, around(): lax.ppermute(back, axis, [(i, (i + 1) % count) for i in range(count)])  7.2 us
  transfers between devices with their start and end apart: 13, of which 4 were waited for; matrix products, arithmetic and copies ran while one was open for 6% of the time, Pallas kernels for 0%

profile of v7, /device:TPU:1, one launch (start us, length us, event | category | flops | bytes accessed | tf_op | source)
XLA Modules:
  0.0 170.9 jit_solution(17639673545492132339)
XLA Ops:
  6.5 0.0 copy-start
  6.5 0.0 all-gather.3.cloned.1.call-start
  6.5 0.7 copy-done
  7.2 0.2 compare_reduce_fusion
  7.4 0.1 broadcast_bitcast_fusion
  7.5 0.9 multiply_bitcast_fusion
  8.5 11.3 %all_to_all.25 = f32[4,16,1792]{2,1,0:T(8,128)} all-to-all(f32[4,16,1792]{2,1,0:T(8,128)S(1)} %broadcast_in_dim.9), channel_id=1, replica_groups=mesh['y'=8,'x'=4,'z'=8,'core'=2] {'x'}, dimensions={0} | all-to-all | bytes 917504 | tf_op jit(solution)/shard_map/all_to_all | solution.py:26
  19.8 0.0 all-gather.3.cloned.1.call-update
  19.8 0.7 convert_element_type.7
  20.5 0.1 copy.7
  20.6 0.0 copy-start.1
  20.6 0.6 mul.58
  21.2 0.1 copy.10
  21.4 1.4 copy-done.1
  22.8 0.0 copy-start.4
  22.8 2.3 %broadcast_multiply_fusion.own_hbm = f32[2,2048,256]{2,1,0:T(8,128)} fusion(f32[2,2048,256]{2,1,0:T(8,128)S(1)} %copy-done.1, f32[2048,256]{1,0:T(8,128)S(1)} %bitcast.41), kind=kLoop, calls=%fused_computation.3 | loop fusion | flops 1048576 | bytes 10485760 | tf_op jit(solution)/shard_map/mul | solution.py:186
  25.1 8.3 %collective-permute-start = (f32[2,2048,256]{2,1,0:T(8,128)}, f32[2,2048,256]{2,1,0:T(8,128)}, u32[]{:S(2)}, u32[]{:S(2)}) collective-permute-start(f32[2,2048,256]{2,1,0:T(8,128)} %broadcast_multiply_fusion.own_hbm), channel_id=1, source_target_pairs={{0,1},{1,0},{2,3},{3,2},{4,5},{5,4},{6,7},{7,6},{8,9},{9,8},{10,11... | collective-permute-start | bytes 12582920 | tf_op jit(solution)/shard_map/ppermute | solution.py:21
  33.4 1.2 slice.36
  34.6 1.2 slice.35
  36.4 0.0 copy-done.4
  36.5 1.9 %collective-permute-start.1 = (f32[16,2048]{1,0:T(8,128)S(1)}, f32[16,2048]{1,0:T(8,128)S(1)}, u32[]{:S(2)}, u32[]{:S(2)}) collective-permute-start(f32[16,2048]{1,0:T(8,128)S(1)} %get-tuple-element.10), channel_id=1, source_target_pairs={{0,448},{64,0},{128,64},{192,128},{256,192},{320,256},{384,320},{4... | collective-permute-start | bytes 393224 | tf_op jit(solution)/shard_map/ppermute | solution.py:33
  38.4 3.4 %collective-permute-start.5 = (f32[16,2048]{1,0:T(8,128)S(1)}, f32[16,2048]{1,0:T(8,128)S(1)}, u32[]{:S(2)}, u32[]{:S(2)}) collective-permute-start(f32[16,2048]{1,0:T(8,128)S(1)} %get-tuple-element.10), channel_id=1, source_target_pairs={{0,64},{64,128},{128,192},{192,256},{256,320},{320,384},{384,448},... | collective-permute-start | bytes 393224 | tf_op jit(solution)/shard_map/ppermute | solution.py:36
  43.0 0.7 broadcast_in_dim.10
  43.7 8.5 %all-to-all-start.1 = ((f32[8,16,256]{2,1,0:T(8,128)}), f32[8,16,256]{2,1,0:T(8,128)S(1)}, u32[]{:S(2)}, u32[]{:S(2)}) async-start(f32[8,16,256]{2,1,0:T(8,128)} %broadcast_in_dim.10), calls=%async_computation.1 | async-start | bytes 262144 | tf_op jit(solution)/shard_map/all_to_all | solution.py:26
  52.2 0.0 collective-permute-done.1
  52.2 4.6 %collective-permute-start.2 = (f32[16,2048]{1,0:T(8,128)S(1)}, f32[16,2048]{1,0:T(8,128)S(1)}, u32[]{:S(2)}, u32[]{:S(2)}) collective-permute-start(f32[16,2048]{1,0:T(8,128)S(1)} %collective-permute-done.1), channel_id=1, source_target_pairs={{0,448},{64,0},{128,64},{192,128},{256,192},{320,256},{384,320},{4... | collective-permute-start | bytes 393224 | tf_op jit(solution)/shard_map/ppermute | solution.py:33
  56.8 0.0 collective-permute-done.5
  56.9 1.9 %collective-permute-start.6 = (f32[16,2048]{1,0:T(8,128)S(1)}, f32[16,2048]{1,0:T(8,128)S(1)}, u32[]{:S(2)}, u32[]{:S(2)}) collective-permute-start(f32[16,2048]{1,0:T(8,128)S(1)} %collective-permute-done.5), channel_id=1, source_target_pairs={{0,64},{64,128},{128,192},{192,256},{256,320},{320,384},{384,448},... | collective-permute-start | bytes 393224 | tf_op jit(solution)/shard_map/ppermute | solution.py:36
  58.8 3.8 %all-to-all-done.1 = f32[8,16,256]{2,1,0:T(8,128)S(1)} async-done(((f32[8,16,256]{2,1,0:T(8,128)}), f32[8,16,256]{2,1,0:T(8,128)S(1)}, u32[]{:S(2)}, u32[]{:S(2)}) %all-to-all-start.1) | async-done | bytes 131104 | tf_op jit(solution)/shard_map/all_to_all | solution.py:26
  62.5 0.9 broadcast_in_dim.11
  63.4 3.5 %all-to-all-start.2 = ((f32[4,8,16,256]{3,2,1,0:T(8,128)}), f32[4,8,16,256]{3,2,1,0:T(8,128)S(1)}, u32[]{:S(2)}, u32[]{:S(2)}) async-start(f32[4,8,16,256]{3,2,1,0:T(8,128)} %broadcast_in_dim.11), calls=%async_computation.2 | async-start | bytes 1048576 | tf_op jit(solution)/shard_map/all_to_all | solution.py:26
  66.9 0.0 reduce-scatter.2.cloned.1.call-start
  67.0 0.0 collective-permute-done.2
  67.0 4.5 %collective-permute-start.3 = (f32[16,2048]{1,0:T(8,128)S(1)}, f32[16,2048]{1,0:T(8,128)S(1)}, u32[]{:S(2)}, u32[]{:S(2)}) collective-permute-start(f32[16,2048]{1,0:T(8,128)S(1)} %collective-permute-done.2), channel_id=1, source_target_pairs={{0,448},{64,0},{128,64},{192,128},{256,192},{320,256},{384,320},{4... | collective-permute-start | bytes 393224 | tf_op jit(solution)/shard_map/ppermute | solution.py:33
  71.5 0.0 collective-permute-done.6
  71.5 1.9 %collective-permute-start.7 = (f32[16,2048]{1,0:T(8,128)S(1)}, f32[16,2048]{1,0:T(8,128)S(1)}, u32[]{:S(2)}, u32[]{:S(2)}) collective-permute-start(f32[16,2048]{1,0:T(8,128)S(1)} %collective-permute-done.6), channel_id=1, source_target_pairs={{0,64},{64,128},{128,192},{192,256},{256,320},{320,384},{384,448},... | collective-permute-start | bytes 393224 | tf_op jit(solution)/shard_map/ppermute | solution.py:36
  73.4 0.0 collective-permute-done.3
  73.4 5.3 %collective-permute-start.4 = (f32[16,2048]{1,0:T(8,128)S(1)}, f32[16,2048]{1,0:T(8,128)S(1)}, u32[]{:S(2)}, u32[]{:S(2)}) collective-permute-start(f32[16,2048]{1,0:T(8,128)S(1)} %collective-permute-done.3), channel_id=1, source_target_pairs={{0,448},{64,0},{128,64},{192,128},{256,192},{320,256},{384,320},{4... | collective-permute-start | bytes 393224 | tf_op jit(solution)/shard_map/ppermute | solution.py:33
  78.8 1.9 %collective-permute-done.4 = f32[16,2048]{1,0:T(8,128)S(1)} collective-permute-done((f32[16,2048]{1,0:T(8,128)S(1)}, f32[16,2048]{1,0:T(8,128)S(1)}, u32[]{:S(2)}, u32[]{:S(2)}) %collective-permute-start.4) | collective-permute-done | bytes 131104 | tf_op jit(solution)/shard_map/ppermute | solution.py:33
  80.7 0.0 collective-permute-done.7
  80.8 0.0 copy-start.2
  80.8 0.0 all-to-all-done.2
  80.8 0.0 copy-start.3
  80.8 0.0 collective-permute-done.other_hbm
  80.8 0.6 all-gather.3.cloned.1.call-done.coef_hbm
  81.4 0.4 copy-done.2
  81.8 0.2 copy-done.3
  81.9 10.1 %shard_map.46 = (f32[512,1024]{1,0:T(8,128)}, f32[8,16,2048]{2,1,0:T(8,128)}) custom-call(f32[512,1792]{1,0:T(8,128)} %all-gather.3.cloned.1.call-done.coef_hbm, f32[512,256]{1,0:T(8,128)} %bitcast.44, f32[2,2048,256]{2,1,0:T(8,128)} %broadcast_multiply_fusion.own_hbm, ...), custom_call_target="tpu_custom_call", output_to_operand_aliasing={{1}: (4, {})} | custom-call | flops 6442450944 | bytes 14680064 | tf_op jit(solution)/shard_map/pallas_call | solution.py:96
  92.1 0.0 reduce-scatter.2.cloned.1.call-update
  92.1 1.4 fusion
  93.5 0.1 fusion.2
  93.6 1.1 pad_maximum_fusion
  94.7 6.1 %all-to-all-start.3 = ((f32[32,16,512]{2,1,0:T(8,128)}), f32[32,16,512]{2,1,0:T(8,128)S(1)}, u32[]{:S(2)}, u32[]{:S(2)}) async-start(f32[32,16,512]{2,1,0:T(8,128)} %bitcast.15), calls=%async_computation.3 | async-start | bytes 2097152 | tf_op jit(solution)/shard_map/all_to_all | solution.py:201
  100.8 30.6 %reduce-scatter.2.cloned.1.call-done = f32[64,1024]{1,0:T(8,128)} async-done(((f32[512,1024]{1,0:T(8,128)}), f32[64,1024]{1,0:T(8,128)}) %reduce-scatter.2.cloned.1.call-update) | async-done | bytes 262160 | tf_op jit(solution)/shard_map/reduce_scatter | solution.py:196
  131.3 6.5 %all-gather = f32[128,1024]{1,0:T(8,128)S(1)} all-gather(f32[64,1024]{1,0:T(8,128)} %reduce-scatter.2.cloned.1.call-done), channel_id=2, replica_groups=mesh['y'=8,'x'=4,'z'=8,'core'=2] {'core'}, dimensions={0}, use_global_device_ids=true | all-gather | bytes 786432 | tf_op jit(solution)/shard_map/all_gather | solution.py:202
  137.9 0.0 all-to-all-done.3
  137.9 0.6 shard_map.47
  138.5 23.9 %all_to_all.26.parts_ref = f32[32,16,256]{2,1,0:T(8,128)} all-to-all(f32[32,16,256]{2,1,0:T(8,128)S(1)} %bitcast.40), channel_id=1, replica_groups=mesh['y'=8,'x'=4,'z'=8,'core'=2] {'x','z'}, dimensions={0} | all-to-all | bytes 1048576 | tf_op jit(solution)/shard_map/all_to_all | solution.py:204
  162.4 1.7 shard_map.48
  (14 shorter events, 0.2 us)
Async XLA Ops:
  6.5 0.7 copy-start
  6.5 74.9 %all-gather.3.cloned.1.call-start = ((), (), s32[]{:S(2)}) async-start(), calls=%async_computation.6 | async-start | bytes 4128768 | tf_op jit(solution)/shard_map/all_gather | solution.py:182
  20.6 2.2 %copy-start.1 = (f32[2,2048,256]{2,1,0:T(8,128)S(1)}, f32[2,2048,256]{2,1,0:T(8,128)}, u32[]{:S(2)}) copy-start(f32[2,2048,256]{2,1,0:T(8,128)} %param.4) | copy-start | bytes 12582916
  22.8 13.7 %copy-start.4 = (f32[2048,16]{0,1:T(8,128)S(1)}, f32[2048,16]{0,1:T(8,128)}, u32[]{:S(2)}) copy-start(f32[2048,16]{0,1:T(8,128)} %param.5) | copy-start | bytes 393220
  25.1 55.7 %collective-permute-start = (f32[2,2048,256]{2,1,0:T(8,128)}, f32[2,2048,256]{2,1,0:T(8,128)}, u32[]{:S(2)}, u32[]{:S(2)}) collective-permute-start(f32[2,2048,256]{2,1,0:T(8,128)} %broadcast_multiply_fusion.own_hbm), channel_id=1, source_target_pairs={{0,1},{1,0},{2,3},{3,2},{4,5},{5,4},{6,7},{7,6},{8,9},{9,8},{10,11... | collective-permute-start | bytes 12582920 | tf_op jit(solution)/shard_map/ppermute | solution.py:21
  36.5 15.7 %collective-permute-start.1 = (f32[16,2048]{1,0:T(8,128)S(1)}, f32[16,2048]{1,0:T(8,128)S(1)}, u32[]{:S(2)}, u32[]{:S(2)}) collective-permute-start(f32[16,2048]{1,0:T(8,128)S(1)} %get-tuple-element.10), channel_id=1, source_target_pairs={{0,448},{64,0},{128,64},{192,128},{256,192},{320,256},{384,320},{4... | collective-permute-start | bytes 393224 | tf_op jit(solution)/shard_map/ppermute | solution.py:33
  38.4 18.4 %collective-permute-start.5 = (f32[16,2048]{1,0:T(8,128)S(1)}, f32[16,2048]{1,0:T(8,128)S(1)}, u32[]{:S(2)}, u32[]{:S(2)}) collective-permute-start(f32[16,2048]{1,0:T(8,128)S(1)} %get-tuple-element.10), channel_id=1, source_target_pairs={{0,64},{64,128},{128,192},{192,256},{256,320},{320,384},{384,448},... | collective-permute-start | bytes 393224 | tf_op jit(solution)/shard_map/ppermute | solution.py:36
  43.7 18.8 %all-to-all-start.1 = ((f32[8,16,256]{2,1,0:T(8,128)}), f32[8,16,256]{2,1,0:T(8,128)S(1)}, u32[]{:S(2)}, u32[]{:S(2)}) async-start(f32[8,16,256]{2,1,0:T(8,128)} %broadcast_in_dim.10), calls=%async_computation.1 | async-start | bytes 262144 | tf_op jit(solution)/shard_map/all_to_all | solution.py:26
  52.2 14.7 %collective-permute-start.2 = (f32[16,2048]{1,0:T(8,128)S(1)}, f32[16,2048]{1,0:T(8,128)S(1)}, u32[]{:S(2)}, u32[]{:S(2)}) collective-permute-start(f32[16,2048]{1,0:T(8,128)S(1)} %collective-permute-done.1), channel_id=1, source_target_pairs={{0,448},{64,0},{128,64},{192,128},{256,192},{320,256},{384,320},{4... | collective-permute-start | bytes 393224 | tf_op jit(solution)/shard_map/ppermute | solution.py:33
  56.9 14.6 %collective-permute-start.6 = (f32[16,2048]{1,0:T(8,128)S(1)}, f32[16,2048]{1,0:T(8,128)S(1)}, u32[]{:S(2)}, u32[]{:S(2)}) collective-permute-start(f32[16,2048]{1,0:T(8,128)S(1)} %collective-permute-done.5), channel_id=1, source_target_pairs={{0,64},{64,128},{128,192},{192,256},{256,320},{320,384},{384,448},... | collective-permute-start | bytes 393224 | tf_op jit(solution)/shard_map/ppermute | solution.py:36
  63.4 17.4 %all-to-all-start.2 = ((f32[4,8,16,256]{3,2,1,0:T(8,128)}), f32[4,8,16,256]{3,2,1,0:T(8,128)S(1)}, u32[]{:S(2)}, u32[]{:S(2)}) async-start(f32[4,8,16,256]{3,2,1,0:T(8,128)} %broadcast_in_dim.11), calls=%async_computation.2 | async-start | bytes 1048576 | tf_op jit(solution)/shard_map/all_to_all | solution.py:26
  66.9 64.4 %reduce-scatter.2.cloned.1.call-start = ((), (), s32[]{:S(2)}) async-start(), calls=%async_computation.7 | async-start | bytes 2359296 | tf_op jit(solution)/shard_map/reduce_scatter | solution.py:196
  67.0 6.5 %collective-permute-start.3 = (f32[16,2048]{1,0:T(8,128)S(1)}, f32[16,2048]{1,0:T(8,128)S(1)}, u32[]{:S(2)}, u32[]{:S(2)}) collective-permute-start(f32[16,2048]{1,0:T(8,128)S(1)} %collective-permute-done.2), channel_id=1, source_target_pairs={{0,448},{64,0},{128,64},{192,128},{256,192},{320,256},{384,320},{4... | collective-permute-start | bytes 393224 | tf_op jit(solution)/shard_map/ppermute | solution.py:33
  71.5 9.2 %collective-permute-start.7 = (f32[16,2048]{1,0:T(8,128)S(1)}, f32[16,2048]{1,0:T(8,128)S(1)}, u32[]{:S(2)}, u32[]{:S(2)}) collective-permute-start(f32[16,2048]{1,0:T(8,128)S(1)} %collective-permute-done.6), channel_id=1, source_target_pairs={{0,64},{64,128},{128,192},{192,256},{256,320},{320,384},{384,448},... | collective-permute-start | bytes 393224 | tf_op jit(solution)/shard_map/ppermute | solution.py:36
  73.4 7.3 %collective-permute-start.4 = (f32[16,2048]{1,0:T(8,128)S(1)}, f32[16,2048]{1,0:T(8,128)S(1)}, u32[]{:S(2)}, u32[]{:S(2)}) collective-permute-start(f32[16,2048]{1,0:T(8,128)S(1)} %collective-permute-done.3), channel_id=1, source_target_pairs={{0,448},{64,0},{128,64},{192,128},{256,192},{320,256},{384,320},{4... | collective-permute-start | bytes 393224 | tf_op jit(solution)/shard_map/ppermute | solution.py:33
  80.8 1.0 copy-start.2
  80.8 1.1 copy-start.3
  94.7 43.2 %all-to-all-start.3 = ((f32[32,16,512]{2,1,0:T(8,128)}), f32[32,16,512]{2,1,0:T(8,128)S(1)}, u32[]{:S(2)}, u32[]{:S(2)}) async-start(f32[32,16,512]{2,1,0:T(8,128)} %bitcast.15), calls=%async_computation.3 | async-start | bytes 2097152 | tf_op jit(solution)/shard_map/all_to_all | solution.py:201
Sparse Core Ops, SparseCore 0:
  20.0 61.4 all-gather.2
  92.2 39.0 reduce-scatter.1

commit v8 on v7

--- a/solution.py
+++ b/solution.py
@@ -7,7 +7,7 @@
 
 TILE = 128
 NX, NZ = 4, 8
-REST = 256
+REST, CHUNK = 256, 256
 BF16 = jnp.bfloat16
 F32 = jnp.float32
 
@@ -38,41 +38,57 @@
 
 
 def first_kernel(
-    coef_hbm, rest_hbm, own_hbm, other_hbm, passed_hbm, out_hbm, passed_out_hbm,
-    coef, rest, own, other, total, sums, coef_sem, rest_sem, own_sem, other_sem, out_sem,
+    own_screen, other_screen, coef_hbm, rest_hbm, own_hbm, other_hbm, passed_hbm, out_hbm, passed_out_hbm,
+    coef, rest, own, other, total, sums, coef_sem, own_sem, other_sem, out_sem,
 ):
     del passed_hbm, passed_out_hbm
-    steps, aux, depth, width = own.shape
+    aux, full_depth, width = own.shape
+    most = coef.shape[1]
+    starts = [*range(0, most, CHUNK), most]
+    ends = [*starts[1:], full_depth]
 
     def copies(step):
-        rows = pl.ds(step * depth, depth)
-        if step < steps - 1:
-            columns = pltpu.make_async_copy(coef_hbm.at[:, rows], coef.at[step], coef_sem.at[step])
+        rows = pl.ds(starts[step], ends[step] - starts[step])
+        if starts[step] < most:
+            columns = pltpu.make_async_copy(coef_hbm.at[:, rows], coef.at[:, rows], coef_sem.at[step])
         else:
-            columns = pltpu.make_async_copy(rest_hbm, rest, rest_sem)
+            columns = pltpu.make_async_copy(rest_hbm, rest, coef_sem.at[step])
         return (
             columns,
-            pltpu.make_async_copy(own_hbm.at[:, rows, :], own.at[step], own_sem.at[step]),
-            pltpu.make_async_copy(other_hbm.at[:, rows, :], other.at[step], other_sem.at[step]),
+            pltpu.make_async_copy(own_hbm.at[:, rows, :], own.at[:, rows, :], own_sem.at[step]),
+            pltpu.make_async_copy(other_hbm.at[:, rows, :], other.at[:, rows, :], other_sem.at[step]),
         )
 
-    for step in range(steps):
+    def screened(integrals, screen, p, start, end):
+        def tile(row, column):
+            block = integrals[p, row * TILE : (row + 1) * TILE, column * TILE : (column + 1) * TILE]
+            return block * screen[row, column].astype(F32)
+
+        return jnp.concatenate(
+            [
+                jnp.concatenate([tile(row, column) for column in range(width // TILE)], axis=1)
+                for row in range(start // TILE, end // TILE)
+            ],
+            axis=0,
+        )
+
+    for step in range(len(starts)):
         for copy in copies(step):
             copy.start()
-    for step in range(steps):
+    for step, (first_row, end_row) in enumerate(zip(starts, ends, strict=True)):
         for copy in copies(step):
             copy.wait()
-        coef_high, coef_low = split(coef[step] if step < steps - 1 else rest[...])
+        coef_high, coef_low = split(coef[:, first_row:end_row] if first_row < most else rest[...])
         for p in range(aux):
-            for place, integrals in enumerate((own, other)):
-                high, low = split(integrals[step, p])
+            for place, (integrals, screen) in enumerate(((own, own_screen), (other, other_screen))):
+                high, low = split(screened(integrals, screen, p, first_row, end_row))
                 part = jnp.dot(coef_high, low, preferred_element_type=F32)
                 part += jnp.dot(coef_low, high, preferred_element_type=F32)
                 part += jnp.dot(coef_high, high, preferred_element_type=F32)
                 columns = slice((2 * p + place) * width, (2 * p + place + 1) * width)
                 if step == 0:
                     total[:, columns] = part
-                elif step < steps - 1:
+                elif first_row < most:
                     total[:, columns] += part
                 else:
                     for z in range(NZ):
@@ -84,14 +100,12 @@
     copy.wait()
 
 
-def first(coef, rest, own, other, passed):
-    occ = coef.shape[0]
+def first(own_screen, other_screen, coef, rest, own, other, passed):
+    occ, most = coef.shape
     aux, full_depth, half_width = own.shape
-    depth = rest.shape[1]
-    steps = full_depth // depth
+    steps = most // CHUNK + 1
     width = 2 * aux * half_width
-    away = pl.BlockSpec(memory_space=pl.ANY)
-    block = pltpu.VMEM((steps, aux, depth, half_width), F32)
+    away, scalars = pl.BlockSpec(memory_space=pl.ANY), pl.BlockSpec(memory_space=pltpu.SMEM)
     sems = pltpu.SemaphoreType.DMA((steps,))
     return pl.pallas_call(
         first_kernel,
@@ -99,18 +113,17 @@
             jax.ShapeDtypeStruct((occ, width), F32),
             jax.ShapeDtypeStruct(passed.shape, passed.dtype),
         ),
-        in_specs=[away] * 5,
+        in_specs=[scalars, scalars] + [away] * 5,
         out_specs=(away, away),
-        input_output_aliases={4: 1},
+        input_output_aliases={6: 1},
         scratch_shapes=[
-            pltpu.VMEM((steps - 1, occ, depth), F32),
-            pltpu.VMEM((occ, depth), F32),
-            block,
-            block,
+            pltpu.VMEM(coef.shape, F32),
+            pltpu.VMEM(rest.shape, F32),
+            pltpu.VMEM(own.shape, F32),
+            pltpu.VMEM(other.shape, F32),
             pltpu.VMEM((occ, width), F32),
             pltpu.VMEM((occ, width), F32),
-            pltpu.SemaphoreType.DMA((steps - 1,)),
-            pltpu.SemaphoreType.DMA,
+            sems,
             sems,
             sems,
             pltpu.SemaphoreType.DMA,
@@ -119,7 +132,7 @@
         cost_estimate=pl.CostEstimate(
             flops=6 * occ * full_depth * width, bytes_accessed=14 * 2**20, transcendentals=0
         ),
-    )(coef, rest, own, other, passed)
+    )(own_screen, other_screen, coef, rest, own, other, passed)
 
 
 def second_kernel(rows_ref, halves_ref, out_ref):
@@ -181,18 +194,11 @@
     along_x = gather(coef[:, :most], "x")
     gathered = lax.all_gather(along_x.reshape(NX * occ, most), "z", axis=0, tiled=True)
 
-    keep = screen.astype(F32)
-    screened = (
-        integrals.reshape(aux, row_tiles, TILE, col_len // TILE, TILE) * keep[None, :, None, :, None]
-    ).reshape(integrals.shape)
-    other = swap(screened)
-
-    after = 0.0 * (along_x[0, 0, 0] + screened[0, 0, 0])
-    rest = gather(gather(coef[:, most:] + after, "z"), "x").reshape(NX * NZ * occ, REST)
-
-    along_y = around(coef + 0.0 * along_x[0, 0, 0], "y")
-
-    half, along_y = first(gathered, rest, screened, other, along_y)
+    rest = gather(gather(coef[:, most:] + 0.0 * along_x[0, :, :REST], "z"), "x").reshape(NX * NZ * occ, REST)
+
+    along_y = around(coef + 0.0 * jnp.pad(along_x[0], ((0, 0), (0, REST))), "y")
+
+    half, along_y = first(screen, swap(screen), gathered, rest, integrals, swap(integrals), along_y)
     half = lax.psum_scatter(half, "y", scatter_dimension=0, tiled=True)
 
     chip_len = 2 * col_len

time: 174 us -> 174 us (level)
  local copies, waits for them, and re-layouts: 7.72 us -> 4.24 us
  waiting for transfers between devices: 36.9 us -> 40.1 us
  starting transfers between devices: 50 us -> 52.4 us
  between operations: 15.6 us -> 13.7 us
    all_gather x1, waiting for transfers between devices: 0.57 us -> 5.06 us  [shards(): lax.all_gather(along_x.reshape(NX * occ, most), 'z', axis=0, tiled=True)]
    slice x3 -> x1, local copies, waits for them, and re-layouts: 2.47 us -> 0.09 us  [the longest x2 2.38 us: shards(): after = 0.0 * (along_x[0, 0, 0] + screened[0, 0, 0])]
    mul x1 -> x0, other arithmetic: 2.34 us -> none  [shards(): integrals.reshape(aux, row_tiles, TILE, col_len // TILE, TILE)]
    ppermute x1 -> x2, starting transfers between devices: 8.27 us -> 10.2 us  [swap(): return lax.ppermute(value, 'core', [(0, 1), (1, 0)])]
  transfers between devices with their start and end apart: 13 -> 14, of which waited for: 4 -> 4; matrix products, arithmetic and copies ran while one was open for 6% -> 4% of each run, Pallas kernels for 0% -> 0%
where the time goes in v8:
time: 174 us; the launch traced here: 171 us
  starting transfers between devices  52.4 us (30%)
  blocking collectives  41.7 us (24%)
  waiting for transfers between devices  40.1 us (23%)
  between operations  13.7 us (8%)
  Pallas kernels  13.5 us (8%)
  other arithmetic  5.21 us (3%)
  local copies, waits for them, and re-layouts  4.24 us (2%)
    reduce_scatter x1, waiting for transfers between devices, shards(): half = lax.psum_scatter(half, 'y', scatter_dimension=0, tiled=True)  29.5 us
    all_to_all x1, blocking collectives, shards(): pairs = lax.all_to_all(pairs, ('x', 'z'), 0, 0, tiled=True)  23.7 us
    ppermute x4, starting transfers between devices, around(): lax.ppermute(found[step - 1], axis, [(i, (i - 1) % count) for i in range(...  16.3 us
    all_to_all x2, starting transfers between devices, gather(): return lax.all_to_all(copies, axis, 0, 0, tiled=True)  12 us
    all_to_all x1, blocking collectives, gather(): return lax.all_to_all(copies, axis, 0, 0, tiled=True)  11.3 us
    pallas_call x1, Pallas kernels, first(): pl.pallas_call(first_kernel, out_shape=(jax.ShapeDtypeStruct((occ, width)...  11.2 us
    ppermute x2, starting transfers between devices, swap(): return lax.ppermute(value, 'core', [(0, 1), (1, 0)])  10.2 us
    ppermute x3, starting transfers between devices, around(): lax.ppermute(back, axis, [(i, (i + 1) % count) for i in range(count)])  7.2 us
  transfers between devices with their start and end apart: 14, of which 4 were waited for; matrix products, arithmetic and copies ran while one was open for 4% of the time, Pallas kernels for 0%

profile of v8, /device:TPU:1, one launch (start us, length us, event | category | flops | bytes accessed | tf_op | source)
XLA Modules:
  0.0 170.9 jit_solution(8351485113655927016)
XLA Ops:
  6.5 0.0 copy-start
  6.5 0.0 all-gather.3.cloned.1.call-start
  6.5 0.7 copy-done
  7.2 0.2 compare_reduce_fusion
  7.4 0.1 broadcast_bitcast_fusion
  7.5 0.9 multiply_bitcast_fusion
  8.5 11.3 %all_to_all.25 = f32[4,16,1792]{2,1,0:T(8,128)} all-to-all(f32[4,16,1792]{2,1,0:T(8,128)S(1)} %broadcast_in_dim.9), channel_id=1, replica_groups=mesh['y'=8,'x'=4,'z'=8,'core'=2] {'x'}, dimensions={0} | all-to-all | bytes 917504 | tf_op jit(solution)/shard_map/all_to_all | solution.py:26
  19.8 0.0 all-gather.3.cloned.1.call-update
  19.8 0.8 copy.9.own_screen
  20.6 0.0 copy-start.3
  20.6 8.3 %collective-permute-start = (s32[16,2]{1,0:T(8,128)S(1)}, s32[16,2]{1,0:T(8,128)S(1)}, u32[]{:S(2)}, u32[]{:S(2)}) collective-permute-start(s32[16,2]{1,0:T(8,128)S(1)} %copy.9.own_screen), channel_id=1, source_target_pairs={{0,1},{1,0},{2,3},{3,2},{4,5},{5,4},{6,7},{7,6},{8,9},{9,8},{10,11... | collective-permute-start | bytes 392 | tf_op jit(solution)/shard_map/ppermute | solution.py:21
  28.9 1.9 %collective-permute-start.1 = (f32[2,2048,256]{2,1,0:T(8,128)}, f32[2,2048,256]{2,1,0:T(8,128)}, u32[]{:S(2)}, u32[]{:S(2)}) collective-permute-start(f32[2,2048,256]{2,1,0:T(8,128)} %own_hbm.1), channel_id=1, source_target_pairs={{0,1},{1,0},{2,3},{3,2},{4,5},{5,4},{6,7},{7,6},{8,9},{9,8},{10,11... | collective-permute-start | bytes 12582920 | tf_op jit(solution)/shard_map/ppermute | solution.py:21
  30.8 0.9 slice_bitcast_fusion
  31.7 0.9 bitcast_dynamic-update-slice_fusion.7
  32.6 1.9 %collective-permute-start.2 = (f32[16,2048]{1,0:T(8,128)S(1)}, f32[16,2048]{1,0:T(8,128)S(1)}, u32[]{:S(2)}, u32[]{:S(2)}) collective-permute-start(f32[16,2048]{1,0:T(8,128)S(1)} %get-tuple-element.10), channel_id=1, source_target_pairs={{0,448},{64,0},{128,64},{192,128},{256,192},{320,256},{384,320},{4... | collective-permute-start | bytes 393224 | tf_op jit(solution)/shard_map/ppermute | solution.py:33
  34.6 3.4 %collective-permute-start.6 = (f32[16,2048]{1,0:T(8,128)S(1)}, f32[16,2048]{1,0:T(8,128)S(1)}, u32[]{:S(2)}, u32[]{:S(2)}) collective-permute-start(f32[16,2048]{1,0:T(8,128)S(1)} %get-tuple-element.10), channel_id=1, source_target_pairs={{0,64},{64,128},{128,192},{192,256},{256,320},{320,384},{384,448},... | collective-permute-start | bytes 393224 | tf_op jit(solution)/shard_map/ppermute | solution.py:36
  37.9 0.7 fusion.2
  38.6 0.7 broadcast_in_dim.10
  39.3 8.6 %all-to-all-start.1 = ((f32[8,16,256]{2,1,0:T(8,128)}), f32[8,16,256]{2,1,0:T(8,128)S(1)}, u32[]{:S(2)}, u32[]{:S(2)}) async-start(f32[8,16,256]{2,1,0:T(8,128)} %broadcast_in_dim.10), calls=%async_computation.1 | async-start | bytes 262144 | tf_op jit(solution)/shard_map/all_to_all | solution.py:26
  47.9 0.0 collective-permute-done.2
  47.9 4.6 %collective-permute-start.3 = (f32[16,2048]{1,0:T(8,128)S(1)}, f32[16,2048]{1,0:T(8,128)S(1)}, u32[]{:S(2)}, u32[]{:S(2)}) collective-permute-start(f32[16,2048]{1,0:T(8,128)S(1)} %collective-permute-done.2), channel_id=1, source_target_pairs={{0,448},{64,0},{128,64},{192,128},{256,192},{320,256},{384,320},{4... | collective-permute-start | bytes 393224 | tf_op jit(solution)/shard_map/ppermute | solution.py:33
  52.5 0.0 collective-permute-done.6
  52.5 1.9 %collective-permute-start.7 = (f32[16,2048]{1,0:T(8,128)S(1)}, f32[16,2048]{1,0:T(8,128)S(1)}, u32[]{:S(2)}, u32[]{:S(2)}) collective-permute-start(f32[16,2048]{1,0:T(8,128)S(1)} %collective-permute-done.6), channel_id=1, source_target_pairs={{0,64},{64,128},{128,192},{192,256},{256,320},{320,384},{384,448},... | collective-permute-start | bytes 393224 | tf_op jit(solution)/shard_map/ppermute | solution.py:36
  54.4 3.6 %all-to-all-done.1 = f32[8,16,256]{2,1,0:T(8,128)S(1)} async-done(((f32[8,16,256]{2,1,0:T(8,128)}), f32[8,16,256]{2,1,0:T(8,128)S(1)}, u32[]{:S(2)}, u32[]{:S(2)}) %all-to-all-start.1) | async-done | bytes 131104 | tf_op jit(solution)/shard_map/all_to_all | solution.py:26
  58.1 0.9 broadcast_in_dim.11
  59.0 3.5 %all-to-all-start.2 = ((f32[4,8,16,256]{3,2,1,0:T(8,128)}), f32[4,8,16,256]{3,2,1,0:T(8,128)S(1)}, u32[]{:S(2)}, u32[]{:S(2)}) async-start(f32[4,8,16,256]{3,2,1,0:T(8,128)} %broadcast_in_dim.11), calls=%async_computation.2 | async-start | bytes 1048576 | tf_op jit(solution)/shard_map/all_to_all | solution.py:26
  62.4 0.0 reduce-scatter.2.cloned.1.call-start
  62.5 0.0 collective-permute-done.3
  62.5 4.5 %collective-permute-start.4 = (f32[16,2048]{1,0:T(8,128)S(1)}, f32[16,2048]{1,0:T(8,128)S(1)}, u32[]{:S(2)}, u32[]{:S(2)}) collective-permute-start(f32[16,2048]{1,0:T(8,128)S(1)} %collective-permute-done.3), channel_id=1, source_target_pairs={{0,448},{64,0},{128,64},{192,128},{256,192},{320,256},{384,320},{4... | collective-permute-start | bytes 393224 | tf_op jit(solution)/shard_map/ppermute | solution.py:33
  67.0 0.0 collective-permute-done.7
  67.0 1.9 %collective-permute-start.8 = (f32[16,2048]{1,0:T(8,128)S(1)}, f32[16,2048]{1,0:T(8,128)S(1)}, u32[]{:S(2)}, u32[]{:S(2)}) collective-permute-start(f32[16,2048]{1,0:T(8,128)S(1)} %collective-permute-done.7), channel_id=1, source_target_pairs={{0,64},{64,128},{128,192},{192,256},{256,320},{320,384},{384,448},... | collective-permute-start | bytes 393224 | tf_op jit(solution)/shard_map/ppermute | solution.py:36
  68.9 0.0 collective-permute-done.4
  68.9 5.3 %collective-permute-start.5 = (f32[16,2048]{1,0:T(8,128)S(1)}, f32[16,2048]{1,0:T(8,128)S(1)}, u32[]{:S(2)}, u32[]{:S(2)}) collective-permute-start(f32[16,2048]{1,0:T(8,128)S(1)} %collective-permute-done.4), channel_id=1, source_target_pairs={{0,448},{64,0},{128,64},{192,128},{256,192},{320,256},{384,320},{4... | collective-permute-start | bytes 393224 | tf_op jit(solution)/shard_map/ppermute | solution.py:33
  74.3 1.9 %collective-permute-done.5 = f32[16,2048]{1,0:T(8,128)S(1)} collective-permute-done((f32[16,2048]{1,0:T(8,128)S(1)}, f32[16,2048]{1,0:T(8,128)S(1)}, u32[]{:S(2)}, u32[]{:S(2)}) %collective-permute-start.5) | collective-permute-done | bytes 131104 | tf_op jit(solution)/shard_map/ppermute | solution.py:33
  76.2 0.0 collective-permute-done.8
  76.3 0.0 copy-start.1
  76.3 0.0 collective-permute-done.other_screen
  76.3 0.0 copy-start.4
  76.3 0.0 all-to-all-done.2
  76.3 0.0 copy-start.2
  76.3 0.0 collective-permute-done.1.other_hbm
  76.4 5.1 %all-gather.3.cloned.1.call-done.coef_hbm = f32[512,1792]{1,0:T(8,128)} async-done(((f32[64,1792]{1,0:T(8,128)}), f32[512,1792]{1,0:T(8,128)}) %all-gather.3.cloned.1.call-update) | async-done | bytes 3670032 | tf_op jit(solution)/shard_map/all_gather | solution.py:195
  81.4 0.0 copy-done.3
  81.4 0.0 copy-done.1
  81.4 0.0 copy-done.4
  81.4 0.0 copy-done.2
  81.4 11.2 %shard_map.46 = (f32[512,1024]{1,0:T(8,128)}, f32[8,16,2048]{2,1,0:T(8,128)}) custom-call(s32[16,2]{1,0:T(8,128)} %copy-done.3, s32[16,2]{1,0:T(8,128)} %copy-done.4, f32[512,1792]{1,0:T(8,128)} %all-gather.3.cloned.1.call-done.coef_hbm, f32[512,256]{1,0:T(8,128)} %bitcast.41, f32[2,2048,256]{2,1,0:T(8,128)} %own_hbm.1, ...), custom_call_target="tpu_custom_call", output_to_operand_aliasing={{1}: (6, {})} | custom-call | flops 6442450944 | bytes 14680064 | tf_op jit(solution)/shard_map/pallas_call | solution.py:110
  92.6 0.0 reduce-scatter.2.cloned.1.call-update
  92.6 1.4 fusion
  94.0 0.1 fusion.4
  94.1 1.1 pad_maximum_fusion
  95.2 6.7 %all-to-all-start.3 = ((f32[32,16,512]{2,1,0:T(8,128)}), f32[32,16,512]{2,1,0:T(8,128)S(1)}, u32[]{:S(2)}, u32[]{:S(2)}) async-start(f32[32,16,512]{2,1,0:T(8,128)} %bitcast.15), calls=%async_computation.3 | async-start | bytes 2097152 | tf_op jit(solution)/shard_map/all_to_all | solution.py:207
  101.8 29.5 %reduce-scatter.2.cloned.1.call-done = f32[64,1024]{1,0:T(8,128)} async-done(((f32[512,1024]{1,0:T(8,128)}), f32[64,1024]{1,0:T(8,128)}) %reduce-scatter.2.cloned.1.call-update) | async-done | bytes 262160 | tf_op jit(solution)/shard_map/reduce_scatter | solution.py:202
  131.3 6.7 %all-gather = f32[128,1024]{1,0:T(8,128)S(1)} all-gather(f32[64,1024]{1,0:T(8,128)} %reduce-scatter.2.cloned.1.call-done), channel_id=2, replica_groups=mesh['y'=8,'x'=4,'z'=8,'core'=2] {'core'}, dimensions={0}, use_global_device_ids=true | all-gather | bytes 786432 | tf_op jit(solution)/shard_map/all_gather | solution.py:208
  138.0 0.0 all-to-all-done.3
  138.0 0.6 shard_map.47
  138.6 23.7 %all_to_all.26.parts_ref = f32[32,16,256]{2,1,0:T(8,128)} all-to-all(f32[32,16,256]{2,1,0:T(8,128)S(1)} %bitcast.39), channel_id=1, replica_groups=mesh['y'=8,'x'=4,'z'=8,'core'=2] {'x','z'}, dimensions={0} | all-to-all | bytes 1048576 | tf_op jit(solution)/shard_map/all_to_all | solution.py:210
  162.3 1.7 shard_map.48
  (12 shorter events, 0.1 us)
Async XLA Ops:
  6.5 0.7 copy-start
  6.5 74.9 %all-gather.3.cloned.1.call-start = ((), (), s32[]{:S(2)}) async-start(), calls=%async_computation.6 | async-start | bytes 4128768 | tf_op jit(solution)/shard_map/all_gather | solution.py:195
  20.6 60.8 %copy-start.3 = (s32[16,2]{1,0:T(8,128)}, s32[16,2]{1,0:T(8,128)S(1)}, u32[]{:S(2)}) copy-start(s32[16,2]{1,0:T(8,128)S(1)} %copy.9.own_screen) | copy-start | bytes 388
  20.6 55.7 %collective-permute-start = (s32[16,2]{1,0:T(8,128)S(1)}, s32[16,2]{1,0:T(8,128)S(1)}, u32[]{:S(2)}, u32[]{:S(2)}) collective-permute-start(s32[16,2]{1,0:T(8,128)S(1)} %copy.9.own_screen), channel_id=1, source_target_pairs={{0,1},{1,0},{2,3},{3,2},{4,5},{5,4},{6,7},{7,6},{8,9},{9,8},{10,11... | collective-permute-start | bytes 392 | tf_op jit(solution)/shard_map/ppermute | solution.py:21
  28.9 47.5 %collective-permute-start.1 = (f32[2,2048,256]{2,1,0:T(8,128)}, f32[2,2048,256]{2,1,0:T(8,128)}, u32[]{:S(2)}, u32[]{:S(2)}) collective-permute-start(f32[2,2048,256]{2,1,0:T(8,128)} %own_hbm.1), channel_id=1, source_target_pairs={{0,1},{1,0},{2,3},{3,2},{4,5},{5,4},{6,7},{7,6},{8,9},{9,8},{10,11... | collective-permute-start | bytes 12582920 | tf_op jit(solution)/shard_map/ppermute | solution.py:21
  32.6 15.3 %collective-permute-start.2 = (f32[16,2048]{1,0:T(8,128)S(1)}, f32[16,2048]{1,0:T(8,128)S(1)}, u32[]{:S(2)}, u32[]{:S(2)}) collective-permute-start(f32[16,2048]{1,0:T(8,128)S(1)} %get-tuple-element.10), channel_id=1, source_target_pairs={{0,448},{64,0},{128,64},{192,128},{256,192},{320,256},{384,320},{4... | collective-permute-start | bytes 393224 | tf_op jit(solution)/shard_map/ppermute | solution.py:33
  34.6 18.0 %collective-permute-start.6 = (f32[16,2048]{1,0:T(8,128)S(1)}, f32[16,2048]{1,0:T(8,128)S(1)}, u32[]{:S(2)}, u32[]{:S(2)}) collective-permute-start(f32[16,2048]{1,0:T(8,128)S(1)} %get-tuple-element.10), channel_id=1, source_target_pairs={{0,64},{64,128},{128,192},{192,256},{256,320},{320,384},{384,448},... | collective-permute-start | bytes 393224 | tf_op jit(solution)/shard_map/ppermute | solution.py:36
  39.3 18.7 %all-to-all-start.1 = ((f32[8,16,256]{2,1,0:T(8,128)}), f32[8,16,256]{2,1,0:T(8,128)S(1)}, u32[]{:S(2)}, u32[]{:S(2)}) async-start(f32[8,16,256]{2,1,0:T(8,128)} %broadcast_in_dim.10), calls=%async_computation.1 | async-start | bytes 262144 | tf_op jit(solution)/shard_map/all_to_all | solution.py:26
  47.9 14.6 %collective-permute-start.3 = (f32[16,2048]{1,0:T(8,128)S(1)}, f32[16,2048]{1,0:T(8,128)S(1)}, u32[]{:S(2)}, u32[]{:S(2)}) collective-permute-start(f32[16,2048]{1,0:T(8,128)S(1)} %collective-permute-done.2), channel_id=1, source_target_pairs={{0,448},{64,0},{128,64},{192,128},{256,192},{320,256},{384,320},{4... | collective-permute-start | bytes 393224 | tf_op jit(solution)/shard_map/ppermute | solution.py:33
  52.5 14.5 %collective-permute-start.7 = (f32[16,2048]{1,0:T(8,128)S(1)}, f32[16,2048]{1,0:T(8,128)S(1)}, u32[]{:S(2)}, u32[]{:S(2)}) collective-permute-start(f32[16,2048]{1,0:T(8,128)S(1)} %collective-permute-done.6), channel_id=1, source_target_pairs={{0,64},{64,128},{128,192},{192,256},{256,320},{320,384},{384,448},... | collective-permute-start | bytes 393224 | tf_op jit(solution)/shard_map/ppermute | solution.py:36
  59.0 17.4 %all-to-all-start.2 = ((f32[4,8,16,256]{3,2,1,0:T(8,128)}), f32[4,8,16,256]{3,2,1,0:T(8,128)S(1)}, u32[]{:S(2)}, u32[]{:S(2)}) async-start(f32[4,8,16,256]{3,2,1,0:T(8,128)} %broadcast_in_dim.11), calls=%async_computation.2 | async-start | bytes 1048576 | tf_op jit(solution)/shard_map/all_to_all | solution.py:26
  62.4 68.9 %reduce-scatter.2.cloned.1.call-start = ((), (), s32[]{:S(2)}) async-start(), calls=%async_computation.7 | async-start | bytes 2359296 | tf_op jit(solution)/shard_map/reduce_scatter | solution.py:202
  62.5 6.4 %collective-permute-start.4 = (f32[16,2048]{1,0:T(8,128)S(1)}, f32[16,2048]{1,0:T(8,128)S(1)}, u32[]{:S(2)}, u32[]{:S(2)}) collective-permute-start(f32[16,2048]{1,0:T(8,128)S(1)} %collective-permute-done.3), channel_id=1, source_target_pairs={{0,448},{64,0},{128,64},{192,128},{256,192},{320,256},{384,320},{4... | collective-permute-start | bytes 393224 | tf_op jit(solution)/shard_map/ppermute | solution.py:33
  67.0 9.2 %collective-permute-start.8 = (f32[16,2048]{1,0:T(8,128)S(1)}, f32[16,2048]{1,0:T(8,128)S(1)}, u32[]{:S(2)}, u32[]{:S(2)}) collective-permute-start(f32[16,2048]{1,0:T(8,128)S(1)} %collective-permute-done.7), channel_id=1, source_target_pairs={{0,64},{64,128},{128,192},{192,256},{256,320},{320,384},{384,448},... | collective-permute-start | bytes 393224 | tf_op jit(solution)/shard_map/ppermute | solution.py:36
  68.9 7.3 %collective-permute-start.5 = (f32[16,2048]{1,0:T(8,128)S(1)}, f32[16,2048]{1,0:T(8,128)S(1)}, u32[]{:S(2)}, u32[]{:S(2)}) collective-permute-start(f32[16,2048]{1,0:T(8,128)S(1)} %collective-permute-done.4), channel_id=1, source_target_pairs={{0,448},{64,0},{128,64},{192,128},{256,192},{320,256},{384,320},{4... | collective-permute-start | bytes 393224 | tf_op jit(solution)/shard_map/ppermute | solution.py:33
  76.3 5.1 %copy-start.1 = (f32[8,16,2048]{2,1,0:T(8,128)}, f32[8,16,2048]{2,1,0:T(8,128)S(1)}, u32[]{:S(2)}) copy-start(f32[8,16,2048]{2,1,0:T(8,128)S(1)} %bitcast_dynamic-update-slice_fusion.passed_hbm) | copy-start | bytes 3145732
  76.3 5.1 %copy-start.4 = (s32[16,2]{1,0:T(8,128)}, s32[16,2]{1,0:T(8,128)S(1)}, u32[]{:S(2)}) copy-start(s32[16,2]{1,0:T(8,128)S(1)} %collective-permute-done.other_screen) | copy-start | bytes 388
  76.3 5.1 %copy-start.2 = (f32[4,8,16,256]{3,2,1,0:T(8,128)}, f32[4,8,16,256]{3,2,1,0:T(8,128)S(1)}, u32[]{:S(2)}) copy-start(f32[4,8,16,256]{3,2,1,0:T(8,128)S(1)} %all-to-all-done.2) | copy-start | bytes 1572868
  95.2 42.8 %all-to-all-start.3 = ((f32[32,16,512]{2,1,0:T(8,128)}), f32[32,16,512]{2,1,0:T(8,128)S(1)}, u32[]{:S(2)}, u32[]{:S(2)}) async-start(f32[32,16,512]{2,1,0:T(8,128)} %bitcast.15), calls=%async_computation.3 | async-start | bytes 2097152 | tf_op jit(solution)/shard_map/all_to_all | solution.py:207
Sparse Core Ops, SparseCore 0:
  20.0 61.4 all-gather.2
  92.8 38.5 reduce-scatter.1

commit v9 on v8

--- a/solution.py
+++ b/solution.py
@@ -7,7 +7,7 @@
 
 TILE = 128
 NX, NZ = 4, 8
-REST, CHUNK = 256, 256
+REST, CHUNK = 512, 256
 BF16 = jnp.bfloat16
 F32 = jnp.float32
 
@@ -103,7 +103,7 @@
 def first(own_screen, other_screen, coef, rest, own, other, passed):
     occ, most = coef.shape
     aux, full_depth, half_width = own.shape
-    steps = most // CHUNK + 1
+    steps = -(-most // CHUNK) + 1
     width = 2 * aux * half_width
     away, scalars = pl.BlockSpec(memory_space=pl.ANY), pl.BlockSpec(memory_space=pltpu.SMEM)
     sems = pltpu.SemaphoreType.DMA((steps,))
@@ -194,9 +194,10 @@
     along_x = gather(coef[:, :most], "x")
     gathered = lax.all_gather(along_x.reshape(NX * occ, most), "z", axis=0, tiled=True)
 
-    rest = gather(gather(coef[:, most:] + 0.0 * along_x[0, :, :REST], "z"), "x").reshape(NX * NZ * occ, REST)
-
-    along_y = around(coef + 0.0 * jnp.pad(along_x[0], ((0, 0), (0, REST))), "y")
+    along_z = gather(coef[:, most:] + 0.0 * along_x[0, :, :REST], "z")
+    rest = gather(along_z, "x").reshape(NX * NZ * occ, REST)
+
+    along_y = around(coef + 0.0 * jnp.pad(along_z[0], ((0, 0), (0, most))), "y")
 
     half, along_y = first(screen, swap(screen), gathered, rest, integrals, swap(integrals), along_y)
     half = lax.psum_scatter(half, "y", scatter_dimension=0, tiled=True)
@@ -206,8 +207,9 @@
     along_y = along_y.reshape(8, occ, row_len // chip_len, chip_len).transpose(0, 2, 1, 3)
     rows = lax.all_to_all(along_y.reshape(NX * NZ, occ, chip_len), ("x", "z"), 0, 0, tiled=True)
     pairs = second(rows.reshape(NX * NZ * occ, chip_len), lax.all_gather(half, "core"))
-    pairs = pairs.reshape(NX * NZ, occ, pairs.shape[1])
-    pairs = lax.all_to_all(pairs, ("x", "z"), 0, 0, tiled=True)
+    pairs = pairs.reshape(NX, NZ, occ, pairs.shape[1])
+    pairs = lax.all_to_all(pairs, "x", 0, 0, tiled=True).sum(axis=0)
+    pairs = lax.all_to_all(pairs, "z", 0, 0, tiled=True)
     return last(pairs).transpose(0, 2, 1)
 
 

time: 174 us -> 175 us (level)
  blocking collectives: 41.7 us -> 44.9 us
  starting transfers between devices: 52.4 us -> 54.7 us
  waiting for transfers between devices: 40.1 us -> 38.1 us
    all_gather x1, waiting for transfers between devices: 5.06 us -> 0.02 us  [shards(): lax.all_gather(along_x.reshape(NX * occ, most), 'z', axis=0, tiled=True)]
    ppermute x4, starting transfers between devices: 16.3 us -> 20.3 us  [around(): lax.ppermute(found[step - 1], axis, [(i, (i - 1) % count) for i in range(...]
    all_to_all x1 -> x2, blocking collectives: 23.7 us -> 27.4 us  [the longest x1 15 us: shards(): pairs = lax.all_to_all(pairs, 'z', 0, 0, tiled=True)]
    all_to_all x2, starting transfers between devices: 12 us -> 14.5 us  [gather(): return lax.all_to_all(copies, axis, 0, 0, tiled=True)]
    all_to_all x1, starting transfers between devices: 6.67 us -> 4.26 us  [shards(): lax.all_to_all(along_y.reshape(NX * NZ, occ, chip_len), ('x', 'z'), 0, 0,...]
  transfers between devices with their start and end apart: 14 -> 14, of which waited for: 4 -> 4; matrix products, arithmetic and copies ran while one was open for 4% -> 3% of each run, Pallas kernels for 0% -> 0%
where the time goes in v9:
time: 175 us; the launch traced here: 173 us
  starting transfers between devices  54.7 us (31%)
  blocking collectives  44.9 us (26%)
  waiting for transfers between devices  38.1 us (22%)
  between operations  13.8 us (8%)
  Pallas kernels  13.2 us (8%)
  other arithmetic  4.38 us (3%)
  local copies, waits for them, and re-layouts  4.12 us (2%)
    reduce_scatter x1, waiting for transfers between devices, shards(): half = lax.psum_scatter(half, 'y', scatter_dimension=0, tiled=True)  30.3 us
    ppermute x4, starting transfers between devices, around(): lax.ppermute(found[step - 1], axis, [(i, (i - 1) % count) for i in range(...  20.3 us
    all_to_all x1, blocking collectives, shards(): pairs = lax.all_to_all(pairs, 'z', 0, 0, tiled=True)  15 us
    all_to_all x2, starting transfers between devices, gather(): return lax.all_to_all(copies, axis, 0, 0, tiled=True)  14.5 us
    all_to_all x1, blocking collectives, shards(): pairs = lax.all_to_all(pairs, 'x', 0, 0, tiled=True).sum(axis=0)  12.4 us
    pallas_call x1, Pallas kernels, first(): pl.pallas_call(first_kernel, out_shape=(jax.ShapeDtypeStruct((occ, width)...  11.1 us
    all_to_all x1, blocking collectives, gather(): return lax.all_to_all(copies, axis, 0, 0, tiled=True)  11 us
    ppermute x2, starting transfers between devices, swap(): return lax.ppermute(value, 'core', [(0, 1), (1, 0)])  9.79 us
  transfers between devices with their start and end apart: 14, of which 4 were waited for; matrix products, arithmetic and copies ran while one was open for 3% of the time, Pallas kernels for 0%

profile of v9, /device:TPU:1, one launch (start us, length us, event | category | flops | bytes accessed | tf_op | source)
XLA Modules:
  0.0 173.1 jit_solution(12769998968026759696)
XLA Ops:
  6.5 0.0 copy-start
  6.5 0.0 copy-start.3
  6.5 0.0 copy-start.5
  6.5 0.0 all-gather.3.cloned.1.call-start
  6.6 0.6 copy-done
  7.2 0.2 compare_reduce_fusion
  7.4 0.1 broadcast_bitcast_fusion
  7.5 0.9 multiply_bitcast_fusion
  8.5 11.0 %all_to_all.30 = f32[4,16,1536]{2,1,0:T(8,128)} all-to-all(f32[4,16,1536]{2,1,0:T(8,128)S(1)} %broadcast_in_dim.9), channel_id=1, replica_groups=mesh['y'=8,'x'=4,'z'=8,'core'=2] {'x'}, dimensions={0} | all-to-all | bytes 786432 | tf_op jit(solution)/shard_map/all_to_all | solution.py:26
  19.5 0.0 all-gather.3.cloned.1.call-update
  19.5 0.8 fusion.2
  20.2 0.7 broadcast_in_dim.10
  21.0 11.0 %all-to-all-start.1 = ((f32[8,16,512]{2,1,0:T(8,128)}), f32[8,16,512]{2,1,0:T(8,128)S(1)}, u32[]{:S(2)}, u32[]{:S(2)}) async-start(f32[8,16,512]{2,1,0:T(8,128)} %broadcast_in_dim.10), calls=%async_computation.1 | async-start | bytes 524288 | tf_op jit(solution)/shard_map/all_to_all | solution.py:26
  31.9 4.0 %collective-permute-start.1 = (f32[2,2048,256]{2,1,0:T(8,128)}, f32[2,2048,256]{2,1,0:T(8,128)}, u32[]{:S(2)}, u32[]{:S(2)}) collective-permute-start(f32[2,2048,256]{2,1,0:T(8,128)} %own_hbm.1), channel_id=1, source_target_pairs={{0,1},{1,0},{2,3},{3,2},{4,5},{5,4},{6,7},{7,6},{8,9},{9,8},{10,11... | collective-permute-start | bytes 12582920 | tf_op jit(solution)/shard_map/ppermute | solution.py:21
  36.0 5.3 %all-to-all-done.1 = f32[8,16,512]{2,1,0:T(8,128)S(1)} async-done(((f32[8,16,512]{2,1,0:T(8,128)}), f32[8,16,512]{2,1,0:T(8,128)S(1)}, u32[]{:S(2)}, u32[]{:S(2)}) %all-to-all-start.1) | async-done | bytes 262176 | tf_op jit(solution)/shard_map/all_to_all | solution.py:26
  41.3 0.0 copy-done.3
  41.3 5.1 %collective-permute-start.2 = (f32[16,2048]{1,0:T(8,128)S(1)}, f32[16,2048]{1,0:T(8,128)S(1)}, u32[]{:S(2)}, u32[]{:S(2)}) collective-permute-start(f32[16,2048]{1,0:T(8,128)S(1)} %get-tuple-element.10), channel_id=1, source_target_pairs={{0,448},{64,0},{128,64},{192,128},{256,192},{320,256},{384,320},{4... | collective-permute-start | bytes 393224 | tf_op jit(solution)/shard_map/ppermute | solution.py:33
  46.4 0.0 copy-done.5
  46.4 0.1 copy.9.own_screen
  46.5 0.0 copy-start.4
  46.5 5.7 %collective-permute-start = (s32[16,2]{1,0:T(8,128)S(1)}, s32[16,2]{1,0:T(8,128)S(1)}, u32[]{:S(2)}, u32[]{:S(2)}) collective-permute-start(s32[16,2]{1,0:T(8,128)S(1)} %copy.9.own_screen), channel_id=1, source_target_pairs={{0,1},{1,0},{2,3},{3,2},{4,5},{5,4},{6,7},{7,6},{8,9},{9,8},{10,11... | collective-permute-start | bytes 392 | tf_op jit(solution)/shard_map/ppermute | solution.py:21
  52.2 1.9 %collective-permute-start.6 = (f32[16,2048]{1,0:T(8,128)S(1)}, f32[16,2048]{1,0:T(8,128)S(1)}, u32[]{:S(2)}, u32[]{:S(2)}) collective-permute-start(f32[16,2048]{1,0:T(8,128)S(1)} %get-tuple-element.10), channel_id=1, source_target_pairs={{0,64},{64,128},{128,192},{192,256},{256,320},{320,384},{384,448},... | collective-permute-start | bytes 393224 | tf_op jit(solution)/shard_map/ppermute | solution.py:36
  54.2 1.2 broadcast_in_dim.11
  55.3 3.5 %all-to-all-start.2 = ((f32[4,8,16,512]{3,2,1,0:T(8,128)}), f32[4,8,16,512]{3,2,1,0:T(8,128)S(1)}, u32[]{:S(2)}, u32[]{:S(2)}) async-start(f32[4,8,16,512]{3,2,1,0:T(8,128)} %broadcast_in_dim.11), calls=%async_computation.2 | async-start | bytes 2097152 | tf_op jit(solution)/shard_map/all_to_all | solution.py:26
  58.9 0.0 reduce-scatter.2.cloned.1.call-start
  58.9 0.0 collective-permute-done.2
  58.9 4.6 %collective-permute-start.3 = (f32[16,2048]{1,0:T(8,128)S(1)}, f32[16,2048]{1,0:T(8,128)S(1)}, u32[]{:S(2)}, u32[]{:S(2)}) collective-permute-start(f32[16,2048]{1,0:T(8,128)S(1)} %collective-permute-done.2), channel_id=1, source_target_pairs={{0,448},{64,0},{128,64},{192,128},{256,192},{320,256},{384,320},{4... | collective-permute-start | bytes 393224 | tf_op jit(solution)/shard_map/ppermute | solution.py:33
  63.5 0.0 collective-permute-done.6
  63.5 1.9 %collective-permute-start.7 = (f32[16,2048]{1,0:T(8,128)S(1)}, f32[16,2048]{1,0:T(8,128)S(1)}, u32[]{:S(2)}, u32[]{:S(2)}) collective-permute-start(f32[16,2048]{1,0:T(8,128)S(1)} %collective-permute-done.6), channel_id=1, source_target_pairs={{0,64},{64,128},{128,192},{192,256},{256,320},{320,384},{384,448},... | collective-permute-start | bytes 393224 | tf_op jit(solution)/shard_map/ppermute | solution.py:36
  65.5 0.6 collective-permute-done.3
  66.1 5.4 %collective-permute-start.4 = (f32[16,2048]{1,0:T(8,128)S(1)}, f32[16,2048]{1,0:T(8,128)S(1)}, u32[]{:S(2)}, u32[]{:S(2)}) collective-permute-start(f32[16,2048]{1,0:T(8,128)S(1)} %collective-permute-done.3), channel_id=1, source_target_pairs={{0,448},{64,0},{128,64},{192,128},{256,192},{320,256},{384,320},{4... | collective-permute-start | bytes 393224 | tf_op jit(solution)/shard_map/ppermute | solution.py:33
  71.5 0.0 collective-permute-done.7
  71.5 1.9 %collective-permute-start.8 = (f32[16,2048]{1,0:T(8,128)S(1)}, f32[16,2048]{1,0:T(8,128)S(1)}, u32[]{:S(2)}, u32[]{:S(2)}) collective-permute-start(f32[16,2048]{1,0:T(8,128)S(1)} %collective-permute-done.7), channel_id=1, source_target_pairs={{0,64},{64,128},{128,192},{192,256},{256,320},{320,384},{384,448},... | collective-permute-start | bytes 393224 | tf_op jit(solution)/shard_map/ppermute | solution.py:36
  73.5 0.0 collective-permute-done.4
  73.5 5.2 %collective-permute-start.5 = (f32[16,2048]{1,0:T(8,128)S(1)}, f32[16,2048]{1,0:T(8,128)S(1)}, u32[]{:S(2)}, u32[]{:S(2)}) collective-permute-start(f32[16,2048]{1,0:T(8,128)S(1)} %collective-permute-done.4), channel_id=1, source_target_pairs={{0,448},{64,0},{128,64},{192,128},{256,192},{320,256},{384,320},{4... | collective-permute-start | bytes 393224 | tf_op jit(solution)/shard_map/ppermute | solution.py:33
  78.7 1.9 %collective-permute-done.5 = f32[16,2048]{1,0:T(8,128)S(1)} collective-permute-done((f32[16,2048]{1,0:T(8,128)S(1)}, f32[16,2048]{1,0:T(8,128)S(1)}, u32[]{:S(2)}, u32[]{:S(2)}) %collective-permute-start.5) | collective-permute-done | bytes 131104 | tf_op jit(solution)/shard_map/ppermute | solution.py:33
  80.7 0.0 collective-permute-done.8
  80.7 0.0 copy-start.1
  80.7 0.0 collective-permute-done.other_screen
  80.7 0.0 copy-start.6
  80.8 0.0 all-to-all-done.2
  80.8 0.0 copy-start.2
  80.8 0.0 collective-permute-done.1.other_hbm
  80.8 0.0 all-gather.3.cloned.1.call-done.coef_hbm
  80.8 0.0 copy-done.4
  80.8 0.9 copy-done.1
  81.7 0.0 copy-done.6
  81.7 0.3 copy-done.2
  82.0 11.1 %shard_map.46 = (f32[512,1024]{1,0:T(8,128)}, f32[8,16,2048]{2,1,0:T(8,128)}) custom-call(s32[16,2]{1,0:T(8,128)} %copy-done.4, s32[16,2]{1,0:T(8,128)} %copy-done.6, f32[512,1536]{1,0:T(8,128)} %all-gather.3.cloned.1.call-done.coef_hbm, f32[512,512]{1,0:T(8,128)} %bitcast.41, f32[2,2048,256]{2,1,0:T(8,128)} %own_hbm.1, ...), custom_call_target="tpu_custom_call", output_to_operand_aliasing={{1}: (6, {})} | custom-call | flops 6442450944 | bytes 14680064 | tf_op jit(solution)/shard_map/pallas_call | solution.py:110
  93.1 0.0 reduce-scatter.2.cloned.1.call-update
  93.1 1.4 fusion
  94.5 0.1 fusion.4
  94.6 1.1 pad_maximum_fusion
  95.7 4.3 %all-to-all-start.3 = ((f32[32,16,512]{2,1,0:T(8,128)}), f32[32,16,512]{2,1,0:T(8,128)S(1)}, u32[]{:S(2)}, u32[]{:S(2)}) async-start(f32[32,16,512]{2,1,0:T(8,128)} %bitcast.15), calls=%async_computation.3 | async-start | bytes 2097152 | tf_op jit(solution)/shard_map/all_to_all | solution.py:208
  100.0 30.3 %reduce-scatter.2.cloned.1.call-done = f32[64,1024]{1,0:T(8,128)} async-done(((f32[512,1024]{1,0:T(8,128)}), f32[64,1024]{1,0:T(8,128)}) %reduce-scatter.2.cloned.1.call-update) | async-done | bytes 262160 | tf_op jit(solution)/shard_map/reduce_scatter | solution.py:203
  130.2 6.5 %all-gather = f32[128,1024]{1,0:T(8,128)S(1)} all-gather(f32[64,1024]{1,0:T(8,128)} %reduce-scatter.2.cloned.1.call-done), channel_id=2, replica_groups=mesh['y'=8,'x'=4,'z'=8,'core'=2] {'core'}, dimensions={0}, use_global_device_ids=true | all-gather | bytes 786432 | tf_op jit(solution)/shard_map/all_gather | solution.py:209
  136.7 0.0 all-to-all-done.3
  136.7 0.6 shard_map.47
  137.3 12.4 %all_to_all.31 = f32[4,8,16,256]{3,2,1,0:T(8,128)S(1)} all-to-all(f32[4,8,16,256]{3,2,1,0:T(8,128)S(1)} %bitcast.39), channel_id=1, replica_groups=mesh['y'=8,'x'=4,'z'=8,'core'=2] {'x'}, dimensions={0} | all-to-all | bytes 1048576 | tf_op jit(solution)/shard_map/all_to_all | solution.py:211
  149.8 15.0 %all_to_all.32.parts_ref = f32[8,16,256]{2,1,0:T(8,128)} all-to-all(f32[8,16,256]{2,1,0:T(8,128)S(1)} %reduce_sum.9), channel_id=1, replica_groups=mesh['y'=8,'x'=4,'z'=8,'core'=2] {'z'}, dimensions={0} | all-to-all | bytes 262144 | tf_op jit(solution)/shard_map/all_to_all | solution.py:212
  164.8 1.5 shard_map.48
  (15 shorter events, 0.2 us)
Async XLA Ops:
  6.5 0.7 copy-start
  6.5 34.7 %copy-start.3 = (f32[2048,16]{0,1:T(8,128)S(1)}, f32[2048,16]{0,1:T(8,128)}, u32[]{:S(2)}) copy-start(f32[2048,16]{0,1:T(8,128)} %param.5) | copy-start | bytes 393220
  6.5 39.8 %copy-start.5 = (s32[16,2]{0,1:T(2,128)S(1)}, s32[16,2]{0,1:T(2,128)}, u32[]{:S(2)}) copy-start(s32[16,2]{0,1:T(2,128)} %param.6) | copy-start | bytes 388
  6.5 74.3 %all-gather.3.cloned.1.call-start = ((), (), s32[]{:S(2)}) async-start(), calls=%async_computation.7 | async-start | bytes 3538944 | tf_op jit(solution)/shard_map/all_gather | solution.py:195
  21.0 20.3 %all-to-all-start.1 = ((f32[8,16,512]{2,1,0:T(8,128)}), f32[8,16,512]{2,1,0:T(8,128)S(1)}, u32[]{:S(2)}, u32[]{:S(2)}) async-start(f32[8,16,512]{2,1,0:T(8,128)} %broadcast_in_dim.10), calls=%async_computation.1 | async-start | bytes 524288 | tf_op jit(solution)/shard_map/all_to_all | solution.py:26
  31.9 48.8 %collective-permute-start.1 = (f32[2,2048,256]{2,1,0:T(8,128)}, f32[2,2048,256]{2,1,0:T(8,128)}, u32[]{:S(2)}, u32[]{:S(2)}) collective-permute-start(f32[2,2048,256]{2,1,0:T(8,128)} %own_hbm.1), channel_id=1, source_target_pairs={{0,1},{1,0},{2,3},{3,2},{4,5},{5,4},{6,7},{7,6},{8,9},{9,8},{10,11... | collective-permute-start | bytes 12582920 | tf_op jit(solution)/shard_map/ppermute | solution.py:21
  41.3 17.6 %collective-permute-start.2 = (f32[16,2048]{1,0:T(8,128)S(1)}, f32[16,2048]{1,0:T(8,128)S(1)}, u32[]{:S(2)}, u32[]{:S(2)}) collective-permute-start(f32[16,2048]{1,0:T(8,128)S(1)} %get-tuple-element.10), channel_id=1, source_target_pairs={{0,448},{64,0},{128,64},{192,128},{256,192},{320,256},{384,320},{4... | collective-permute-start | bytes 393224 | tf_op jit(solution)/shard_map/ppermute | solution.py:33
  46.5 34.3 %copy-start.4 = (s32[16,2]{1,0:T(8,128)}, s32[16,2]{1,0:T(8,128)S(1)}, u32[]{:S(2)}) copy-start(s32[16,2]{1,0:T(8,128)S(1)} %copy.9.own_screen) | copy-start | bytes 388
  46.5 34.3 %collective-permute-start = (s32[16,2]{1,0:T(8,128)S(1)}, s32[16,2]{1,0:T(8,128)S(1)}, u32[]{:S(2)}, u32[]{:S(2)}) collective-permute-start(s32[16,2]{1,0:T(8,128)S(1)} %copy.9.own_screen), channel_id=1, source_target_pairs={{0,1},{1,0},{2,3},{3,2},{4,5},{5,4},{6,7},{7,6},{8,9},{9,8},{10,11... | collective-permute-start | bytes 392 | tf_op jit(solution)/shard_map/ppermute | solution.py:21
  52.2 11.3 %collective-permute-start.6 = (f32[16,2048]{1,0:T(8,128)S(1)}, f32[16,2048]{1,0:T(8,128)S(1)}, u32[]{:S(2)}, u32[]{:S(2)}) collective-permute-start(f32[16,2048]{1,0:T(8,128)S(1)} %get-tuple-element.10), channel_id=1, source_target_pairs={{0,64},{64,128},{128,192},{192,256},{256,320},{320,384},{384,448},... | collective-permute-start | bytes 393224 | tf_op jit(solution)/shard_map/ppermute | solution.py:36
  55.3 25.4 %all-to-all-start.2 = ((f32[4,8,16,512]{3,2,1,0:T(8,128)}), f32[4,8,16,512]{3,2,1,0:T(8,128)S(1)}, u32[]{:S(2)}, u32[]{:S(2)}) async-start(f32[4,8,16,512]{3,2,1,0:T(8,128)} %broadcast_in_dim.11), calls=%async_computation.2 | async-start | bytes 2097152 | tf_op jit(solution)/shard_map/all_to_all | solution.py:26
  58.9 71.3 %reduce-scatter.2.cloned.1.call-start = ((), (), s32[]{:S(2)}) async-start(), calls=%async_computation.8 | async-start | bytes 2359296 | tf_op jit(solution)/shard_map/reduce_scatter | solution.py:203
  58.9 7.2 %collective-permute-start.3 = (f32[16,2048]{1,0:T(8,128)S(1)}, f32[16,2048]{1,0:T(8,128)S(1)}, u32[]{:S(2)}, u32[]{:S(2)}) collective-permute-start(f32[16,2048]{1,0:T(8,128)S(1)} %collective-permute-done.2), channel_id=1, source_target_pairs={{0,448},{64,0},{128,64},{192,128},{256,192},{320,256},{384,320},{4... | collective-permute-start | bytes 393224 | tf_op jit(solution)/shard_map/ppermute | solution.py:33
  63.5 8.0 %collective-permute-start.7 = (f32[16,2048]{1,0:T(8,128)S(1)}, f32[16,2048]{1,0:T(8,128)S(1)}, u32[]{:S(2)}, u32[]{:S(2)}) collective-permute-start(f32[16,2048]{1,0:T(8,128)S(1)} %collective-permute-done.6), channel_id=1, source_target_pairs={{0,64},{64,128},{128,192},{192,256},{256,320},{320,384},{384,448},... | collective-permute-start | bytes 393224 | tf_op jit(solution)/shard_map/ppermute | solution.py:36
  66.1 7.4 %collective-permute-start.4 = (f32[16,2048]{1,0:T(8,128)S(1)}, f32[16,2048]{1,0:T(8,128)S(1)}, u32[]{:S(2)}, u32[]{:S(2)}) collective-permute-start(f32[16,2048]{1,0:T(8,128)S(1)} %collective-permute-done.3), channel_id=1, source_target_pairs={{0,448},{64,0},{128,64},{192,128},{256,192},{320,256},{384,320},{4... | collective-permute-start | bytes 393224 | tf_op jit(solution)/shard_map/ppermute | solution.py:33
  71.5 9.1 %collective-permute-start.8 = (f32[16,2048]{1,0:T(8,128)S(1)}, f32[16,2048]{1,0:T(8,128)S(1)}, u32[]{:S(2)}, u32[]{:S(2)}) collective-permute-start(f32[16,2048]{1,0:T(8,128)S(1)} %collective-permute-done.7), channel_id=1, source_target_pairs={{0,64},{64,128},{128,192},{192,256},{256,320},{320,384},{384,448},... | collective-permute-start | bytes 393224 | tf_op jit(solution)/shard_map/ppermute | solution.py:36
  73.5 7.2 %collective-permute-start.5 = (f32[16,2048]{1,0:T(8,128)S(1)}, f32[16,2048]{1,0:T(8,128)S(1)}, u32[]{:S(2)}, u32[]{:S(2)}) collective-permute-start(f32[16,2048]{1,0:T(8,128)S(1)} %collective-permute-done.4), channel_id=1, source_target_pairs={{0,448},{64,0},{128,64},{192,128},{256,192},{320,256},{384,320},{4... | collective-permute-start | bytes 393224 | tf_op jit(solution)/shard_map/ppermute | solution.py:33
  80.7 1.0 copy-start.1
  80.7 1.0 copy-start.6
  80.8 1.3 copy-start.2
  95.7 41.0 %all-to-all-start.3 = ((f32[32,16,512]{2,1,0:T(8,128)}), f32[32,16,512]{2,1,0:T(8,128)S(1)}, u32[]{:S(2)}, u32[]{:S(2)}) async-start(f32[32,16,512]{2,1,0:T(8,128)} %bitcast.15), calls=%async_computation.3 | async-start | bytes 2097152 | tf_op jit(solution)/shard_map/all_to_all | solution.py:208
Sparse Core Ops, SparseCore 0:
  19.6 53.6 all-gather.2
  93.3 36.9 reduce-scatter.1

commit v10 on v9

--- a/solution.py
+++ b/solution.py
@@ -26,22 +26,18 @@
     return lax.all_to_all(copies, axis, 0, 0, tiled=True)
 
 
-def around(value, axis):
+def shifts(value, axis):
     count = lax.axis_size(axis)
-    found = [value] * count
-    for step in range(1, count // 2 + 1):
-        found[step] = lax.ppermute(found[step - 1], axis, [(i, (i - 1) % count) for i in range(count)])
-        if 2 * step < count:
-            back = found[(1 - step) % count]
-            found[-step] = lax.ppermute(back, axis, [(i, (i + 1) % count) for i in range(count)])
-    return jnp.stack(found)
+    sent = [lax.ppermute(value, axis, [(i, (i + step) % count) for i in range(count)]) for step in range(1, count)]
+    return [value, *sent]
 
 
 def first_kernel(
-    own_screen, other_screen, coef_hbm, rest_hbm, own_hbm, other_hbm, passed_hbm, out_hbm, passed_out_hbm,
-    coef, rest, own, other, total, sums, coef_sem, own_sem, other_sem, out_sem,
+    own_x, own_screen, other_screen, coef_hbm, rest_0, rest_1, rest_2, rest_3, own_hbm, other_hbm, passed_hbm,
+    out_hbm, passed_out_hbm, coef, rest, own, other, total, sums, coef_sem, rest_sem, own_sem, other_sem, out_sem,
 ):
     del passed_hbm, passed_out_hbm
+    rests = rest_0, rest_1, rest_2, rest_3
     aux, full_depth, width = own.shape
     most = coef.shape[1]
     starts = [*range(0, most, CHUNK), most]
@@ -50,11 +46,11 @@
     def copies(step):
         rows = pl.ds(starts[step], ends[step] - starts[step])
         if starts[step] < most:
-            columns = pltpu.make_async_copy(coef_hbm.at[:, rows], coef.at[:, rows], coef_sem.at[step])
+            columns = [pltpu.make_async_copy(coef_hbm.at[:, rows], coef.at[:, rows], coef_sem.at[step])]
         else:
-            columns = pltpu.make_async_copy(rest_hbm, rest, coef_sem.at[step])
+            columns = [pltpu.make_async_copy(rests[x], rest.at[x], rest_sem.at[x]) for x in range(NX)]
         return (
-            columns,
+            *columns,
             pltpu.make_async_copy(own_hbm.at[:, rows, :], own.at[:, rows, :], own_sem.at[step]),
             pltpu.make_async_copy(other_hbm.at[:, rows, :], other.at[:, rows, :], other_sem.at[step]),
         )
@@ -78,7 +74,7 @@
     for step, (first_row, end_row) in enumerate(zip(starts, ends, strict=True)):
         for copy in copies(step):
             copy.wait()
-        coef_high, coef_low = split(coef[:, first_row:end_row] if first_row < most else rest[...])
+        coef_high, coef_low = split(coef[:, first_row:end_row] if first_row < most else rest[...].reshape(-1, rest.shape[3]))
         for p in range(aux):
             for place, (integrals, screen) in enumerate(((own, own_screen), (other, other_screen))):
                 high, low = split(screened(integrals, screen, p, first_row, end_row))
@@ -93,14 +89,17 @@
                 else:
                     for z in range(NZ):
                         for x in range(NX):
-                            start, end = (z * NX + x) * 16, (x * NZ + z) * 16
-                            sums[end : end + 16, columns] = total[start : start + 16, columns] + part[end : end + 16]
+                            row = (x * NZ + z) * 16
+                            true_x = lax.rem(own_x[0] + NX - x, NX)
+                            start = pl.ds(pl.multiple_of((z * NX + true_x) * 16, 16), 16)
+                            end = pl.ds(pl.multiple_of((true_x * NZ + z) * 16, 16), 16)
+                            sums[end, columns] = total[start, columns] + part[row : row + 16]
     copy = pltpu.make_async_copy(sums, out_hbm, out_sem)
     copy.start()
     copy.wait()
 
 
-def first(own_screen, other_screen, coef, rest, own, other, passed):
+def first(own_x, own_screen, other_screen, coef, rests, own, other, passed):
     occ, most = coef.shape
     aux, full_depth, half_width = own.shape
     steps = -(-most // CHUNK) + 1
@@ -113,17 +112,18 @@
             jax.ShapeDtypeStruct((occ, width), F32),
             jax.ShapeDtypeStruct(passed.shape, passed.dtype),
         ),
-        in_specs=[scalars, scalars] + [away] * 5,
+        in_specs=[scalars] * 3 + [away] * (4 + NX),
         out_specs=(away, away),
-        input_output_aliases={6: 1},
+        input_output_aliases={6 + NX: 1},
         scratch_shapes=[
             pltpu.VMEM(coef.shape, F32),
-            pltpu.VMEM(rest.shape, F32),
+            pltpu.VMEM((NX, *rests[0].shape), F32),
             pltpu.VMEM(own.shape, F32),
             pltpu.VMEM(other.shape, F32),
             pltpu.VMEM((occ, width), F32),
             pltpu.VMEM((occ, width), F32),
             sems,
+            pltpu.SemaphoreType.DMA((NX,)),
             sems,
             sems,
             pltpu.SemaphoreType.DMA,
@@ -132,7 +132,7 @@
         cost_estimate=pl.CostEstimate(
             flops=6 * occ * full_depth * width, bytes_accessed=14 * 2**20, transcendentals=0
         ),
-    )(own_screen, other_screen, coef, rest, own, other, passed)
+    )(own_x, own_screen, other_screen, coef, *rests, own, other, passed)
 
 
 def second_kernel(rows_ref, halves_ref, out_ref):
@@ -195,21 +195,20 @@
     gathered = lax.all_gather(along_x.reshape(NX * occ, most), "z", axis=0, tiled=True)
 
     along_z = gather(coef[:, most:] + 0.0 * along_x[0, :, :REST], "z")
-    rest = gather(along_z, "x").reshape(NX * NZ * occ, REST)
-
-    along_y = around(coef + 0.0 * jnp.pad(along_z[0], ((0, 0), (0, most))), "y")
-
-    half, along_y = first(screen, swap(screen), gathered, rest, integrals, swap(integrals), along_y)
+    rests = shifts(along_z, "x")
+
+    along_y = gather(coef + 0.0 * jnp.pad(along_z[0], ((0, 0), (0, most))), "y")
+
+    own_x = lax.axis_index("x")[None]
+    half, along_y = first(own_x, screen, swap(screen), gathered, rests, integrals, swap(integrals), along_y)
     half = lax.psum_scatter(half, "y", scatter_dimension=0, tiled=True)
 
     chip_len = 2 * col_len
-    along_y = lax.dynamic_slice_in_dim(jnp.concatenate([along_y, along_y]), lax.rem(8 - row, 8), 8, 0)
     along_y = along_y.reshape(8, occ, row_len // chip_len, chip_len).transpose(0, 2, 1, 3)
     rows = lax.all_to_all(along_y.reshape(NX * NZ, occ, chip_len), ("x", "z"), 0, 0, tiled=True)
     pairs = second(rows.reshape(NX * NZ * occ, chip_len), lax.all_gather(half, "core"))
-    pairs = pairs.reshape(NX, NZ, occ, pairs.shape[1])
-    pairs = lax.all_to_all(pairs, "x", 0, 0, tiled=True).sum(axis=0)
-    pairs = lax.all_to_all(pairs, "z", 0, 0, tiled=True)
+    pairs = pairs.reshape(NX * NZ, occ, pairs.shape[1])
+    pairs = lax.all_to_all(pairs, ("x", "z"), 0, 0, tiled=True)
     return last(pairs).transpose(0, 2, 1)
 
 

time: 175 us -> 170 us (0.971)
  starting transfers between devices: 54.7 us -> 29.9 us
  blocking collectives: 44.9 us -> 60.6 us
  waiting for transfers between devices: 38.1 us -> 41.1 us
    all_to_all x1 -> x2, blocking collectives: 11 us -> 30 us  [gather(): return lax.all_to_all(copies, axis, 0, 0, tiled=True)]
    ppermute x7 -> x3, starting transfers between devices: 26.1 us -> 7.2 us  [shifts(): lax.ppermute(value, axis, [(i, (i + step) % count) for i in range(count)])]
    all_to_all x2 -> x1, starting transfers between devices: 14.5 us -> 6.96 us  [gather(): return lax.all_to_all(copies, axis, 0, 0, tiled=True)]
    reduce_scatter x1, waiting for transfers between devices: 30.3 us -> 22.8 us  [shards(): half = lax.psum_scatter(half, 'y', scatter_dimension=0, tiled=True)]
    all_to_all x2 -> x1, waiting for transfers between devices: 5.27 us -> 10.4 us  [gather(): return lax.all_to_all(copies, axis, 0, 0, tiled=True)]
    ppermute x7 -> x3, waiting for transfers between devices: 2.54 us -> 7.09 us  [shifts(): lax.ppermute(value, axis, [(i, (i + step) % count) for i in range(count)])]
    all_to_all x2 -> x1, blocking collectives: 27.4 us -> 23.8 us  [shards(): pairs = lax.all_to_all(pairs, ('x', 'z'), 0, 0, tiled=True)]
    ppermute x2, starting transfers between devices: 9.79 us -> 11.7 us  [swap(): return lax.ppermute(value, 'core', [(0, 1), (1, 0)])]
  transfers between devices with their start and end apart: 14 -> 9, of which waited for: 4 -> 5; matrix products, arithmetic and copies ran while one was open for 3% -> 3% of each run, Pallas kernels for 0% -> 0%
where the time goes in v10:
time: 170 us; the launch traced here: 167 us
  blocking collectives  60.6 us (36%)
  waiting for transfers between devices  41.1 us (24%)
  starting transfers between devices  29.9 us (18%)
  Pallas kernels  13.6 us (8%)
  between operations  13.6 us (8%)
  local copies, waits for them, and re-layouts  4.29 us (3%)
  other arithmetic  3.97 us (2%)
    all_to_all x2, blocking collectives, gather(): return lax.all_to_all(copies, axis, 0, 0, tiled=True)  30 us
    all_to_all x1, blocking collectives, shards(): pairs = lax.all_to_all(pairs, ('x', 'z'), 0, 0, tiled=True)  23.8 us
    reduce_scatter x1, waiting for transfers between devices, shards(): half = lax.psum_scatter(half, 'y', scatter_dimension=0, tiled=True)  22.8 us
    ppermute x2, starting transfers between devices, swap(): return lax.ppermute(value, 'core', [(0, 1), (1, 0)])  11.7 us
    pallas_call x1, Pallas kernels, first(): pl.pallas_call(first_kernel, out_shape=(jax.ShapeDtypeStruct((occ, width)...  11.3 us
    all_to_all x1, waiting for transfers between devices, gather(): return lax.all_to_all(copies, axis, 0, 0, tiled=True)  10.4 us
    ppermute x3, starting transfers between devices, shifts(): lax.ppermute(value, axis, [(i, (i + step) % count) for i in range(count)])  7.2 us
    ppermute x3, waiting for transfers between devices, shifts(): lax.ppermute(value, axis, [(i, (i + step) % count) for i in range(count)])  7.09 us
  transfers between devices with their start and end apart: 9, of which 5 were waited for; matrix products, arithmetic and copies ran while one was open for 3% of the time, Pallas kernels for 0%

profile of v10, /device:TPU:1, one launch (start us, length us, event | category | flops | bytes accessed | tf_op | source)
XLA Modules:
  0.0 167.0 jit_solution(1103680398078997823)
XLA Ops:
  6.5 0.0 copy-start
  6.5 0.0 copy-start.4
  6.5 0.0 all-gather.3.cloned.1.call-start
  6.6 0.7 copy-done
  7.2 0.2 compare_reduce_fusion
  7.4 0.1 broadcast_bitcast_fusion
  7.5 0.9 multiply_bitcast_fusion
  8.5 11.0 %all_to_all.25 = f32[4,16,1536]{2,1,0:T(8,128)} all-to-all(f32[4,16,1536]{2,1,0:T(8,128)S(1)} %broadcast_in_dim.12), channel_id=1, replica_groups=mesh['y'=8,'x'=4,'z'=8,'core'=2] {'x'}, dimensions={0} | all-to-all | bytes 786432 | tf_op jit(solution)/shard_map/all_to_all | solution.py:26
  19.5 0.0 all-gather.3.cloned.1.call-update
  19.5 8.3 %collective-permute-start.4 = (f32[2,2048,256]{2,1,0:T(8,128)}, f32[2,2048,256]{2,1,0:T(8,128)}, u32[]{:S(2)}, u32[]{:S(2)}) collective-permute-start(f32[2,2048,256]{2,1,0:T(8,128)} %own_hbm.1), channel_id=1, source_target_pairs={{0,1},{1,0},{2,3},{3,2},{4,5},{5,4},{6,7},{7,6},{8,9},{9,8},{10,11... | collective-permute-start | bytes 12582920 | tf_op jit(solution)/shard_map/ppermute | solution.py:21
  27.8 0.8 fusion.1
  28.5 19.0 %all_to_all.26.rest_0 = f32[8,16,512]{2,1,0:T(8,128)S(1)} all-to-all(f32[8,16,512]{2,1,0:T(8,128)S(1)} %broadcast_in_dim.13), channel_id=1, replica_groups=mesh['y'=8,'x'=4,'z'=8,'core'=2] {'z'}, dimensions={0} | all-to-all | bytes 524288 | tf_op jit(solution)/shard_map/all_to_all | solution.py:26
  47.6 0.0 copy-start.2
  47.6 1.0 multiply_add_fusion
  48.6 1.1 broadcast_in_dim.14
  49.8 7.0 %all-to-all-start.2 = ((f32[8,16,2048]{2,1,0:T(8,128)}), f32[8,16,2048]{2,1,0:T(8,128)S(1)}, u32[]{:S(2)}, u32[]{:S(2)}) async-start(f32[8,16,2048]{2,1,0:T(8,128)} %broadcast_in_dim.14), calls=%async_computation.2 | async-start | bytes 2097152 | tf_op jit(solution)/shard_map/all_to_all | solution.py:26
  56.7 0.0 reduce-scatter.2.cloned.1.call-start
  56.8 1.9 %collective-permute-start.3 = (f32[8,16,512]{2,1,0:T(8,128)S(1)}, f32[8,16,512]{2,1,0:T(8,128)S(1)}, u32[]{:S(2)}, u32[]{:S(2)}) collective-permute-start(f32[8,16,512]{2,1,0:T(8,128)S(1)} %all_to_all.26.rest_0), channel_id=1, source_target_pairs={{0,48},{16,0},{32,16},{48,32},{1,49},{17,1},{33,17},{49,33},{2,50}... | collective-permute-start | bytes 786440 | tf_op jit(solution)/shard_map/ppermute | solution.py:31
  58.7 3.3 %collective-permute-start.2 = (f32[8,16,512]{2,1,0:T(8,128)S(1)}, f32[8,16,512]{2,1,0:T(8,128)S(1)}, u32[]{:S(2)}, u32[]{:S(2)}) collective-permute-start(f32[8,16,512]{2,1,0:T(8,128)S(1)} %all_to_all.26.rest_0), channel_id=1, source_target_pairs={{0,32},{16,48},{32,0},{48,16},{1,33},{17,49},{33,1},{49,17},{2,34}... | collective-permute-start | bytes 786440 | tf_op jit(solution)/shard_map/ppermute | solution.py:31
  62.0 1.9 %collective-permute-start.1 = (f32[8,16,512]{2,1,0:T(8,128)S(1)}, f32[8,16,512]{2,1,0:T(8,128)S(1)}, u32[]{:S(2)}, u32[]{:S(2)}) collective-permute-start(f32[8,16,512]{2,1,0:T(8,128)S(1)} %all_to_all.26.rest_0), channel_id=1, source_target_pairs={{0,16},{16,32},{32,48},{48,0},{1,17},{17,33},{33,49},{49,1},{2,18}... | collective-permute-start | bytes 786440 | tf_op jit(solution)/shard_map/ppermute | solution.py:31
  64.0 0.0 copy-done.4
  64.0 0.1 copy.9.own_screen
  64.1 0.0 copy-start.3
  64.1 3.5 %collective-permute-start = (s32[16,2]{1,0:T(8,128)S(1)}, s32[16,2]{1,0:T(8,128)S(1)}, u32[]{:S(2)}, u32[]{:S(2)}) collective-permute-start(s32[16,2]{1,0:T(8,128)S(1)} %copy.9.own_screen), channel_id=1, source_target_pairs={{0,1},{1,0},{2,3},{3,2},{4,5},{5,4},{6,7},{7,6},{8,9},{9,8},{10,11... | collective-permute-start | bytes 392 | tf_op jit(solution)/shard_map/ppermute | solution.py:21
  67.6 0.8 collective-permute-done.other_screen
  68.4 0.0 copy-start.8
  68.4 0.0 collective-permute-done.3.rest_3
  68.4 0.0 copy-start.5
  68.4 0.2 collective-permute-done.2.rest_2
  68.6 0.0 copy-start.6
  68.6 6.9 %collective-permute-done.1.rest_1 = f32[8,16,512]{2,1,0:T(8,128)S(1)} collective-permute-done((f32[8,16,512]{2,1,0:T(8,128)S(1)}, f32[8,16,512]{2,1,0:T(8,128)S(1)}, u32[]{:S(2)}, u32[]{:S(2)}) %collective-permute-start.1) | collective-permute-done | bytes 262176 | tf_op jit(solution)/shard_map/ppermute | solution.py:31
  75.5 0.0 copy-start.7
  75.5 10.4 %all-to-all-done.2.passed_hbm = f32[8,16,2048]{2,1,0:T(8,128)S(1)} async-done(((f32[8,16,2048]{2,1,0:T(8,128)}), f32[8,16,2048]{2,1,0:T(8,128)S(1)}, u32[]{:S(2)}, u32[]{:S(2)}) %all-to-all-start.2) | async-done | bytes 1048608 | tf_op jit(solution)/shard_map/all_to_all | solution.py:26
  85.9 0.0 copy-start.1
  85.9 0.0 collective-permute-done.4.other_hbm
  85.9 0.0 all-gather.3.cloned.1.call-done.coef_hbm
  85.9 0.0 copy-done.2
  85.9 0.0 copy-done.3
  85.9 0.0 copy-done.8
  86.0 0.0 copy-done.5
  86.0 0.0 copy-done.6
  86.0 0.0 copy-done.7
  86.0 0.9 copy-done.1
  86.9 11.3 %shard_map.46 = (f32[512,1024]{1,0:T(8,128)}, f32[8,16,2048]{2,1,0:T(8,128)}) custom-call(s32[1]{0:T(128)} %bitcast.own_x, s32[16,2]{1,0:T(8,128)} %copy-done.3, s32[16,2]{1,0:T(8,128)} %copy-done.8, f32[512,1536]{1,0:T(8,128)} %all-gather.3.cloned.1.call-done.coef_hbm, f32[8,16,512]{2,1,0:T(8,128)} %copy-done.2, ...), custom_call_target="tpu_custom_call", output_to_operand_aliasing={{1}: (10, {})} | custom-call | flops 6442450944 | bytes 14680064 | tf_op jit(solution)/shard_map/pallas_call | solution.py:109
  98.2 0.0 reduce-scatter.2.cloned.1.call-update
  98.2 1.3 fusion.2
  99.5 1.1 pad_maximum_fusion
  100.6 3.9 %all-to-all-start.3 = ((f32[32,16,512]{2,1,0:T(8,128)}), f32[32,16,512]{2,1,0:T(8,128)S(1)}, u32[]{:S(2)}, u32[]{:S(2)}) async-start(f32[32,16,512]{2,1,0:T(8,128)} %bitcast.7), calls=%async_computation.3 | async-start | bytes 2097152 | tf_op jit(solution)/shard_map/all_to_all | solution.py:208
  104.5 22.8 %reduce-scatter.2.cloned.1.call-done = f32[64,1024]{1,0:T(8,128)} async-done(((f32[512,1024]{1,0:T(8,128)}), f32[64,1024]{1,0:T(8,128)}) %reduce-scatter.2.cloned.1.call-update) | async-done | bytes 262160 | tf_op jit(solution)/shard_map/reduce_scatter | solution.py:204
  127.3 6.7 %all-gather = f32[128,1024]{1,0:T(8,128)S(1)} all-gather(f32[64,1024]{1,0:T(8,128)} %reduce-scatter.2.cloned.1.call-done), channel_id=2, replica_groups=mesh['y'=8,'x'=4,'z'=8,'core'=2] {'core'}, dimensions={0}, use_global_device_ids=true | all-gather | bytes 786432 | tf_op jit(solution)/shard_map/all_gather | solution.py:209
  134.0 0.0 all-to-all-done.3
  134.0 0.6 shard_map.47
  134.6 23.8 %all_to_all.27.parts_ref = f32[32,16,256]{2,1,0:T(8,128)} all-to-all(f32[32,16,256]{2,1,0:T(8,128)S(1)} %bitcast.23), channel_id=1, replica_groups=mesh['y'=8,'x'=4,'z'=8,'core'=2] {'x','z'}, dimensions={0} | all-to-all | bytes 1048576 | tf_op jit(solution)/shard_map/all_to_all | solution.py:211
  158.5 1.7 %shard_map.48 = f32[2,16,128]{2,1,0:T(8,128)} custom-call(f32[32,16,256]{2,1,0:T(8,128)} %all_to_all.27.parts_ref), custom_call_target="tpu_custom_call" | custom-call | tf_op jit(solution)/shard_map/pallas_call | solution.py:175
  (7 shorter events, 0.1 us)
Async XLA Ops:
  6.5 0.7 copy-start
  6.5 57.5 %copy-start.4 = (s32[16,2]{0,1:T(2,128)S(1)}, s32[16,2]{0,1:T(2,128)}, u32[]{:S(2)}) copy-start(s32[16,2]{0,1:T(2,128)} %param.6) | copy-start | bytes 388
  6.5 79.4 %all-gather.3.cloned.1.call-start = ((), (), s32[]{:S(2)}) async-start(), calls=%async_computation.6 | async-start | bytes 3538944 | tf_op jit(solution)/shard_map/all_gather | solution.py:195
  19.5 66.4 %collective-permute-start.4 = (f32[2,2048,256]{2,1,0:T(8,128)}, f32[2,2048,256]{2,1,0:T(8,128)}, u32[]{:S(2)}, u32[]{:S(2)}) collective-permute-start(f32[2,2048,256]{2,1,0:T(8,128)} %own_hbm.1), channel_id=1, source_target_pairs={{0,1},{1,0},{2,3},{3,2},{4,5},{5,4},{6,7},{7,6},{8,9},{9,8},{10,11... | collective-permute-start | bytes 12582920 | tf_op jit(solution)/shard_map/ppermute | solution.py:21
  47.6 38.3 %copy-start.2 = (f32[8,16,512]{2,1,0:T(8,128)}, f32[8,16,512]{2,1,0:T(8,128)S(1)}, u32[]{:S(2)}) copy-start(f32[8,16,512]{2,1,0:T(8,128)S(1)} %all_to_all.26.rest_0) | copy-start | bytes 786436
  49.8 36.2 %all-to-all-start.2 = ((f32[8,16,2048]{2,1,0:T(8,128)}), f32[8,16,2048]{2,1,0:T(8,128)S(1)}, u32[]{:S(2)}, u32[]{:S(2)}) async-start(f32[8,16,2048]{2,1,0:T(8,128)} %broadcast_in_dim.14), calls=%async_computation.2 | async-start | bytes 2097152 | tf_op jit(solution)/shard_map/all_to_all | solution.py:26
  56.7 70.6 %reduce-scatter.2.cloned.1.call-start = ((), (), s32[]{:S(2)}) async-start(), calls=%async_computation.7 | async-start | bytes 2359296 | tf_op jit(solution)/shard_map/reduce_scatter | solution.py:204
  56.8 11.6 %collective-permute-start.3 = (f32[8,16,512]{2,1,0:T(8,128)S(1)}, f32[8,16,512]{2,1,0:T(8,128)S(1)}, u32[]{:S(2)}, u32[]{:S(2)}) collective-permute-start(f32[8,16,512]{2,1,0:T(8,128)S(1)} %all_to_all.26.rest_0), channel_id=1, source_target_pairs={{0,48},{16,0},{32,16},{48,32},{1,49},{17,1},{33,17},{49,33},{2,50}... | collective-permute-start | bytes 786440 | tf_op jit(solution)/shard_map/ppermute | solution.py:31
  58.7 9.9 %collective-permute-start.2 = (f32[8,16,512]{2,1,0:T(8,128)S(1)}, f32[8,16,512]{2,1,0:T(8,128)S(1)}, u32[]{:S(2)}, u32[]{:S(2)}) collective-permute-start(f32[8,16,512]{2,1,0:T(8,128)S(1)} %all_to_all.26.rest_0), channel_id=1, source_target_pairs={{0,32},{16,48},{32,0},{48,16},{1,33},{17,49},{33,1},{49,17},{2,34}... | collective-permute-start | bytes 786440 | tf_op jit(solution)/shard_map/ppermute | solution.py:31
  62.0 13.4 %collective-permute-start.1 = (f32[8,16,512]{2,1,0:T(8,128)S(1)}, f32[8,16,512]{2,1,0:T(8,128)S(1)}, u32[]{:S(2)}, u32[]{:S(2)}) collective-permute-start(f32[8,16,512]{2,1,0:T(8,128)S(1)} %all_to_all.26.rest_0), channel_id=1, source_target_pairs={{0,16},{16,32},{32,48},{48,0},{1,17},{17,33},{33,49},{49,1},{2,18}... | collective-permute-start | bytes 786440 | tf_op jit(solution)/shard_map/ppermute | solution.py:31
  64.1 21.8 %copy-start.3 = (s32[16,2]{1,0:T(8,128)}, s32[16,2]{1,0:T(8,128)S(1)}, u32[]{:S(2)}) copy-start(s32[16,2]{1,0:T(8,128)S(1)} %copy.9.own_screen) | copy-start | bytes 388
  64.1 4.3 %collective-permute-start = (s32[16,2]{1,0:T(8,128)S(1)}, s32[16,2]{1,0:T(8,128)S(1)}, u32[]{:S(2)}, u32[]{:S(2)}) collective-permute-start(s32[16,2]{1,0:T(8,128)S(1)} %copy.9.own_screen), channel_id=1, source_target_pairs={{0,1},{1,0},{2,3},{3,2},{4,5},{5,4},{6,7},{7,6},{8,9},{9,8},{10,11... | collective-permute-start | bytes 392 | tf_op jit(solution)/shard_map/ppermute | solution.py:21
  68.4 17.6 %copy-start.8 = (s32[16,2]{1,0:T(8,128)}, s32[16,2]{1,0:T(8,128)S(1)}, u32[]{:S(2)}) copy-start(s32[16,2]{1,0:T(8,128)S(1)} %collective-permute-done.other_screen) | copy-start | bytes 388
  68.4 17.6 %copy-start.5 = (f32[8,16,512]{2,1,0:T(8,128)}, f32[8,16,512]{2,1,0:T(8,128)S(1)}, u32[]{:S(2)}) copy-start(f32[8,16,512]{2,1,0:T(8,128)S(1)} %collective-permute-done.3.rest_3) | copy-start | bytes 786436
  68.6 17.4 %copy-start.6 = (f32[8,16,512]{2,1,0:T(8,128)}, f32[8,16,512]{2,1,0:T(8,128)S(1)}, u32[]{:S(2)}) copy-start(f32[8,16,512]{2,1,0:T(8,128)S(1)} %collective-permute-done.2.rest_2) | copy-start | bytes 786436
  75.5 10.5 %copy-start.7 = (f32[8,16,512]{2,1,0:T(8,128)}, f32[8,16,512]{2,1,0:T(8,128)S(1)}, u32[]{:S(2)}) copy-start(f32[8,16,512]{2,1,0:T(8,128)S(1)} %collective-permute-done.1.rest_1) | copy-start | bytes 786436
  85.9 1.0 copy-start.1
  100.6 33.4 %all-to-all-start.3 = ((f32[32,16,512]{2,1,0:T(8,128)}), f32[32,16,512]{2,1,0:T(8,128)S(1)}, u32[]{:S(2)}, u32[]{:S(2)}) async-start(f32[32,16,512]{2,1,0:T(8,128)} %bitcast.7), calls=%async_computation.3 | async-start | bytes 2097152 | tf_op jit(solution)/shard_map/all_to_all | solution.py:208
Sparse Core Ops, SparseCore 0:
  19.6 54.6 all-gather.2
  98.3 28.9 reduce-scatter.1

commit v11 on v10

--- a/solution.py
+++ b/solution.py
@@ -33,10 +33,9 @@
 
 
 def first_kernel(
-    own_x, own_screen, other_screen, coef_hbm, rest_0, rest_1, rest_2, rest_3, own_hbm, other_hbm, passed_hbm,
-    out_hbm, passed_out_hbm, coef, rest, own, other, total, sums, coef_sem, rest_sem, own_sem, other_sem, out_sem,
+    own_x, own_screen, other_screen, coef_hbm, rest_0, rest_1, rest_2, rest_3, own_hbm, other_hbm, out_hbm,
+    coef, rest, own, other, total, sums, coef_sem, rest_sem, own_sem, other_sem, out_sem,
 ):
-    del passed_hbm, passed_out_hbm
     rests = rest_0, rest_1, rest_2, rest_3
     aux, full_depth, width = own.shape
     most = coef.shape[1]
@@ -99,7 +98,7 @@
     copy.wait()
 
 
-def first(own_x, own_screen, other_screen, coef, rests, own, other, passed):
+def first(own_x, own_screen, other_screen, coef, rests, own, other):
     occ, most = coef.shape
     aux, full_depth, half_width = own.shape
     steps = -(-most // CHUNK) + 1
@@ -108,13 +107,9 @@
     sems = pltpu.SemaphoreType.DMA((steps,))
     return pl.pallas_call(
         first_kernel,
-        out_shape=(
-            jax.ShapeDtypeStruct((occ, width), F32),
-            jax.ShapeDtypeStruct(passed.shape, passed.dtype),
-        ),
-        in_specs=[scalars] * 3 + [away] * (4 + NX),
-        out_specs=(away, away),
-        input_output_aliases={6 + NX: 1},
+        out_shape=jax.ShapeDtypeStruct((occ, width), F32),
+        in_specs=[scalars] * 3 + [away] * (3 + NX),
+        out_specs=away,
         scratch_shapes=[
             pltpu.VMEM(coef.shape, F32),
             pltpu.VMEM((NX, *rests[0].shape), F32),
@@ -132,7 +127,7 @@
         cost_estimate=pl.CostEstimate(
             flops=6 * occ * full_depth * width, bytes_accessed=14 * 2**20, transcendentals=0
         ),
-    )(own_x, own_screen, other_screen, coef, *rests, own, other, passed)
+    )(own_x, own_screen, other_screen, coef, *rests, own, other)
 
 
 def second_kernel(rows_ref, halves_ref, out_ref):
@@ -200,12 +195,13 @@
     along_y = gather(coef + 0.0 * jnp.pad(along_z[0], ((0, 0), (0, most))), "y")
 
     own_x = lax.axis_index("x")[None]
-    half, along_y = first(own_x, screen, swap(screen), gathered, rests, integrals, swap(integrals), along_y)
-    half = lax.psum_scatter(half, "y", scatter_dimension=0, tiled=True)
+    products = first(own_x, screen, swap(screen), gathered, rests, integrals, swap(integrals))
+    half = lax.psum_scatter(products, "y", scatter_dimension=0, tiled=True)
 
     chip_len = 2 * col_len
     along_y = along_y.reshape(8, occ, row_len // chip_len, chip_len).transpose(0, 2, 1, 3)
-    rows = lax.all_to_all(along_y.reshape(NX * NZ, occ, chip_len), ("x", "z"), 0, 0, tiled=True)
+    along_y = along_y.reshape(NX * NZ, occ, chip_len) + 0.0 * products[None, :occ, :chip_len]
+    rows = lax.all_to_all(along_y, ("x", "z"), 0, 0, tiled=True)
     pairs = second(rows.reshape(NX * NZ * occ, chip_len), lax.all_gather(half, "core"))
     pairs = pairs.reshape(NX * NZ, occ, pairs.shape[1])
     pairs = lax.all_to_all(pairs, ("x", "z"), 0, 0, tiled=True)

time: 170 us -> 167 us (0.982)
  blocking collectives: 60.6 us -> 41.4 us
  waiting for transfers between devices: 41.1 us -> 52.2 us
  starting transfers between devices: 29.9 us -> 36.4 us
    all_to_all x2 -> x1, blocking collectives: 30 us -> 11 us  [gather(): return lax.all_to_all(copies, axis, 0, 0, tiled=True)]
    all_to_all x1 -> x2, waiting for transfers between devices: 10.4 us -> 19.1 us  [gather(): return lax.all_to_all(copies, axis, 0, 0, tiled=True)]
    all_gather x1, waiting for transfers between devices: 0.01 us -> 7.75 us  [shards(): lax.all_gather(along_x.reshape(NX * occ, most), 'z', axis=0, tiled=True)]
    all_to_all x1 -> x2, starting transfers between devices: 6.96 us -> 13.5 us  [gather(): return lax.all_to_all(copies, axis, 0, 0, tiled=True)]
    ppermute x3, waiting for transfers between devices: 7.09 us -> 1.71 us  [shifts(): lax.ppermute(value, axis, [(i, (i + step) % count) for i in range(count)])]
  transfers between devices with their start and end apart: 9 -> 10, of which waited for: 5 -> 5; matrix products, arithmetic and copies ran while one was open for 3% -> 3% of each run, Pallas kernels for 0% -> 7%
where the time goes in v11:
time: 167 us; the launch traced here: 164 us
  waiting for transfers between devices  52.2 us (31%)
  blocking collectives  41.4 us (25%)
  starting transfers between devices  36.4 us (22%)
  Pallas kernels  13.6 us (8%)
  between operations  13.6 us (8%)
  other arithmetic  3.83 us (2%)
  local copies, waits for them, and re-layouts  2.78 us (2%)
    all_to_all x1, blocking collectives, shards(): pairs = lax.all_to_all(pairs, ('x', 'z'), 0, 0, tiled=True)  23.9 us
    reduce_scatter x1, waiting for transfers between devices, shards(): half = lax.psum_scatter(products, 'y', scatter_dimension=0, tiled=True)  23.6 us
    all_to_all x2, waiting for transfers between devices, gather(): return lax.all_to_all(copies, axis, 0, 0, tiled=True)  19.1 us
    all_to_all x2, starting transfers between devices, gather(): return lax.all_to_all(copies, axis, 0, 0, tiled=True)  13.5 us
    pallas_call x1, Pallas kernels, first(): pl.pallas_call(first_kernel, out_shape=jax.ShapeDtypeStruct((occ, width),...  11.3 us
    all_to_all x1, blocking collectives, gather(): return lax.all_to_all(copies, axis, 0, 0, tiled=True)  11 us
    ppermute x2, starting transfers between devices, swap(): return lax.ppermute(value, 'core', [(0, 1), (1, 0)])  10.5 us
    ppermute x3, starting transfers between devices, shifts(): lax.ppermute(value, axis, [(i, (i + step) % count) for i in range(count)])  8.4 us
  transfers between devices with their start and end apart: 10, of which 5 were waited for; matrix products, arithmetic and copies ran while one was open for 3% of the time, Pallas kernels for 7%

profile of v11, /device:TPU:1, one launch (start us, length us, event | category | flops | bytes accessed | tf_op | source)
XLA Modules:
  0.0 163.9 jit_solution(17344890081042600873)
XLA Ops:
  6.5 0.0 copy-start
  6.5 0.0 copy-start.1
  6.5 0.0 copy-start.4
  6.5 0.0 all-gather.3.cloned.1.call-start
  6.6 0.6 copy-done
  7.2 0.2 compare_reduce_fusion
  7.4 0.1 broadcast_bitcast_fusion
  7.5 0.9 multiply_bitcast_fusion
  8.5 11.0 %all_to_all.25 = f32[4,16,1536]{2,1,0:T(8,128)} all-to-all(f32[4,16,1536]{2,1,0:T(8,128)S(1)} %broadcast_in_dim.11), channel_id=1, replica_groups=mesh['y'=8,'x'=4,'z'=8,'core'=2] {'x'}, dimensions={0} | all-to-all | bytes 786432 | tf_op jit(solution)/shard_map/all_to_all | solution.py:26
  19.5 0.0 all-gather.3.cloned.1.call-update
  19.5 8.3 %collective-permute-start.4 = (f32[2,2048,256]{2,1,0:T(8,128)}, f32[2,2048,256]{2,1,0:T(8,128)}, u32[]{:S(2)}, u32[]{:S(2)}) collective-permute-start(f32[2,2048,256]{2,1,0:T(8,128)} %own_hbm.1), channel_id=1, source_target_pairs={{0,1},{1,0},{2,3},{3,2},{4,5},{5,4},{6,7},{7,6},{8,9},{9,8},{10,11... | collective-permute-start | bytes 12582920 | tf_op jit(solution)/shard_map/ppermute | solution.py:21
  27.8 0.8 fusion.1
  28.5 0.7 broadcast_in_dim.12
  29.3 6.5 %all-to-all-start.1 = ((f32[8,16,512]{2,1,0:T(8,128)}), f32[8,16,512]{2,1,0:T(8,128)S(1)}, u32[]{:S(2)}, u32[]{:S(2)}) async-start(f32[8,16,512]{2,1,0:T(8,128)} %broadcast_in_dim.12), calls=%async_computation.1 | async-start | bytes 524288 | tf_op jit(solution)/shard_map/all_to_all | solution.py:26
  35.7 0.0 copy-done.4
  35.7 0.1 copy.8.own_screen
  35.8 0.0 copy-start.3
  35.8 2.2 %collective-permute-start = (s32[16,2]{1,0:T(8,128)S(1)}, s32[16,2]{1,0:T(8,128)S(1)}, u32[]{:S(2)}, u32[]{:S(2)}) collective-permute-start(s32[16,2]{1,0:T(8,128)S(1)} %copy.8.own_screen), channel_id=1, source_target_pairs={{0,1},{1,0},{2,3},{3,2},{4,5},{5,4},{6,7},{7,6},{8,9},{9,8},{10,11... | collective-permute-start | bytes 392 | tf_op jit(solution)/shard_map/ppermute | solution.py:21
  38.0 10.8 %all-to-all-done.1.rest_0 = f32[8,16,512]{2,1,0:T(8,128)S(1)} async-done(((f32[8,16,512]{2,1,0:T(8,128)}), f32[8,16,512]{2,1,0:T(8,128)S(1)}, u32[]{:S(2)}, u32[]{:S(2)}) %all-to-all-start.1) | async-done | bytes 262176 | tf_op jit(solution)/shard_map/all_to_all | solution.py:26
  48.8 0.0 copy-start.2
  48.8 1.9 %collective-permute-start.1 = (f32[8,16,512]{2,1,0:T(8,128)S(1)}, f32[8,16,512]{2,1,0:T(8,128)S(1)}, u32[]{:S(2)}, u32[]{:S(2)}) collective-permute-start(f32[8,16,512]{2,1,0:T(8,128)S(1)} %all-to-all-done.1.rest_0), channel_id=1, source_target_pairs={{0,16},{16,32},{32,48},{48,0},{1,17},{17,33},{33,49},{49,1},{2,18}... | collective-permute-start | bytes 786440 | tf_op jit(solution)/shard_map/ppermute | solution.py:31
  50.8 3.1 %collective-permute-start.2 = (f32[8,16,512]{2,1,0:T(8,128)S(1)}, f32[8,16,512]{2,1,0:T(8,128)S(1)}, u32[]{:S(2)}, u32[]{:S(2)}) collective-permute-start(f32[8,16,512]{2,1,0:T(8,128)S(1)} %all-to-all-done.1.rest_0), channel_id=1, source_target_pairs={{0,32},{16,48},{32,0},{48,16},{1,33},{17,49},{33,1},{49,17},{2,34}... | collective-permute-start | bytes 786440 | tf_op jit(solution)/shard_map/ppermute | solution.py:31
  53.8 3.4 %collective-permute-start.3 = (f32[8,16,512]{2,1,0:T(8,128)S(1)}, f32[8,16,512]{2,1,0:T(8,128)S(1)}, u32[]{:S(2)}, u32[]{:S(2)}) collective-permute-start(f32[8,16,512]{2,1,0:T(8,128)S(1)} %all-to-all-done.1.rest_0), channel_id=1, source_target_pairs={{0,48},{16,0},{32,16},{48,32},{1,49},{17,1},{33,17},{49,33},{2,50}... | collective-permute-start | bytes 786440 | tf_op jit(solution)/shard_map/ppermute | solution.py:31
  57.3 0.0 copy-done.1
  57.3 1.1 broadcast_in_dim.13
  58.4 7.0 %all-to-all-start.2 = ((f32[8,16,2048]{2,1,0:T(8,128)}), f32[8,16,2048]{2,1,0:T(8,128)S(1)}, u32[]{:S(2)}, u32[]{:S(2)}) async-start(f32[8,16,2048]{2,1,0:T(8,128)} %broadcast_in_dim.13), calls=%async_computation.2 | async-start | bytes 2097152 | tf_op jit(solution)/shard_map/all_to_all | solution.py:26
  65.5 0.0 reduce-scatter.2.cloned.1.call-start
  65.5 0.0 collective-permute-done.other_screen
  65.5 0.0 copy-start.8
  65.5 0.0 collective-permute-done.1.rest_1
  65.5 0.0 copy-start.5
  65.5 0.0 collective-permute-done.2.rest_2
  65.6 0.0 copy-start.6
  65.6 1.7 %collective-permute-done.3.rest_3 = f32[8,16,512]{2,1,0:T(8,128)S(1)} collective-permute-done((f32[8,16,512]{2,1,0:T(8,128)S(1)}, f32[8,16,512]{2,1,0:T(8,128)S(1)}, u32[]{:S(2)}, u32[]{:S(2)}) %collective-permute-start.3) | collective-permute-done | bytes 262176 | tf_op jit(solution)/shard_map/ppermute | solution.py:31
  67.3 0.0 copy-start.7
  67.3 0.0 collective-permute-done.4.other_hbm
  67.3 7.7 %all-gather.3.cloned.1.call-done.coef_hbm = f32[512,1536]{1,0:T(8,128)} async-done(((f32[64,1536]{1,0:T(8,128)}), f32[512,1536]{1,0:T(8,128)}) %all-gather.3.cloned.1.call-update) | async-done | bytes 3145744 | tf_op jit(solution)/shard_map/all_gather | solution.py:190
  75.0 0.0 copy-done.3
  75.0 0.0 copy-done.2
  75.0 0.0 copy-done.8
  75.0 0.0 copy-done.5
  75.0 0.0 copy-done.6
  75.0 0.0 copy-done.7
  75.0 11.3 %shard_map.46 = f32[512,1024]{1,0:T(8,128)} custom-call(s32[1]{0:T(128)} %bitcast.6.own_x, s32[16,2]{1,0:T(8,128)} %copy-done.3, s32[16,2]{1,0:T(8,128)} %copy-done.8, f32[512,1536]{1,0:T(8,128)} %all-gather.3.cloned.1.call-done.coef_hbm, f32[8,16,512]{2,1,0:T(8,128)} %copy-done.2, f32[8,16,512]{2,1,0:T(8,128)} %copy-done.5, f32[8,16,512]{2,1,0:T(8,128)} %copy-done.6, ...), custom_call_target="tpu_custom_call" | custom-call | flops 6442450944 | bytes 14680064 | tf_op jit(solution)/shard_map/pallas_call | solution.py:108
  86.3 0.0 reduce-scatter.2.cloned.1.call-update
  86.4 8.3 %all-to-all-done.2 = f32[8,16,2048]{2,1,0:T(8,128)S(1)} async-done(((f32[8,16,2048]{2,1,0:T(8,128)}), f32[8,16,2048]{2,1,0:T(8,128)S(1)}, u32[]{:S(2)}, u32[]{:S(2)}) %all-to-all-start.2) | async-done | bytes 1048608 | tf_op jit(solution)/shard_map/all_to_all | solution.py:26
  94.6 0.1 fusion.2
  94.7 0.1 pad_maximum_fusion
  94.8 0.8 slice_multiply_fusion
  95.6 1.1 broadcast_add_fusion
  96.7 4.0 %all-to-all-start.3 = ((f32[32,16,512]{2,1,0:T(8,128)}), f32[32,16,512]{2,1,0:T(8,128)S(1)}, u32[]{:S(2)}, u32[]{:S(2)}) async-start(f32[32,16,512]{2,1,0:T(8,128)} %broadcast_add_fusion), calls=%async_computation.3 | async-start | bytes 2097152 | tf_op jit(solution)/shard_map/all_to_all | solution.py:204
  100.7 23.6 %reduce-scatter.2.cloned.1.call-done = f32[64,1024]{1,0:T(8,128)} async-done(((f32[512,1024]{1,0:T(8,128)}), f32[64,1024]{1,0:T(8,128)}) %reduce-scatter.2.cloned.1.call-update) | async-done | bytes 262160 | tf_op jit(solution)/shard_map/reduce_scatter | solution.py:199
  124.3 6.5 %all-gather = f32[128,1024]{1,0:T(8,128)S(1)} all-gather(f32[64,1024]{1,0:T(8,128)} %reduce-scatter.2.cloned.1.call-done), channel_id=2, replica_groups=mesh['y'=8,'x'=4,'z'=8,'core'=2] {'core'}, dimensions={0}, use_global_device_ids=true | all-gather | bytes 786432 | tf_op jit(solution)/shard_map/all_gather | solution.py:205
  130.8 0.0 all-to-all-done.3
  130.8 0.6 shard_map.47
  131.5 23.9 %all_to_all.26.parts_ref = f32[32,16,256]{2,1,0:T(8,128)} all-to-all(f32[32,16,256]{2,1,0:T(8,128)S(1)} %bitcast.23), channel_id=1, replica_groups=mesh['y'=8,'x'=4,'z'=8,'core'=2] {'x','z'}, dimensions={0} | all-to-all | bytes 1048576 | tf_op jit(solution)/shard_map/all_to_all | solution.py:207
  155.3 1.7 %shard_map.48 = f32[2,16,128]{2,1,0:T(8,128)} custom-call(f32[32,16,256]{2,1,0:T(8,128)} %all_to_all.26.parts_ref), custom_call_target="tpu_custom_call" | custom-call | tf_op jit(solution)/shard_map/pallas_call | solution.py:170
  (7 shorter events, 0.1 us)
Async XLA Ops:
  6.5 0.7 copy-start
  6.5 50.8 %copy-start.1 = (f32[2048,16]{0,1:T(8,128)S(1)}, f32[2048,16]{0,1:T(8,128)}, u32[]{:S(2)}) copy-start(f32[2048,16]{0,1:T(8,128)} %param.5) | copy-start | bytes 393220
  6.5 29.2 %copy-start.4 = (s32[16,2]{0,1:T(2,128)S(1)}, s32[16,2]{0,1:T(2,128)}, u32[]{:S(2)}) copy-start(s32[16,2]{0,1:T(2,128)} %param.6) | copy-start | bytes 388
  6.5 68.5 %all-gather.3.cloned.1.call-start = ((), (), s32[]{:S(2)}) async-start(), calls=%async_computation.6 | async-start | bytes 3538944 | tf_op jit(solution)/shard_map/all_gather | solution.py:190
  19.5 47.8 %collective-permute-start.4 = (f32[2,2048,256]{2,1,0:T(8,128)}, f32[2,2048,256]{2,1,0:T(8,128)}, u32[]{:S(2)}, u32[]{:S(2)}) collective-permute-start(f32[2,2048,256]{2,1,0:T(8,128)} %own_hbm.1), channel_id=1, source_target_pairs={{0,1},{1,0},{2,3},{3,2},{4,5},{5,4},{6,7},{7,6},{8,9},{9,8},{10,11... | collective-permute-start | bytes 12582920 | tf_op jit(solution)/shard_map/ppermute | solution.py:21
  29.3 19.6 %all-to-all-start.1 = ((f32[8,16,512]{2,1,0:T(8,128)}), f32[8,16,512]{2,1,0:T(8,128)S(1)}, u32[]{:S(2)}, u32[]{:S(2)}) async-start(f32[8,16,512]{2,1,0:T(8,128)} %broadcast_in_dim.12), calls=%async_computation.1 | async-start | bytes 524288 | tf_op jit(solution)/shard_map/all_to_all | solution.py:26
  35.8 39.2 %copy-start.3 = (s32[16,2]{1,0:T(8,128)}, s32[16,2]{1,0:T(8,128)S(1)}, u32[]{:S(2)}) copy-start(s32[16,2]{1,0:T(8,128)S(1)} %copy.8.own_screen) | copy-start | bytes 388
  35.8 29.7 %collective-permute-start = (s32[16,2]{1,0:T(8,128)S(1)}, s32[16,2]{1,0:T(8,128)S(1)}, u32[]{:S(2)}, u32[]{:S(2)}) collective-permute-start(s32[16,2]{1,0:T(8,128)S(1)} %copy.8.own_screen), channel_id=1, source_target_pairs={{0,1},{1,0},{2,3},{3,2},{4,5},{5,4},{6,7},{7,6},{8,9},{9,8},{10,11... | collective-permute-start | bytes 392 | tf_op jit(solution)/shard_map/ppermute | solution.py:21
  48.8 26.2 %copy-start.2 = (f32[8,16,512]{2,1,0:T(8,128)}, f32[8,16,512]{2,1,0:T(8,128)S(1)}, u32[]{:S(2)}) copy-start(f32[8,16,512]{2,1,0:T(8,128)S(1)} %all-to-all-done.1.rest_0) | copy-start | bytes 786436
  48.8 16.7 %collective-permute-start.1 = (f32[8,16,512]{2,1,0:T(8,128)S(1)}, f32[8,16,512]{2,1,0:T(8,128)S(1)}, u32[]{:S(2)}, u32[]{:S(2)}) collective-permute-start(f32[8,16,512]{2,1,0:T(8,128)S(1)} %all-to-all-done.1.rest_0), channel_id=1, source_target_pairs={{0,16},{16,32},{32,48},{48,0},{1,17},{17,33},{33,49},{49,1},{2,18}... | collective-permute-start | bytes 786440 | tf_op jit(solution)/shard_map/ppermute | solution.py:31
  50.8 14.8 %collective-permute-start.2 = (f32[8,16,512]{2,1,0:T(8,128)S(1)}, f32[8,16,512]{2,1,0:T(8,128)S(1)}, u32[]{:S(2)}, u32[]{:S(2)}) collective-permute-start(f32[8,16,512]{2,1,0:T(8,128)S(1)} %all-to-all-done.1.rest_0), channel_id=1, source_target_pairs={{0,32},{16,48},{32,0},{48,16},{1,33},{17,49},{33,1},{49,17},{2,34}... | collective-permute-start | bytes 786440 | tf_op jit(solution)/shard_map/ppermute | solution.py:31
  53.8 13.4 %collective-permute-start.3 = (f32[8,16,512]{2,1,0:T(8,128)S(1)}, f32[8,16,512]{2,1,0:T(8,128)S(1)}, u32[]{:S(2)}, u32[]{:S(2)}) collective-permute-start(f32[8,16,512]{2,1,0:T(8,128)S(1)} %all-to-all-done.1.rest_0), channel_id=1, source_target_pairs={{0,48},{16,0},{32,16},{48,32},{1,49},{17,1},{33,17},{49,33},{2,50}... | collective-permute-start | bytes 786440 | tf_op jit(solution)/shard_map/ppermute | solution.py:31
  58.4 36.2 %all-to-all-start.2 = ((f32[8,16,2048]{2,1,0:T(8,128)}), f32[8,16,2048]{2,1,0:T(8,128)S(1)}, u32[]{:S(2)}, u32[]{:S(2)}) async-start(f32[8,16,2048]{2,1,0:T(8,128)} %broadcast_in_dim.13), calls=%async_computation.2 | async-start | bytes 2097152 | tf_op jit(solution)/shard_map/all_to_all | solution.py:26
  65.5 58.8 %reduce-scatter.2.cloned.1.call-start = ((), (), s32[]{:S(2)}) async-start(), calls=%async_computation.7 | async-start | bytes 2359296 | tf_op jit(solution)/shard_map/reduce_scatter | solution.py:199
  65.5 9.5 %copy-start.8 = (s32[16,2]{1,0:T(8,128)}, s32[16,2]{1,0:T(8,128)S(1)}, u32[]{:S(2)}) copy-start(s32[16,2]{1,0:T(8,128)S(1)} %collective-permute-done.other_screen) | copy-start | bytes 388
  65.5 9.5 %copy-start.5 = (f32[8,16,512]{2,1,0:T(8,128)}, f32[8,16,512]{2,1,0:T(8,128)S(1)}, u32[]{:S(2)}) copy-start(f32[8,16,512]{2,1,0:T(8,128)S(1)} %collective-permute-done.1.rest_1) | copy-start | bytes 786436
  65.6 9.5 %copy-start.6 = (f32[8,16,512]{2,1,0:T(8,128)}, f32[8,16,512]{2,1,0:T(8,128)S(1)}, u32[]{:S(2)}) copy-start(f32[8,16,512]{2,1,0:T(8,128)S(1)} %collective-permute-done.2.rest_2) | copy-start | bytes 786436
  67.3 7.8 %copy-start.7 = (f32[8,16,512]{2,1,0:T(8,128)}, f32[8,16,512]{2,1,0:T(8,128)S(1)}, u32[]{:S(2)}) copy-start(f32[8,16,512]{2,1,0:T(8,128)S(1)} %collective-permute-done.3.rest_3) | copy-start | bytes 786436
  96.7 34.2 %all-to-all-start.3 = ((f32[32,16,512]{2,1,0:T(8,128)}), f32[32,16,512]{2,1,0:T(8,128)S(1)}, u32[]{:S(2)}, u32[]{:S(2)}) async-start(f32[32,16,512]{2,1,0:T(8,128)} %broadcast_add_fusion), calls=%async_computation.3 | async-start | bytes 2097152 | tf_op jit(solution)/shard_map/all_to_all | solution.py:204
Sparse Core Ops, SparseCore 0:
  19.6 55.3 all-gather.2
  86.5 37.7 reduce-scatter.1

commit v12 on v11

--- a/solution.py
+++ b/solution.py
@@ -124,9 +124,7 @@
             pltpu.SemaphoreType.DMA,
         ],
         compiler_params=pltpu.CompilerParams(vmem_limit_bytes=56 * 2**20),
-        cost_estimate=pl.CostEstimate(
-            flops=6 * occ * full_depth * width, bytes_accessed=14 * 2**20, transcendentals=0
-        ),
+        cost_estimate=pl.CostEstimate(flops=0, bytes_accessed=0, transcendentals=0),
     )(own_x, own_screen, other_screen, coef, *rests, own, other)
 
 

time: 167 us -> 166 us (level)
  blocking collectives: 41.4 us -> 60.5 us
  waiting for transfers between devices: 52.2 us -> 36.7 us
  starting transfers between devices: 36.4 us -> 32.2 us
    all_to_all x2 -> x1, waiting for transfers between devices: 19.1 us -> 0.01 us  [gather(): return lax.all_to_all(copies, axis, 0, 0, tiled=True)]
    all_to_all x1 -> x2, blocking collectives: 11 us -> 30 us  [gather(): return lax.all_to_all(copies, axis, 0, 0, tiled=True)]
    all_gather x1, waiting for transfers between devices: 7.75 us -> 0.11 us  [shards(): lax.all_gather(along_x.reshape(NX * occ, most), 'z', axis=0, tiled=True)]
    reduce_scatter x1, waiting for transfers between devices: 23.6 us -> 30.2 us  [shards(): half = lax.psum_scatter(products, 'y', scatter_dimension=0, tiled=True)]
    all_to_all x2 -> x1, starting transfers between devices: 13.5 us -> 6.96 us  [gather(): return lax.all_to_all(copies, axis, 0, 0, tiled=True)]
    ppermute x3, waiting for transfers between devices: 1.71 us -> 5.6 us  [shifts(): lax.ppermute(value, axis, [(i, (i + step) % count) for i in range(count)])]
  transfers between devices with their start and end apart: 10 -> 9, of which waited for: 5 -> 5; matrix products, arithmetic and copies ran while one was open for 3% -> 2% of each run, Pallas kernels for 7% -> 7%
where the time goes in v12:
time: 166 us; the launch traced here: 163 us
  blocking collectives  60.5 us (36%)
  waiting for transfers between devices  36.7 us (22%)
  starting transfers between devices  32.2 us (19%)
  Pallas kernels  13.6 us (8%)
  between operations  13.6 us (8%)
  other arithmetic  3.82 us (2%)
  local copies, waits for them, and re-layouts  2.65 us (2%)
    reduce_scatter x1, waiting for transfers between devices, shards(): half = lax.psum_scatter(products, 'y', scatter_dimension=0, tiled=True)  30.2 us
    all_to_all x2, blocking collectives, gather(): return lax.all_to_all(copies, axis, 0, 0, tiled=True)  30 us
    all_to_all x1, blocking collectives, shards(): pairs = lax.all_to_all(pairs, ('x', 'z'), 0, 0, tiled=True)  23.9 us
    ppermute x2, starting transfers between devices, swap(): return lax.ppermute(value, 'core', [(0, 1), (1, 0)])  11.7 us
    pallas_call x1, Pallas kernels, first(): pl.pallas_call(first_kernel, out_shape=jax.ShapeDtypeStruct((occ, width),...  11.3 us
    ppermute x3, starting transfers between devices, shifts(): lax.ppermute(value, axis, [(i, (i + step) % count) for i in range(count)])  8.41 us
    all_to_all x1, starting transfers between devices, gather(): return lax.all_to_all(copies, axis, 0, 0, tiled=True)  6.96 us
    all_gather x1, blocking collectives, shards(): lax.all_gather(half, 'core')  6.64 us
  transfers between devices with their start and end apart: 9, of which 5 were waited for; matrix products, arithmetic and copies ran while one was open for 2% of the time, Pallas kernels for 7%

profile of v12, /device:TPU:1, one launch (start us, length us, event | category | flops | bytes accessed | tf_op | source)
XLA Modules:
  0.0 163.1 jit_solution(2799920544737607812)
XLA Ops:
  6.5 0.0 copy-start
  6.5 0.0 copy-start.2
  6.5 0.0 all-gather.3.cloned.1.call-start
  6.6 0.7 copy-done
  7.2 0.2 compare_reduce_fusion
  7.4 0.1 broadcast_bitcast_fusion
  7.5 0.9 multiply_bitcast_fusion
  8.4 0.0 copy-start.8
  8.5 11.0 %all_to_all.25 = f32[4,16,1536]{2,1,0:T(8,128)} all-to-all(f32[4,16,1536]{2,1,0:T(8,128)S(1)} %broadcast_in_dim.11), channel_id=1, replica_groups=mesh['y'=8,'x'=4,'z'=8,'core'=2] {'x'}, dimensions={0} | all-to-all | bytes 786432 | tf_op jit(solution)/shard_map/all_to_all | solution.py:26
  19.5 0.0 all-gather.3.cloned.1.call-update
  19.5 8.3 %collective-permute-start.4 = (f32[2,2048,256]{2,1,0:T(8,128)}, f32[2,2048,256]{2,1,0:T(8,128)}, u32[]{:S(2)}, u32[]{:S(2)}) collective-permute-start(f32[2,2048,256]{2,1,0:T(8,128)} %own_hbm.1), channel_id=1, source_target_pairs={{0,1},{1,0},{2,3},{3,2},{4,5},{5,4},{6,7},{7,6},{8,9},{9,8},{10,11... | collective-permute-start | bytes 12582920 | tf_op jit(solution)/shard_map/ppermute | solution.py:21
  27.8 0.8 fusion.1
  28.6 19.0 %all_to_all.26.rest_0 = f32[8,16,512]{2,1,0:T(8,128)S(1)} all-to-all(f32[8,16,512]{2,1,0:T(8,128)S(1)} %broadcast_in_dim.12), channel_id=1, replica_groups=mesh['y'=8,'x'=4,'z'=8,'core'=2] {'z'}, dimensions={0} | all-to-all | bytes 524288 | tf_op jit(solution)/shard_map/all_to_all | solution.py:26
  47.6 0.0 copy-start.1
  47.6 0.0 copy-done.2
  47.6 1.1 broadcast_in_dim.13
  48.7 7.0 %all-to-all-start.2 = ((f32[8,16,2048]{2,1,0:T(8,128)}), f32[8,16,2048]{2,1,0:T(8,128)S(1)}, u32[]{:S(2)}, u32[]{:S(2)}) async-start(f32[8,16,2048]{2,1,0:T(8,128)} %broadcast_in_dim.13), calls=%async_computation.2 | async-start | bytes 2097152 | tf_op jit(solution)/shard_map/all_to_all | solution.py:26
  55.7 0.0 reduce-scatter.2.cloned.1.call-start
  55.7 1.9 %collective-permute-start.1 = (f32[8,16,512]{2,1,0:T(8,128)S(1)}, f32[8,16,512]{2,1,0:T(8,128)S(1)}, u32[]{:S(2)}, u32[]{:S(2)}) collective-permute-start(f32[8,16,512]{2,1,0:T(8,128)S(1)} %all_to_all.26.rest_0), channel_id=1, source_target_pairs={{0,16},{16,32},{32,48},{48,0},{1,17},{17,33},{33,49},{49,1},{2,18}... | collective-permute-start | bytes 786440 | tf_op jit(solution)/shard_map/ppermute | solution.py:31
  57.7 3.1 %collective-permute-start.2 = (f32[8,16,512]{2,1,0:T(8,128)S(1)}, f32[8,16,512]{2,1,0:T(8,128)S(1)}, u32[]{:S(2)}, u32[]{:S(2)}) collective-permute-start(f32[8,16,512]{2,1,0:T(8,128)S(1)} %all_to_all.26.rest_0), channel_id=1, source_target_pairs={{0,32},{16,48},{32,0},{48,16},{1,33},{17,49},{33,1},{49,17},{2,34}... | collective-permute-start | bytes 786440 | tf_op jit(solution)/shard_map/ppermute | solution.py:31
  60.7 3.4 %collective-permute-start.3 = (f32[8,16,512]{2,1,0:T(8,128)S(1)}, f32[8,16,512]{2,1,0:T(8,128)S(1)}, u32[]{:S(2)}, u32[]{:S(2)}) collective-permute-start(f32[8,16,512]{2,1,0:T(8,128)S(1)} %all_to_all.26.rest_0), channel_id=1, source_target_pairs={{0,48},{16,0},{32,16},{48,32},{1,49},{17,1},{33,17},{49,33},{2,50}... | collective-permute-start | bytes 786440 | tf_op jit(solution)/shard_map/ppermute | solution.py:31
  64.2 0.0 copy-done.8
  64.2 0.1 copy.8.own_screen
  64.3 0.0 copy-start.6
  64.3 3.5 %collective-permute-start = (s32[16,2]{1,0:T(8,128)S(1)}, s32[16,2]{1,0:T(8,128)S(1)}, u32[]{:S(2)}, u32[]{:S(2)}) collective-permute-start(s32[16,2]{1,0:T(8,128)S(1)} %copy.8.own_screen), channel_id=1, source_target_pairs={{0,1},{1,0},{2,3},{3,2},{4,5},{5,4},{6,7},{7,6},{8,9},{9,8},{10,11... | collective-permute-start | bytes 392 | tf_op jit(solution)/shard_map/ppermute | solution.py:21
  67.7 0.8 collective-permute-done.other_screen
  68.5 0.0 copy-start.7
  68.6 0.0 collective-permute-done.1.rest_1
  68.6 0.0 copy-start.3
  68.6 1.1 collective-permute-done.2.rest_2
  69.7 0.0 copy-start.4
  69.7 4.5 %collective-permute-done.3.rest_3 = f32[8,16,512]{2,1,0:T(8,128)S(1)} collective-permute-done((f32[8,16,512]{2,1,0:T(8,128)S(1)}, f32[8,16,512]{2,1,0:T(8,128)S(1)}, u32[]{:S(2)}, u32[]{:S(2)}) %collective-permute-start.3) | collective-permute-done | bytes 262176 | tf_op jit(solution)/shard_map/ppermute | solution.py:31
  74.2 0.0 copy-start.5
  74.2 0.0 collective-permute-done.4.other_hbm
  74.2 0.1 all-gather.3.cloned.1.call-done.coef_hbm
  74.3 0.0 copy-done.1
  74.3 0.0 copy-done.6
  74.3 0.0 copy-done.7
  74.3 0.0 copy-done.3
  74.3 0.0 copy-done.4
  74.3 0.6 copy-done.5
  74.9 11.3 %shard_map.46 = f32[512,1024]{1,0:T(8,128)} custom-call(s32[1]{0:T(128)} %bitcast.6.own_x, s32[16,2]{1,0:T(8,128)} %copy-done.6, s32[16,2]{1,0:T(8,128)} %copy-done.7, f32[512,1536]{1,0:T(8,128)} %all-gather.3.cloned.1.call-done.coef_hbm, f32[8,16,512]{2,1,0:T(8,128)} %copy-done.1, f32[8,16,512]{2,1,0:T(8,128)} %copy-done.3, f32[8,16,512]{2,1,0:T(8,128)} %copy-done.4, ...), custom_call_target="tpu_custom_call" | custom-call | tf_op jit(solution)/shard_map/pallas_call | solution.py:108
  86.1 0.0 reduce-scatter.2.cloned.1.call-update
  86.2 0.0 all-to-all-done.2
  86.2 0.1 fusion.2
  86.3 0.1 pad_maximum_fusion
  86.3 0.8 slice_multiply_fusion
  87.1 1.1 broadcast_add_fusion
  88.2 5.1 %all-to-all-start.3 = ((f32[32,16,512]{2,1,0:T(8,128)}), f32[32,16,512]{2,1,0:T(8,128)S(1)}, u32[]{:S(2)}, u32[]{:S(2)}) async-start(f32[32,16,512]{2,1,0:T(8,128)} %broadcast_add_fusion), calls=%async_computation.3 | async-start | bytes 2097152 | tf_op jit(solution)/shard_map/all_to_all | solution.py:202
  93.3 30.2 %reduce-scatter.2.cloned.1.call-done = f32[64,1024]{1,0:T(8,128)} async-done(((f32[512,1024]{1,0:T(8,128)}), f32[64,1024]{1,0:T(8,128)}) %reduce-scatter.2.cloned.1.call-update) | async-done | bytes 262160 | tf_op jit(solution)/shard_map/reduce_scatter | solution.py:197
  123.5 6.6 %all-gather = f32[128,1024]{1,0:T(8,128)S(1)} all-gather(f32[64,1024]{1,0:T(8,128)} %reduce-scatter.2.cloned.1.call-done), channel_id=2, replica_groups=mesh['y'=8,'x'=4,'z'=8,'core'=2] {'core'}, dimensions={0}, use_global_device_ids=true | all-gather | bytes 786432 | tf_op jit(solution)/shard_map/all_gather | solution.py:203
  130.1 0.0 all-to-all-done.3
  130.1 0.6 shard_map.47
  130.7 23.9 %all_to_all.27.parts_ref = f32[32,16,256]{2,1,0:T(8,128)} all-to-all(f32[32,16,256]{2,1,0:T(8,128)S(1)} %bitcast.23), channel_id=1, replica_groups=mesh['y'=8,'x'=4,'z'=8,'core'=2] {'x','z'}, dimensions={0} | all-to-all | bytes 1048576 | tf_op jit(solution)/shard_map/all_to_all | solution.py:205
  154.6 1.7 %shard_map.48 = f32[2,16,128]{2,1,0:T(8,128)} custom-call(f32[32,16,256]{2,1,0:T(8,128)} %all_to_all.27.parts_ref), custom_call_target="tpu_custom_call" | custom-call | tf_op jit(solution)/shard_map/pallas_call | solution.py:168
  (8 shorter events, 0.1 us)
Async XLA Ops:
  6.5 0.7 copy-start
  6.5 41.1 %copy-start.2 = (f32[2048,16]{0,1:T(8,128)S(1)}, f32[2048,16]{0,1:T(8,128)}, u32[]{:S(2)}) copy-start(f32[2048,16]{0,1:T(8,128)} %param.5) | copy-start | bytes 393220
  6.5 67.7 %all-gather.3.cloned.1.call-start = ((), (), s32[]{:S(2)}) async-start(), calls=%async_computation.6 | async-start | bytes 3538944 | tf_op jit(solution)/shard_map/all_gather | solution.py:188
  8.4 55.7 %copy-start.8 = (s32[16,2]{0,1:T(2,128)S(1)}, s32[16,2]{0,1:T(2,128)}, u32[]{:S(2)}) copy-start(s32[16,2]{0,1:T(2,128)} %param.6) | copy-start | bytes 388
  19.5 54.7 %collective-permute-start.4 = (f32[2,2048,256]{2,1,0:T(8,128)}, f32[2,2048,256]{2,1,0:T(8,128)}, u32[]{:S(2)}, u32[]{:S(2)}) collective-permute-start(f32[2,2048,256]{2,1,0:T(8,128)} %own_hbm.1), channel_id=1, source_target_pairs={{0,1},{1,0},{2,3},{3,2},{4,5},{5,4},{6,7},{7,6},{8,9},{9,8},{10,11... | collective-permute-start | bytes 12582920 | tf_op jit(solution)/shard_map/ppermute | solution.py:21
  47.6 26.7 %copy-start.1 = (f32[8,16,512]{2,1,0:T(8,128)}, f32[8,16,512]{2,1,0:T(8,128)S(1)}, u32[]{:S(2)}) copy-start(f32[8,16,512]{2,1,0:T(8,128)S(1)} %all_to_all.26.rest_0) | copy-start | bytes 786436
  48.7 37.4 %all-to-all-start.2 = ((f32[8,16,2048]{2,1,0:T(8,128)}), f32[8,16,2048]{2,1,0:T(8,128)S(1)}, u32[]{:S(2)}, u32[]{:S(2)}) async-start(f32[8,16,2048]{2,1,0:T(8,128)} %broadcast_in_dim.13), calls=%async_computation.2 | async-start | bytes 2097152 | tf_op jit(solution)/shard_map/all_to_all | solution.py:26
  55.7 67.8 %reduce-scatter.2.cloned.1.call-start = ((), (), s32[]{:S(2)}) async-start(), calls=%async_computation.7 | async-start | bytes 2359296 | tf_op jit(solution)/shard_map/reduce_scatter | solution.py:197
  55.7 12.8 %collective-permute-start.1 = (f32[8,16,512]{2,1,0:T(8,128)S(1)}, f32[8,16,512]{2,1,0:T(8,128)S(1)}, u32[]{:S(2)}, u32[]{:S(2)}) collective-permute-start(f32[8,16,512]{2,1,0:T(8,128)S(1)} %all_to_all.26.rest_0), channel_id=1, source_target_pairs={{0,16},{16,32},{32,48},{48,0},{1,17},{17,33},{33,49},{49,1},{2,18}... | collective-permute-start | bytes 786440 | tf_op jit(solution)/shard_map/ppermute | solution.py:31
  57.7 12.0 %collective-permute-start.2 = (f32[8,16,512]{2,1,0:T(8,128)S(1)}, f32[8,16,512]{2,1,0:T(8,128)S(1)}, u32[]{:S(2)}, u32[]{:S(2)}) collective-permute-start(f32[8,16,512]{2,1,0:T(8,128)S(1)} %all_to_all.26.rest_0), channel_id=1, source_target_pairs={{0,32},{16,48},{32,0},{48,16},{1,33},{17,49},{33,1},{49,17},{2,34}... | collective-permute-start | bytes 786440 | tf_op jit(solution)/shard_map/ppermute | solution.py:31
  60.7 13.4 %collective-permute-start.3 = (f32[8,16,512]{2,1,0:T(8,128)S(1)}, f32[8,16,512]{2,1,0:T(8,128)S(1)}, u32[]{:S(2)}, u32[]{:S(2)}) collective-permute-start(f32[8,16,512]{2,1,0:T(8,128)S(1)} %all_to_all.26.rest_0), channel_id=1, source_target_pairs={{0,48},{16,0},{32,16},{48,32},{1,49},{17,1},{33,17},{49,33},{2,50}... | collective-permute-start | bytes 786440 | tf_op jit(solution)/shard_map/ppermute | solution.py:31
  64.3 10.0 %copy-start.6 = (s32[16,2]{1,0:T(8,128)}, s32[16,2]{1,0:T(8,128)S(1)}, u32[]{:S(2)}) copy-start(s32[16,2]{1,0:T(8,128)S(1)} %copy.8.own_screen) | copy-start | bytes 388
  64.3 4.3 %collective-permute-start = (s32[16,2]{1,0:T(8,128)S(1)}, s32[16,2]{1,0:T(8,128)S(1)}, u32[]{:S(2)}, u32[]{:S(2)}) collective-permute-start(s32[16,2]{1,0:T(8,128)S(1)} %copy.8.own_screen), channel_id=1, source_target_pairs={{0,1},{1,0},{2,3},{3,2},{4,5},{5,4},{6,7},{7,6},{8,9},{9,8},{10,11... | collective-permute-start | bytes 392 | tf_op jit(solution)/shard_map/ppermute | solution.py:21
  68.5 5.7 %copy-start.7 = (s32[16,2]{1,0:T(8,128)}, s32[16,2]{1,0:T(8,128)S(1)}, u32[]{:S(2)}) copy-start(s32[16,2]{1,0:T(8,128)S(1)} %collective-permute-done.other_screen) | copy-start | bytes 388
  68.6 5.7 %copy-start.3 = (f32[8,16,512]{2,1,0:T(8,128)}, f32[8,16,512]{2,1,0:T(8,128)S(1)}, u32[]{:S(2)}) copy-start(f32[8,16,512]{2,1,0:T(8,128)S(1)} %collective-permute-done.1.rest_1) | copy-start | bytes 786436
  69.7 4.6 %copy-start.4 = (f32[8,16,512]{2,1,0:T(8,128)}, f32[8,16,512]{2,1,0:T(8,128)S(1)}, u32[]{:S(2)}) copy-start(f32[8,16,512]{2,1,0:T(8,128)S(1)} %collective-permute-done.2.rest_2) | copy-start | bytes 786436
  74.2 0.7 copy-start.5
  88.2 41.9 %all-to-all-start.3 = ((f32[32,16,512]{2,1,0:T(8,128)}), f32[32,16,512]{2,1,0:T(8,128)S(1)}, u32[]{:S(2)}, u32[]{:S(2)}) async-start(f32[32,16,512]{2,1,0:T(8,128)} %broadcast_add_fusion), calls=%async_computation.3 | async-start | bytes 2097152 | tf_op jit(solution)/shard_map/all_to_all | solution.py:202
Sparse Core Ops, SparseCore 0:
  19.6 54.6 all-gather.2
  86.3 37.1 reduce-scatter.1

commit v13 on v12

--- a/solution.py
+++ b/solution.py
@@ -190,7 +190,7 @@
     along_z = gather(coef[:, most:] + 0.0 * along_x[0, :, :REST], "z")
     rests = shifts(along_z, "x")
 
-    along_y = gather(coef + 0.0 * jnp.pad(along_z[0], ((0, 0), (0, most))), "y")
+    along_y = gather(coef + 0.0 * jnp.pad(along_x[0], ((0, 0), (0, REST))), "y")
 
     own_x = lax.axis_index("x")[None]
     products = first(own_x, screen, swap(screen), gathered, rests, integrals, swap(integrals))

time: 166 us -> 168 us (1.012)
  blocking collectives: 60.5 us -> 41.4 us
  waiting for transfers between devices: 36.7 us -> 48.8 us
  starting transfers between devices: 32.2 us -> 38.8 us
  local copies, waits for them, and re-layouts: 2.65 us -> 4.35 us
    all_to_all x2 -> x1, blocking collectives: 30 us -> 11 us  [gather(): return lax.all_to_all(copies, axis, 0, 0, tiled=True)]
    all_to_all x1 -> x2, waiting for transfers between devices: 0.01 us -> 12.2 us  [gather(): return lax.all_to_all(copies, axis, 0, 0, tiled=True)]
    all_to_all x1 -> x2, starting transfers between devices: 6.96 us -> 13.5 us  [gather(): return lax.all_to_all(copies, axis, 0, 0, tiled=True)]
  transfers between devices with their start and end apart: 9 -> 10, of which waited for: 5 -> 5; matrix products, arithmetic and copies ran while one was open for 2% -> 3% of each run, Pallas kernels for 7% -> 7%
where the time goes in v13:
time: 168 us; the launch traced here: 164 us
  waiting for transfers between devices  48.8 us (29%)
  blocking collectives  41.4 us (25%)
  starting transfers between devices  38.8 us (23%)
  Pallas kernels  13.6 us (8%)
  between operations  13.6 us (8%)
  local copies, waits for them, and re-layouts  4.35 us (3%)
  other arithmetic  3.83 us (2%)
    reduce_scatter x1, waiting for transfers between devices, shards(): half = lax.psum_scatter(products, 'y', scatter_dimension=0, tiled=True)  30.2 us
    all_to_all x1, blocking collectives, shards(): pairs = lax.all_to_all(pairs, ('x', 'z'), 0, 0, tiled=True)  23.9 us
    all_to_all x2, starting transfers between devices, gather(): return lax.all_to_all(copies, axis, 0, 0, tiled=True)  13.5 us
    all_to_all x2, waiting for transfers between devices, gather(): return lax.all_to_all(copies, axis, 0, 0, tiled=True)  12.2 us
    ppermute x2, starting transfers between devices, swap(): return lax.ppermute(value, 'core', [(0, 1), (1, 0)])  11.7 us
    pallas_call x1, Pallas kernels, first(): pl.pallas_call(first_kernel, out_shape=jax.ShapeDtypeStruct((occ, width),...  11.3 us
    all_to_all x1, blocking collectives, gather(): return lax.all_to_all(copies, axis, 0, 0, tiled=True)  11 us
    ppermute x3, starting transfers between devices, shifts(): lax.ppermute(value, axis, [(i, (i + step) % count) for i in range(count)])  8.41 us
  transfers between devices with their start and end apart: 10, of which 5 were waited for; matrix products, arithmetic and copies ran while one was open for 3% of the time, Pallas kernels for 7%

profile of v13, /device:TPU:1, one launch (start us, length us, event | category | flops | bytes accessed | tf_op | source)
XLA Modules:
  0.0 164.4 jit_solution(5427846216475456304)
XLA Ops:
  6.5 0.0 copy-start
  6.5 0.0 copy-start.2
  6.5 0.0 all-gather.3.cloned.1.call-start
  6.6 0.7 copy-done
  7.2 0.2 compare_reduce_fusion
  7.4 0.1 broadcast_bitcast_fusion
  7.5 0.9 multiply_bitcast_fusion
  8.4 0.0 copy-start.8
  8.5 11.0 %all_to_all.25 = f32[4,16,1536]{2,1,0:T(8,128)} all-to-all(f32[4,16,1536]{2,1,0:T(8,128)S(1)} %broadcast_in_dim.11), channel_id=1, replica_groups=mesh['y'=8,'x'=4,'z'=8,'core'=2] {'x'}, dimensions={0} | all-to-all | bytes 786432 | tf_op jit(solution)/shard_map/all_to_all | solution.py:26
  19.5 0.0 all-gather.3.cloned.1.call-update
  19.5 8.3 %collective-permute-start.4 = (f32[2,2048,256]{2,1,0:T(8,128)}, f32[2,2048,256]{2,1,0:T(8,128)}, u32[]{:S(2)}, u32[]{:S(2)}) collective-permute-start(f32[2,2048,256]{2,1,0:T(8,128)} %own_hbm.1), channel_id=1, source_target_pairs={{0,1},{1,0},{2,3},{3,2},{4,5},{5,4},{6,7},{7,6},{8,9},{9,8},{10,11... | collective-permute-start | bytes 12582920 | tf_op jit(solution)/shard_map/ppermute | solution.py:21
  27.8 0.8 fusion.1
  28.5 0.7 broadcast_in_dim.14
  29.3 6.5 %all-to-all-start.2 = ((f32[8,16,512]{2,1,0:T(8,128)}), f32[8,16,512]{2,1,0:T(8,128)S(1)}, u32[]{:S(2)}, u32[]{:S(2)}) async-start(f32[8,16,512]{2,1,0:T(8,128)} %broadcast_in_dim.14), calls=%async_computation.2 | async-start | bytes 524288 | tf_op jit(solution)/shard_map/all_to_all | solution.py:26
  35.7 0.9 slice_bitcast_fusion
  36.6 0.0 copy-done.2
  36.7 12.2 %all-to-all-done.2.rest_0 = f32[8,16,512]{2,1,0:T(8,128)S(1)} async-done(((f32[8,16,512]{2,1,0:T(8,128)}), f32[8,16,512]{2,1,0:T(8,128)S(1)}, u32[]{:S(2)}, u32[]{:S(2)}) %all-to-all-start.2) | async-done | bytes 262176 | tf_op jit(solution)/shard_map/all_to_all | solution.py:26
  48.9 0.0 copy-start.1
  48.9 1.1 broadcast_in_dim.12
  50.0 7.0 %all-to-all-start.1 = ((f32[8,16,2048]{2,1,0:T(8,128)}), f32[8,16,2048]{2,1,0:T(8,128)S(1)}, u32[]{:S(2)}, u32[]{:S(2)}) async-start(f32[8,16,2048]{2,1,0:T(8,128)} %broadcast_in_dim.12), calls=%async_computation.1 | async-start | bytes 2097152 | tf_op jit(solution)/shard_map/all_to_all | solution.py:26
  57.0 0.0 reduce-scatter.2.cloned.1.call-start
  57.0 1.9 %collective-permute-start.1 = (f32[8,16,512]{2,1,0:T(8,128)S(1)}, f32[8,16,512]{2,1,0:T(8,128)S(1)}, u32[]{:S(2)}, u32[]{:S(2)}) collective-permute-start(f32[8,16,512]{2,1,0:T(8,128)S(1)} %all-to-all-done.2.rest_0), channel_id=1, source_target_pairs={{0,16},{16,32},{32,48},{48,0},{1,17},{17,33},{33,49},{49,1},{2,18}... | collective-permute-start | bytes 786440 | tf_op jit(solution)/shard_map/ppermute | solution.py:31
  59.0 3.2 %collective-permute-start.2 = (f32[8,16,512]{2,1,0:T(8,128)S(1)}, f32[8,16,512]{2,1,0:T(8,128)S(1)}, u32[]{:S(2)}, u32[]{:S(2)}) collective-permute-start(f32[8,16,512]{2,1,0:T(8,128)S(1)} %all-to-all-done.2.rest_0), channel_id=1, source_target_pairs={{0,32},{16,48},{32,0},{48,16},{1,33},{17,49},{33,1},{49,17},{2,34}... | collective-permute-start | bytes 786440 | tf_op jit(solution)/shard_map/ppermute | solution.py:31
  62.2 3.3 %collective-permute-start.3 = (f32[8,16,512]{2,1,0:T(8,128)S(1)}, f32[8,16,512]{2,1,0:T(8,128)S(1)}, u32[]{:S(2)}, u32[]{:S(2)}) collective-permute-start(f32[8,16,512]{2,1,0:T(8,128)S(1)} %all-to-all-done.2.rest_0), channel_id=1, source_target_pairs={{0,48},{16,0},{32,16},{48,32},{1,49},{17,1},{33,17},{49,33},{2,50}... | collective-permute-start | bytes 786440 | tf_op jit(solution)/shard_map/ppermute | solution.py:31
  65.5 0.0 copy-done.8
  65.5 0.1 copy.8.own_screen
  65.6 0.0 copy-start.6
  65.6 3.5 %collective-permute-start = (s32[16,2]{1,0:T(8,128)S(1)}, s32[16,2]{1,0:T(8,128)S(1)}, u32[]{:S(2)}, u32[]{:S(2)}) collective-permute-start(s32[16,2]{1,0:T(8,128)S(1)} %copy.8.own_screen), channel_id=1, source_target_pairs={{0,1},{1,0},{2,3},{3,2},{4,5},{5,4},{6,7},{7,6},{8,9},{9,8},{10,11... | collective-permute-start | bytes 392 | tf_op jit(solution)/shard_map/ppermute | solution.py:21
  69.0 0.8 collective-permute-done.other_screen
  69.9 0.0 copy-start.7
  69.9 0.0 collective-permute-done.1.rest_1
  69.9 0.0 copy-start.3
  69.9 1.4 collective-permute-done.2.rest_2
  71.3 0.0 copy-start.4
  71.3 4.2 %collective-permute-done.3.rest_3 = f32[8,16,512]{2,1,0:T(8,128)S(1)} collective-permute-done((f32[8,16,512]{2,1,0:T(8,128)S(1)}, f32[8,16,512]{2,1,0:T(8,128)S(1)}, u32[]{:S(2)}, u32[]{:S(2)}) %collective-permute-start.3) | collective-permute-done | bytes 262176 | tf_op jit(solution)/shard_map/ppermute | solution.py:31
  75.5 0.0 copy-start.5
  75.5 0.0 collective-permute-done.4.other_hbm
  75.5 0.0 all-gather.3.cloned.1.call-done.coef_hbm
  75.5 0.0 copy-done.1
  75.5 0.0 copy-done.6
  75.5 0.0 copy-done.7
  75.5 0.0 copy-done.3
  75.5 0.0 copy-done.4
  75.5 0.6 copy-done.5
  76.2 11.3 %shard_map.46 = f32[512,1024]{1,0:T(8,128)} custom-call(s32[1]{0:T(128)} %bitcast.5.own_x, s32[16,2]{1,0:T(8,128)} %copy-done.6, s32[16,2]{1,0:T(8,128)} %copy-done.7, f32[512,1536]{1,0:T(8,128)} %all-gather.3.cloned.1.call-done.coef_hbm, f32[8,16,512]{2,1,0:T(8,128)} %copy-done.1, f32[8,16,512]{2,1,0:T(8,128)} %copy-done.3, f32[8,16,512]{2,1,0:T(8,128)} %copy-done.4, ...), custom_call_target="tpu_custom_call" | custom-call | tf_op jit(solution)/shard_map/pallas_call | solution.py:108
  87.4 0.0 reduce-scatter.2.cloned.1.call-update
  87.5 0.0 all-to-all-done.1
  87.5 0.1 fusion.2
  87.6 0.1 pad_maximum_fusion
  87.7 0.8 slice_multiply_fusion
  88.4 1.1 broadcast_add_fusion
  89.5 5.1 %all-to-all-start.3 = ((f32[32,16,512]{2,1,0:T(8,128)}), f32[32,16,512]{2,1,0:T(8,128)S(1)}, u32[]{:S(2)}, u32[]{:S(2)}) async-start(f32[32,16,512]{2,1,0:T(8,128)} %broadcast_add_fusion), calls=%async_computation.3 | async-start | bytes 2097152 | tf_op jit(solution)/shard_map/all_to_all | solution.py:202
  94.6 30.2 %reduce-scatter.2.cloned.1.call-done = f32[64,1024]{1,0:T(8,128)} async-done(((f32[512,1024]{1,0:T(8,128)}), f32[64,1024]{1,0:T(8,128)}) %reduce-scatter.2.cloned.1.call-update) | async-done | bytes 262160 | tf_op jit(solution)/shard_map/reduce_scatter | solution.py:197
  124.8 6.5 %all-gather = f32[128,1024]{1,0:T(8,128)S(1)} all-gather(f32[64,1024]{1,0:T(8,128)} %reduce-scatter.2.cloned.1.call-done), channel_id=2, replica_groups=mesh['y'=8,'x'=4,'z'=8,'core'=2] {'core'}, dimensions={0}, use_global_device_ids=true | all-gather | bytes 786432 | tf_op jit(solution)/shard_map/all_gather | solution.py:203
  131.3 0.0 all-to-all-done.3
  131.3 0.6 shard_map.47
  131.9 23.9 %all_to_all.26.parts_ref = f32[32,16,256]{2,1,0:T(8,128)} all-to-all(f32[32,16,256]{2,1,0:T(8,128)S(1)} %bitcast.23), channel_id=1, replica_groups=mesh['y'=8,'x'=4,'z'=8,'core'=2] {'x','z'}, dimensions={0} | all-to-all | bytes 1048576 | tf_op jit(solution)/shard_map/all_to_all | solution.py:205
  155.8 1.7 %shard_map.48 = f32[2,16,128]{2,1,0:T(8,128)} custom-call(f32[32,16,256]{2,1,0:T(8,128)} %all_to_all.26.parts_ref), custom_call_target="tpu_custom_call" | custom-call | tf_op jit(solution)/shard_map/pallas_call | solution.py:168
  (6 shorter events, 0.1 us)
Async XLA Ops:
  6.5 0.7 copy-start
  6.5 30.1 %copy-start.2 = (f32[2048,16]{0,1:T(8,128)S(1)}, f32[2048,16]{0,1:T(8,128)}, u32[]{:S(2)}) copy-start(f32[2048,16]{0,1:T(8,128)} %param.5) | copy-start | bytes 393220
  6.5 68.9 %all-gather.3.cloned.1.call-start = ((), (), s32[]{:S(2)}) async-start(), calls=%async_computation.6 | async-start | bytes 3538944 | tf_op jit(solution)/shard_map/all_gather | solution.py:188
  8.4 57.0 %copy-start.8 = (s32[16,2]{0,1:T(2,128)S(1)}, s32[16,2]{0,1:T(2,128)}, u32[]{:S(2)}) copy-start(s32[16,2]{0,1:T(2,128)} %param.6) | copy-start | bytes 388
  19.5 56.0 %collective-permute-start.4 = (f32[2,2048,256]{2,1,0:T(8,128)}, f32[2,2048,256]{2,1,0:T(8,128)}, u32[]{:S(2)}, u32[]{:S(2)}) collective-permute-start(f32[2,2048,256]{2,1,0:T(8,128)} %own_hbm.1), channel_id=1, source_target_pairs={{0,1},{1,0},{2,3},{3,2},{4,5},{5,4},{6,7},{7,6},{8,9},{9,8},{10,11... | collective-permute-start | bytes 12582920 | tf_op jit(solution)/shard_map/ppermute | solution.py:21
  29.3 19.6 %all-to-all-start.2 = ((f32[8,16,512]{2,1,0:T(8,128)}), f32[8,16,512]{2,1,0:T(8,128)S(1)}, u32[]{:S(2)}, u32[]{:S(2)}) async-start(f32[8,16,512]{2,1,0:T(8,128)} %broadcast_in_dim.14), calls=%async_computation.2 | async-start | bytes 524288 | tf_op jit(solution)/shard_map/all_to_all | solution.py:26
  48.9 26.6 %copy-start.1 = (f32[8,16,512]{2,1,0:T(8,128)}, f32[8,16,512]{2,1,0:T(8,128)S(1)}, u32[]{:S(2)}) copy-start(f32[8,16,512]{2,1,0:T(8,128)S(1)} %all-to-all-done.2.rest_0) | copy-start | bytes 786436
  50.0 37.5 %all-to-all-start.1 = ((f32[8,16,2048]{2,1,0:T(8,128)}), f32[8,16,2048]{2,1,0:T(8,128)S(1)}, u32[]{:S(2)}, u32[]{:S(2)}) async-start(f32[8,16,2048]{2,1,0:T(8,128)} %broadcast_in_dim.12), calls=%async_computation.1 | async-start | bytes 2097152 | tf_op jit(solution)/shard_map/all_to_all | solution.py:26
  57.0 67.8 %reduce-scatter.2.cloned.1.call-start = ((), (), s32[]{:S(2)}) async-start(), calls=%async_computation.7 | async-start | bytes 2359296 | tf_op jit(solution)/shard_map/reduce_scatter | solution.py:197
  57.0 12.8 %collective-permute-start.1 = (f32[8,16,512]{2,1,0:T(8,128)S(1)}, f32[8,16,512]{2,1,0:T(8,128)S(1)}, u32[]{:S(2)}, u32[]{:S(2)}) collective-permute-start(f32[8,16,512]{2,1,0:T(8,128)S(1)} %all-to-all-done.2.rest_0), channel_id=1, source_target_pairs={{0,16},{16,32},{32,48},{48,0},{1,17},{17,33},{33,49},{49,1},{2,18}... | collective-permute-start | bytes 786440 | tf_op jit(solution)/shard_map/ppermute | solution.py:31
  59.0 12.3 %collective-permute-start.2 = (f32[8,16,512]{2,1,0:T(8,128)S(1)}, f32[8,16,512]{2,1,0:T(8,128)S(1)}, u32[]{:S(2)}, u32[]{:S(2)}) collective-permute-start(f32[8,16,512]{2,1,0:T(8,128)S(1)} %all-to-all-done.2.rest_0), channel_id=1, source_target_pairs={{0,32},{16,48},{32,0},{48,16},{1,33},{17,49},{33,1},{49,17},{2,34}... | collective-permute-start | bytes 786440 | tf_op jit(solution)/shard_map/ppermute | solution.py:31
  62.2 13.3 %collective-permute-start.3 = (f32[8,16,512]{2,1,0:T(8,128)S(1)}, f32[8,16,512]{2,1,0:T(8,128)S(1)}, u32[]{:S(2)}, u32[]{:S(2)}) collective-permute-start(f32[8,16,512]{2,1,0:T(8,128)S(1)} %all-to-all-done.2.rest_0), channel_id=1, source_target_pairs={{0,48},{16,0},{32,16},{48,32},{1,49},{17,1},{33,17},{49,33},{2,50}... | collective-permute-start | bytes 786440 | tf_op jit(solution)/shard_map/ppermute | solution.py:31
  65.6 9.9 %copy-start.6 = (s32[16,2]{1,0:T(8,128)}, s32[16,2]{1,0:T(8,128)S(1)}, u32[]{:S(2)}) copy-start(s32[16,2]{1,0:T(8,128)S(1)} %copy.8.own_screen) | copy-start | bytes 388
  65.6 4.3 %collective-permute-start = (s32[16,2]{1,0:T(8,128)S(1)}, s32[16,2]{1,0:T(8,128)S(1)}, u32[]{:S(2)}, u32[]{:S(2)}) collective-permute-start(s32[16,2]{1,0:T(8,128)S(1)} %copy.8.own_screen), channel_id=1, source_target_pairs={{0,1},{1,0},{2,3},{3,2},{4,5},{5,4},{6,7},{7,6},{8,9},{9,8},{10,11... | collective-permute-start | bytes 392 | tf_op jit(solution)/shard_map/ppermute | solution.py:21
  69.9 5.6 %copy-start.7 = (s32[16,2]{1,0:T(8,128)}, s32[16,2]{1,0:T(8,128)S(1)}, u32[]{:S(2)}) copy-start(s32[16,2]{1,0:T(8,128)S(1)} %collective-permute-done.other_screen) | copy-start | bytes 388
  69.9 5.6 %copy-start.3 = (f32[8,16,512]{2,1,0:T(8,128)}, f32[8,16,512]{2,1,0:T(8,128)S(1)}, u32[]{:S(2)}) copy-start(f32[8,16,512]{2,1,0:T(8,128)S(1)} %collective-permute-done.1.rest_1) | copy-start | bytes 786436
  71.3 4.3 %copy-start.4 = (f32[8,16,512]{2,1,0:T(8,128)}, f32[8,16,512]{2,1,0:T(8,128)S(1)}, u32[]{:S(2)}) copy-start(f32[8,16,512]{2,1,0:T(8,128)S(1)} %collective-permute-done.2.rest_2) | copy-start | bytes 786436
  75.5 0.7 copy-start.5
  89.5 41.8 %all-to-all-start.3 = ((f32[32,16,512]{2,1,0:T(8,128)}), f32[32,16,512]{2,1,0:T(8,128)S(1)}, u32[]{:S(2)}, u32[]{:S(2)}) async-start(f32[32,16,512]{2,1,0:T(8,128)} %broadcast_add_fusion), calls=%async_computation.3 | async-start | bytes 2097152 | tf_op jit(solution)/shard_map/all_to_all | solution.py:202
Sparse Core Ops, SparseCore 0:
  19.6 55.3 all-gather.2
  87.6 37.1 reduce-scatter.1

commit v14 on v12

--- a/solution.py
+++ b/solution.py
@@ -70,6 +70,7 @@
     for step in range(len(starts)):
         for copy in copies(step):
             copy.start()
+    outs = []
     for step, (first_row, end_row) in enumerate(zip(starts, ends, strict=True)):
         for copy in copies(step):
             copy.wait()
@@ -93,9 +94,11 @@
                             start = pl.ds(pl.multiple_of((z * NX + true_x) * 16, 16), 16)
                             end = pl.ds(pl.multiple_of((true_x * NZ + z) * 16, 16), 16)
                             sums[end, columns] = total[start, columns] + part[row : row + 16]
-    copy = pltpu.make_async_copy(sums, out_hbm, out_sem)
-    copy.start()
-    copy.wait()
+                    block = 2 * p + place
+                    outs.append(pltpu.make_async_copy(sums.at[:, columns], out_hbm.at[:, columns], out_sem.at[block]))
+                    outs[-1].start()
+    for copy in outs:
+        copy.wait()
 
 
 def first(own_x, own_screen, other_screen, coef, rests, own, other):
@@ -121,7 +124,7 @@
             pltpu.SemaphoreType.DMA((NX,)),
             sems,
             sems,
-            pltpu.SemaphoreType.DMA,
+            pltpu.SemaphoreType.DMA((2 * aux,)),
         ],
         compiler_params=pltpu.CompilerParams(vmem_limit_bytes=56 * 2**20),
         cost_estimate=pl.CostEstimate(flops=0, bytes_accessed=0, transcendentals=0),
@@ -187,7 +190,7 @@
     along_x = gather(coef[:, :most], "x")
     gathered = lax.all_gather(along_x.reshape(NX * occ, most), "z", axis=0, tiled=True)
 
-    along_z = gather(coef[:, most:] + 0.0 * along_x[0, :, :REST], "z")
+    along_z = gather(coef[:, most:], "z")
     rests = shifts(along_z, "x")
 
     along_y = gather(coef + 0.0 * jnp.pad(along_z[0], ((0, 0), (0, most))), "y")

time: 166 us -> 166 us (level)
  no operation moved by 1% of the time
where the time goes in v14:
time: 166 us; the launch traced here: 162 us
  blocking collectives  59.8 us (36%)
  waiting for transfers between devices  37.5 us (23%)
  starting transfers between devices  33.1 us (20%)
  between operations  13.6 us (8%)
  Pallas kernels  13.3 us (8%)
  other arithmetic  3.05 us (2%)
  local copies, waits for them, and re-layouts  2.1 us (1%)
    reduce_scatter x1, waiting for transfers between devices, shards(): half = lax.psum_scatter(products, 'y', scatter_dimension=0, tiled=True)  30.2 us
    all_to_all x2, blocking collectives, gather(): return lax.all_to_all(copies, axis, 0, 0, tiled=True)  29.4 us
    all_to_all x1, blocking collectives, shards(): pairs = lax.all_to_all(pairs, ('x', 'z'), 0, 0, tiled=True)  24 us
    ppermute x2, starting transfers between devices, swap(): return lax.ppermute(value, 'core', [(0, 1), (1, 0)])  11.8 us
    pallas_call x1, Pallas kernels, first(): pl.pallas_call(first_kernel, out_shape=jax.ShapeDtypeStruct((occ, width),...  11 us
    ppermute x3, starting transfers between devices, shifts(): lax.ppermute(value, axis, [(i, (i + step) % count) for i in range(count)])  8.41 us
    all_to_all x1, starting transfers between devices, gather(): return lax.all_to_all(copies, axis, 0, 0, tiled=True)  7.1 us
    all_gather x1, blocking collectives, shards(): lax.all_gather(half, 'core')  6.5 us
  transfers between devices with their start and end apart: 9, of which 5 were waited for; matrix products, arithmetic and copies ran while one was open for 2% of the time, Pallas kernels for 7%

profile of v14, /device:TPU:1, one launch (start us, length us, event | category | flops | bytes accessed | tf_op | source)
XLA Modules:
  0.0 162.5 jit_solution(7156960295511668791)
XLA Ops:
  6.5 0.0 copy-start
  6.5 0.0 copy-start.2
  6.5 0.0 all-gather.3.cloned.1.call-start
  6.6 0.7 copy-done
  7.2 0.2 compare_reduce_fusion
  7.4 0.1 broadcast_bitcast_fusion
  7.5 0.9 multiply_bitcast_fusion
  8.4 0.0 copy-start.8
  8.5 11.0 %all_to_all.25 = f32[4,16,1536]{2,1,0:T(8,128)} all-to-all(f32[4,16,1536]{2,1,0:T(8,128)S(1)} %broadcast_in_dim.14), channel_id=1, replica_groups=mesh['y'=8,'x'=4,'z'=8,'core'=2] {'x'}, dimensions={0} | all-to-all | bytes 786432 | tf_op jit(solution)/shard_map/all_to_all | solution.py:26
  19.5 0.0 all-gather.3.cloned.1.call-update
  19.5 8.3 %collective-permute-start.4 = (f32[2,2048,256]{2,1,0:T(8,128)}, f32[2,2048,256]{2,1,0:T(8,128)}, u32[]{:S(2)}, u32[]{:S(2)}) collective-permute-start(f32[2,2048,256]{2,1,0:T(8,128)} %own_hbm.1), channel_id=1, source_target_pairs={{0,1},{1,0},{2,3},{3,2},{4,5},{5,4},{6,7},{7,6},{8,9},{9,8},{10,11... | collective-permute-start | bytes 12582920 | tf_op jit(solution)/shard_map/ppermute | solution.py:21
  27.8 18.4 %all_to_all.26.rest_0 = f32[8,16,512]{2,1,0:T(8,128)S(1)} all-to-all(f32[8,16,512]{2,1,0:T(8,128)S(1)} %broadcast_in_dim.11), channel_id=1, replica_groups=mesh['y'=8,'x'=4,'z'=8,'core'=2] {'z'}, dimensions={0} | all-to-all | bytes 524288 | tf_op jit(solution)/shard_map/all_to_all | solution.py:26
  46.2 0.0 copy-start.1
  46.2 0.0 copy-done.2
  46.2 1.1 broadcast_in_dim.12
  47.3 7.1 %all-to-all-start.1 = ((f32[8,16,2048]{2,1,0:T(8,128)}), f32[8,16,2048]{2,1,0:T(8,128)S(1)}, u32[]{:S(2)}, u32[]{:S(2)}) async-start(f32[8,16,2048]{2,1,0:T(8,128)} %broadcast_in_dim.12), calls=%async_computation.1 | async-start | bytes 2097152 | tf_op jit(solution)/shard_map/all_to_all | solution.py:26
  54.4 0.0 reduce-scatter.2.cloned.1.call-start
  54.5 1.9 %collective-permute-start.1 = (f32[8,16,512]{2,1,0:T(8,128)S(1)}, f32[8,16,512]{2,1,0:T(8,128)S(1)}, u32[]{:S(2)}, u32[]{:S(2)}) collective-permute-start(f32[8,16,512]{2,1,0:T(8,128)S(1)} %all_to_all.26.rest_0), channel_id=1, source_target_pairs={{0,16},{16,32},{32,48},{48,0},{1,17},{17,33},{33,49},{49,1},{2,18}... | collective-permute-start | bytes 786440 | tf_op jit(solution)/shard_map/ppermute | solution.py:31
  56.4 3.9 %collective-permute-start.2 = (f32[8,16,512]{2,1,0:T(8,128)S(1)}, f32[8,16,512]{2,1,0:T(8,128)S(1)}, u32[]{:S(2)}, u32[]{:S(2)}) collective-permute-start(f32[8,16,512]{2,1,0:T(8,128)S(1)} %all_to_all.26.rest_0), channel_id=1, source_target_pairs={{0,32},{16,48},{32,0},{48,16},{1,33},{17,49},{33,1},{49,17},{2,34}... | collective-permute-start | bytes 786440 | tf_op jit(solution)/shard_map/ppermute | solution.py:31
  60.3 2.6 %collective-permute-start.3 = (f32[8,16,512]{2,1,0:T(8,128)S(1)}, f32[8,16,512]{2,1,0:T(8,128)S(1)}, u32[]{:S(2)}, u32[]{:S(2)}) collective-permute-start(f32[8,16,512]{2,1,0:T(8,128)S(1)} %all_to_all.26.rest_0), channel_id=1, source_target_pairs={{0,48},{16,0},{32,16},{48,32},{1,49},{17,1},{33,17},{49,33},{2,50}... | collective-permute-start | bytes 786440 | tf_op jit(solution)/shard_map/ppermute | solution.py:31
  62.9 0.0 copy-done.8
  62.9 0.1 copy.8.own_screen
  63.0 0.0 copy-start.6
  63.0 3.5 %collective-permute-start = (s32[16,2]{1,0:T(8,128)S(1)}, s32[16,2]{1,0:T(8,128)S(1)}, u32[]{:S(2)}, u32[]{:S(2)}) collective-permute-start(s32[16,2]{1,0:T(8,128)S(1)} %copy.8.own_screen), channel_id=1, source_target_pairs={{0,1},{1,0},{2,3},{3,2},{4,5},{5,4},{6,7},{7,6},{8,9},{9,8},{10,11... | collective-permute-start | bytes 392 | tf_op jit(solution)/shard_map/ppermute | solution.py:21
  66.5 0.8 collective-permute-done.other_screen
  67.3 0.0 copy-start.7
  67.3 0.0 collective-permute-done.1.rest_1
  67.3 0.0 copy-start.3
  67.3 2.3 %collective-permute-done.2.rest_2 = f32[8,16,512]{2,1,0:T(8,128)S(1)} collective-permute-done((f32[8,16,512]{2,1,0:T(8,128)S(1)}, f32[8,16,512]{2,1,0:T(8,128)S(1)}, u32[]{:S(2)}, u32[]{:S(2)}) %collective-permute-start.2) | collective-permute-done | bytes 262176 | tf_op jit(solution)/shard_map/ppermute | solution.py:31
  69.6 0.0 copy-start.4
  69.6 3.3 %collective-permute-done.3.rest_3 = f32[8,16,512]{2,1,0:T(8,128)S(1)} collective-permute-done((f32[8,16,512]{2,1,0:T(8,128)S(1)}, f32[8,16,512]{2,1,0:T(8,128)S(1)}, u32[]{:S(2)}, u32[]{:S(2)}) %collective-permute-start.3) | collective-permute-done | bytes 262176 | tf_op jit(solution)/shard_map/ppermute | solution.py:31
  72.9 0.0 copy-start.5
  72.9 0.0 collective-permute-done.4.other_hbm
  72.9 0.9 all-gather.3.cloned.1.call-done.coef_hbm
  73.8 0.0 copy-done.1
  73.8 0.0 copy-done.6
  73.8 0.0 copy-done.7
  73.8 0.0 copy-done.3
  73.8 0.0 copy-done.4
  73.8 0.0 copy-done.5
  73.8 11.0 %shard_map.46 = f32[512,1024]{1,0:T(8,128)} custom-call(s32[1]{0:T(128)} %bitcast.5.own_x, s32[16,2]{1,0:T(8,128)} %copy-done.6, s32[16,2]{1,0:T(8,128)} %copy-done.7, f32[512,1536]{1,0:T(8,128)} %all-gather.3.cloned.1.call-done.coef_hbm, f32[8,16,512]{2,1,0:T(8,128)} %copy-done.1, f32[8,16,512]{2,1,0:T(8,128)} %copy-done.3, f32[8,16,512]{2,1,0:T(8,128)} %copy-done.4, ...), custom_call_target="tpu_custom_call" | custom-call | tf_op jit(solution)/shard_map/pallas_call | solution.py:111
  84.8 0.0 reduce-scatter.2.cloned.1.call-update
  84.9 0.0 all-to-all-done.1
  84.9 0.1 fusion
  85.0 0.1 pad_maximum_fusion
  85.0 0.8 slice_multiply_fusion
  85.8 1.1 broadcast_add_fusion
  86.9 5.8 %all-to-all-start.3 = ((f32[32,16,512]{2,1,0:T(8,128)}), f32[32,16,512]{2,1,0:T(8,128)S(1)}, u32[]{:S(2)}, u32[]{:S(2)}) async-start(f32[32,16,512]{2,1,0:T(8,128)} %broadcast_add_fusion), calls=%async_computation.3 | async-start | bytes 2097152 | tf_op jit(solution)/shard_map/all_to_all | solution.py:205
  92.7 30.2 %reduce-scatter.2.cloned.1.call-done = f32[64,1024]{1,0:T(8,128)} async-done(((f32[512,1024]{1,0:T(8,128)}), f32[64,1024]{1,0:T(8,128)}) %reduce-scatter.2.cloned.1.call-update) | async-done | bytes 262160 | tf_op jit(solution)/shard_map/reduce_scatter | solution.py:200
  122.9 6.5 %all-gather = f32[128,1024]{1,0:T(8,128)S(1)} all-gather(f32[64,1024]{1,0:T(8,128)} %reduce-scatter.2.cloned.1.call-done), channel_id=2, replica_groups=mesh['y'=8,'x'=4,'z'=8,'core'=2] {'core'}, dimensions={0}, use_global_device_ids=true | all-gather | bytes 786432 | tf_op jit(solution)/shard_map/all_gather | solution.py:206
  129.4 0.0 all-to-all-done.3
  129.4 0.6 shard_map.47
  130.0 24.0 %all_to_all.27.parts_ref = f32[32,16,256]{2,1,0:T(8,128)} all-to-all(f32[32,16,256]{2,1,0:T(8,128)S(1)} %bitcast.19), channel_id=1, replica_groups=mesh['y'=8,'x'=4,'z'=8,'core'=2] {'x','z'}, dimensions={0} | all-to-all | bytes 1048576 | tf_op jit(solution)/shard_map/all_to_all | solution.py:208
  153.9 1.7 %shard_map.48 = f32[2,16,128]{2,1,0:T(8,128)} custom-call(f32[32,16,256]{2,1,0:T(8,128)} %all_to_all.27.parts_ref), custom_call_target="tpu_custom_call" | custom-call | tf_op jit(solution)/shard_map/pallas_call | solution.py:171
  (9 shorter events, 0.1 us)
Async XLA Ops:
  6.5 0.7 copy-start
  6.5 39.7 %copy-start.2 = (f32[2048,16]{0,1:T(8,128)S(1)}, f32[2048,16]{0,1:T(8,128)}, u32[]{:S(2)}) copy-start(f32[2048,16]{0,1:T(8,128)} %param.5) | copy-start | bytes 393220
  6.5 67.2 %all-gather.3.cloned.1.call-start = ((), (), s32[]{:S(2)}) async-start(), calls=%async_computation.6 | async-start | bytes 3538944 | tf_op jit(solution)/shard_map/all_gather | solution.py:191
  8.4 54.5 %copy-start.8 = (s32[16,2]{0,1:T(2,128)S(1)}, s32[16,2]{0,1:T(2,128)}, u32[]{:S(2)}) copy-start(s32[16,2]{0,1:T(2,128)} %param.6) | copy-start | bytes 388
  19.5 53.4 %collective-permute-start.4 = (f32[2,2048,256]{2,1,0:T(8,128)}, f32[2,2048,256]{2,1,0:T(8,128)}, u32[]{:S(2)}, u32[]{:S(2)}) collective-permute-start(f32[2,2048,256]{2,1,0:T(8,128)} %own_hbm.1), channel_id=1, source_target_pairs={{0,1},{1,0},{2,3},{3,2},{4,5},{5,4},{6,7},{7,6},{8,9},{9,8},{10,11... | collective-permute-start | bytes 12582920 | tf_op jit(solution)/shard_map/ppermute | solution.py:21
  46.2 27.6 %copy-start.1 = (f32[8,16,512]{2,1,0:T(8,128)}, f32[8,16,512]{2,1,0:T(8,128)S(1)}, u32[]{:S(2)}) copy-start(f32[8,16,512]{2,1,0:T(8,128)S(1)} %all_to_all.26.rest_0) | copy-start | bytes 786436
  47.3 37.5 %all-to-all-start.1 = ((f32[8,16,2048]{2,1,0:T(8,128)}), f32[8,16,2048]{2,1,0:T(8,128)S(1)}, u32[]{:S(2)}, u32[]{:S(2)}) async-start(f32[8,16,2048]{2,1,0:T(8,128)} %broadcast_in_dim.12), calls=%async_computation.1 | async-start | bytes 2097152 | tf_op jit(solution)/shard_map/all_to_all | solution.py:26
  54.4 68.4 %reduce-scatter.2.cloned.1.call-start = ((), (), s32[]{:S(2)}) async-start(), calls=%async_computation.7 | async-start | bytes 2359296 | tf_op jit(solution)/shard_map/reduce_scatter | solution.py:200
  54.5 12.8 %collective-permute-start.1 = (f32[8,16,512]{2,1,0:T(8,128)S(1)}, f32[8,16,512]{2,1,0:T(8,128)S(1)}, u32[]{:S(2)}, u32[]{:S(2)}) collective-permute-start(f32[8,16,512]{2,1,0:T(8,128)S(1)} %all_to_all.26.rest_0), channel_id=1, source_target_pairs={{0,16},{16,32},{32,48},{48,0},{1,17},{17,33},{33,49},{49,1},{2,18}... | collective-permute-start | bytes 786440 | tf_op jit(solution)/shard_map/ppermute | solution.py:31
  56.4 13.2 %collective-permute-start.2 = (f32[8,16,512]{2,1,0:T(8,128)S(1)}, f32[8,16,512]{2,1,0:T(8,128)S(1)}, u32[]{:S(2)}, u32[]{:S(2)}) collective-permute-start(f32[8,16,512]{2,1,0:T(8,128)S(1)} %all_to_all.26.rest_0), channel_id=1, source_target_pairs={{0,32},{16,48},{32,0},{48,16},{1,33},{17,49},{33,1},{49,17},{2,34}... | collective-permute-start | bytes 786440 | tf_op jit(solution)/shard_map/ppermute | solution.py:31
  60.3 12.6 %collective-permute-start.3 = (f32[8,16,512]{2,1,0:T(8,128)S(1)}, f32[8,16,512]{2,1,0:T(8,128)S(1)}, u32[]{:S(2)}, u32[]{:S(2)}) collective-permute-start(f32[8,16,512]{2,1,0:T(8,128)S(1)} %all_to_all.26.rest_0), channel_id=1, source_target_pairs={{0,48},{16,0},{32,16},{48,32},{1,49},{17,1},{33,17},{49,33},{2,50}... | collective-permute-start | bytes 786440 | tf_op jit(solution)/shard_map/ppermute | solution.py:31
  63.0 10.8 %copy-start.6 = (s32[16,2]{1,0:T(8,128)}, s32[16,2]{1,0:T(8,128)S(1)}, u32[]{:S(2)}) copy-start(s32[16,2]{1,0:T(8,128)S(1)} %copy.8.own_screen) | copy-start | bytes 388
  63.0 4.3 %collective-permute-start = (s32[16,2]{1,0:T(8,128)S(1)}, s32[16,2]{1,0:T(8,128)S(1)}, u32[]{:S(2)}, u32[]{:S(2)}) collective-permute-start(s32[16,2]{1,0:T(8,128)S(1)} %copy.8.own_screen), channel_id=1, source_target_pairs={{0,1},{1,0},{2,3},{3,2},{4,5},{5,4},{6,7},{7,6},{8,9},{9,8},{10,11... | collective-permute-start | bytes 392 | tf_op jit(solution)/shard_map/ppermute | solution.py:21
  67.3 6.5 %copy-start.7 = (s32[16,2]{1,0:T(8,128)}, s32[16,2]{1,0:T(8,128)S(1)}, u32[]{:S(2)}) copy-start(s32[16,2]{1,0:T(8,128)S(1)} %collective-permute-done.other_screen) | copy-start | bytes 388
  67.3 6.5 %copy-start.3 = (f32[8,16,512]{2,1,0:T(8,128)}, f32[8,16,512]{2,1,0:T(8,128)S(1)}, u32[]{:S(2)}) copy-start(f32[8,16,512]{2,1,0:T(8,128)S(1)} %collective-permute-done.1.rest_1) | copy-start | bytes 786436
  69.6 4.2 %copy-start.4 = (f32[8,16,512]{2,1,0:T(8,128)}, f32[8,16,512]{2,1,0:T(8,128)S(1)}, u32[]{:S(2)}) copy-start(f32[8,16,512]{2,1,0:T(8,128)S(1)} %collective-permute-done.2.rest_2) | copy-start | bytes 786436
  72.9 0.9 copy-start.5
  86.9 42.5 %all-to-all-start.3 = ((f32[32,16,512]{2,1,0:T(8,128)}), f32[32,16,512]{2,1,0:T(8,128)S(1)}, u32[]{:S(2)}, u32[]{:S(2)}) async-start(f32[32,16,512]{2,1,0:T(8,128)} %broadcast_add_fusion), calls=%async_computation.3 | async-start | bytes 2097152 | tf_op jit(solution)/shard_map/all_to_all | solution.py:205
Sparse Core Ops, SparseCore 0:
  19.6 54.1 all-gather.2
  85.0 37.8 reduce-scatter.1

commit v15 on v14

--- a/solution.py
+++ b/solution.py
@@ -171,6 +171,8 @@
     return pl.pallas_call(
         last_kernel,
         out_shape=jax.ShapeDtypeStruct((2, parts.shape[1], parts.shape[2] // 2), F32),
+        in_specs=[pl.BlockSpec(memory_space=pltpu.VMEM)],
+        compiler_params=pltpu.CompilerParams(vmem_limit_bytes=8 * 2**20),
     )(parts)
 
 

time: 166 us -> 164 us (0.988)
  no operation moved by 1% of the time
where the time goes in v15:
time: 164 us; the launch traced here: 161 us
  blocking collectives  59.7 us (36%)
  waiting for transfers between devices  37.5 us (23%)
  starting transfers between devices  33.1 us (20%)
  between operations  13.6 us (8%)
  Pallas kernels  12.3 us (8%)
  other arithmetic  3.05 us (2%)
  local copies, waits for them, and re-layouts  2.1 us (1%)
    reduce_scatter x1, waiting for transfers between devices, shards(): half = lax.psum_scatter(products, 'y', scatter_dimension=0, tiled=True)  30.2 us
    all_to_all x2, blocking collectives, gather(): return lax.all_to_all(copies, axis, 0, 0, tiled=True)  29.4 us
    all_to_all x1, blocking collectives, shards(): pairs = lax.all_to_all(pairs, ('x', 'z'), 0, 0, tiled=True)  23.9 us
    ppermute x2, starting transfers between devices, swap(): return lax.ppermute(value, 'core', [(0, 1), (1, 0)])  11.8 us
    pallas_call x1, Pallas kernels, first(): pl.pallas_call(first_kernel, out_shape=jax.ShapeDtypeStruct((occ, width),...  11 us
    ppermute x3, starting transfers between devices, shifts(): lax.ppermute(value, axis, [(i, (i + step) % count) for i in range(count)])  8.41 us
    all_to_all x1, starting transfers between devices, gather(): return lax.all_to_all(copies, axis, 0, 0, tiled=True)  7.1 us
    all_gather x1, blocking collectives, shards(): lax.all_gather(half, 'core')  6.5 us
  transfers between devices with their start and end apart: 9, of which 5 were waited for; matrix products, arithmetic and copies ran while one was open for 2% of the time, Pallas kernels for 7%

profile of v15, /device:TPU:1, one launch (start us, length us, event | category | flops | bytes accessed | tf_op | source)
XLA Modules:
  0.0 161.3 jit_solution(15632003649352602881)
XLA Ops:
  6.5 0.0 copy-start
  6.5 0.0 copy-start.2
  6.5 0.0 all-gather.3.cloned.1.call-start
  6.6 0.7 copy-done
  7.2 0.2 compare_reduce_fusion
  7.4 0.1 broadcast_bitcast_fusion
  7.5 0.9 multiply_bitcast_fusion
  8.4 0.0 copy-start.8
  8.5 11.0 %all_to_all.25 = f32[4,16,1536]{2,1,0:T(8,128)} all-to-all(f32[4,16,1536]{2,1,0:T(8,128)S(1)} %broadcast_in_dim.14), channel_id=1, replica_groups=mesh['y'=8,'x'=4,'z'=8,'core'=2] {'x'}, dimensions={0} | all-to-all | bytes 786432 | tf_op jit(solution)/shard_map/all_to_all | solution.py:26
  19.5 0.0 all-gather.3.cloned.1.call-update
  19.5 8.3 %collective-permute-start.4 = (f32[2,2048,256]{2,1,0:T(8,128)}, f32[2,2048,256]{2,1,0:T(8,128)}, u32[]{:S(2)}, u32[]{:S(2)}) collective-permute-start(f32[2,2048,256]{2,1,0:T(8,128)} %own_hbm.1), channel_id=1, source_target_pairs={{0,1},{1,0},{2,3},{3,2},{4,5},{5,4},{6,7},{7,6},{8,9},{9,8},{10,11... | collective-permute-start | bytes 12582920 | tf_op jit(solution)/shard_map/ppermute | solution.py:21
  27.8 18.4 %all_to_all.26.rest_0 = f32[8,16,512]{2,1,0:T(8,128)S(1)} all-to-all(f32[8,16,512]{2,1,0:T(8,128)S(1)} %broadcast_in_dim.11), channel_id=1, replica_groups=mesh['y'=8,'x'=4,'z'=8,'core'=2] {'z'}, dimensions={0} | all-to-all | bytes 524288 | tf_op jit(solution)/shard_map/all_to_all | solution.py:26
  46.2 0.0 copy-start.1
  46.2 0.0 copy-done.2
  46.2 1.1 broadcast_in_dim.12
  47.3 7.1 %all-to-all-start.1 = ((f32[8,16,2048]{2,1,0:T(8,128)}), f32[8,16,2048]{2,1,0:T(8,128)S(1)}, u32[]{:S(2)}, u32[]{:S(2)}) async-start(f32[8,16,2048]{2,1,0:T(8,128)} %broadcast_in_dim.12), calls=%async_computation.1 | async-start | bytes 2097152 | tf_op jit(solution)/shard_map/all_to_all | solution.py:26
  54.4 0.0 reduce-scatter.2.cloned.1.call-start
  54.5 1.9 %collective-permute-start.1 = (f32[8,16,512]{2,1,0:T(8,128)S(1)}, f32[8,16,512]{2,1,0:T(8,128)S(1)}, u32[]{:S(2)}, u32[]{:S(2)}) collective-permute-start(f32[8,16,512]{2,1,0:T(8,128)S(1)} %all_to_all.26.rest_0), channel_id=1, source_target_pairs={{0,16},{16,32},{32,48},{48,0},{1,17},{17,33},{33,49},{49,1},{2,18}... | collective-permute-start | bytes 786440 | tf_op jit(solution)/shard_map/ppermute | solution.py:31
  56.4 3.9 %collective-permute-start.2 = (f32[8,16,512]{2,1,0:T(8,128)S(1)}, f32[8,16,512]{2,1,0:T(8,128)S(1)}, u32[]{:S(2)}, u32[]{:S(2)}) collective-permute-start(f32[8,16,512]{2,1,0:T(8,128)S(1)} %all_to_all.26.rest_0), channel_id=1, source_target_pairs={{0,32},{16,48},{32,0},{48,16},{1,33},{17,49},{33,1},{49,17},{2,34}... | collective-permute-start | bytes 786440 | tf_op jit(solution)/shard_map/ppermute | solution.py:31
  60.3 2.6 %collective-permute-start.3 = (f32[8,16,512]{2,1,0:T(8,128)S(1)}, f32[8,16,512]{2,1,0:T(8,128)S(1)}, u32[]{:S(2)}, u32[]{:S(2)}) collective-permute-start(f32[8,16,512]{2,1,0:T(8,128)S(1)} %all_to_all.26.rest_0), channel_id=1, source_target_pairs={{0,48},{16,0},{32,16},{48,32},{1,49},{17,1},{33,17},{49,33},{2,50}... | collective-permute-start | bytes 786440 | tf_op jit(solution)/shard_map/ppermute | solution.py:31
  62.9 0.0 copy-done.8
  62.9 0.1 copy.8.own_screen
  63.0 0.0 copy-start.6
  63.0 3.5 %collective-permute-start = (s32[16,2]{1,0:T(8,128)S(1)}, s32[16,2]{1,0:T(8,128)S(1)}, u32[]{:S(2)}, u32[]{:S(2)}) collective-permute-start(s32[16,2]{1,0:T(8,128)S(1)} %copy.8.own_screen), channel_id=1, source_target_pairs={{0,1},{1,0},{2,3},{3,2},{4,5},{5,4},{6,7},{7,6},{8,9},{9,8},{10,11... | collective-permute-start | bytes 392 | tf_op jit(solution)/shard_map/ppermute | solution.py:21
  66.5 0.8 collective-permute-done.other_screen
  67.3 0.0 copy-start.7
  67.3 0.0 collective-permute-done.1.rest_1
  67.3 0.0 copy-start.3
  67.3 2.3 %collective-permute-done.2.rest_2 = f32[8,16,512]{2,1,0:T(8,128)S(1)} collective-permute-done((f32[8,16,512]{2,1,0:T(8,128)S(1)}, f32[8,16,512]{2,1,0:T(8,128)S(1)}, u32[]{:S(2)}, u32[]{:S(2)}) %collective-permute-start.2) | collective-permute-done | bytes 262176 | tf_op jit(solution)/shard_map/ppermute | solution.py:31
  69.6 0.0 copy-start.4
  69.6 3.3 %collective-permute-done.3.rest_3 = f32[8,16,512]{2,1,0:T(8,128)S(1)} collective-permute-done((f32[8,16,512]{2,1,0:T(8,128)S(1)}, f32[8,16,512]{2,1,0:T(8,128)S(1)}, u32[]{:S(2)}, u32[]{:S(2)}) %collective-permute-start.3) | collective-permute-done | bytes 262176 | tf_op jit(solution)/shard_map/ppermute | solution.py:31
  72.9 0.0 copy-start.5
  72.9 0.0 collective-permute-done.4.other_hbm
  72.9 0.9 all-gather.3.cloned.1.call-done.coef_hbm
  73.8 0.0 copy-done.1
  73.8 0.0 copy-done.6
  73.8 0.0 copy-done.7
  73.8 0.0 copy-done.3
  73.8 0.0 copy-done.4
  73.8 0.0 copy-done.5
  73.8 11.0 %shard_map.46 = f32[512,1024]{1,0:T(8,128)} custom-call(s32[1]{0:T(128)} %bitcast.5.own_x, s32[16,2]{1,0:T(8,128)} %copy-done.6, s32[16,2]{1,0:T(8,128)} %copy-done.7, f32[512,1536]{1,0:T(8,128)} %all-gather.3.cloned.1.call-done.coef_hbm, f32[8,16,512]{2,1,0:T(8,128)} %copy-done.1, f32[8,16,512]{2,1,0:T(8,128)} %copy-done.3, f32[8,16,512]{2,1,0:T(8,128)} %copy-done.4, ...), custom_call_target="tpu_custom_call" | custom-call | tf_op jit(solution)/shard_map/pallas_call | solution.py:111
  84.8 0.0 reduce-scatter.2.cloned.1.call-update
  84.9 0.0 all-to-all-done.1
  84.9 0.1 fusion
  85.0 0.1 pad_maximum_fusion
  85.0 0.8 slice_multiply_fusion
  85.8 1.1 broadcast_add_fusion
  86.9 5.8 %all-to-all-start.3 = ((f32[32,16,512]{2,1,0:T(8,128)}), f32[32,16,512]{2,1,0:T(8,128)S(1)}, u32[]{:S(2)}, u32[]{:S(2)}) async-start(f32[32,16,512]{2,1,0:T(8,128)} %broadcast_add_fusion), calls=%async_computation.3 | async-start | bytes 2097152 | tf_op jit(solution)/shard_map/all_to_all | solution.py:207
  92.7 30.2 %reduce-scatter.2.cloned.1.call-done = f32[64,1024]{1,0:T(8,128)} async-done(((f32[512,1024]{1,0:T(8,128)}), f32[64,1024]{1,0:T(8,128)}) %reduce-scatter.2.cloned.1.call-update) | async-done | bytes 262160 | tf_op jit(solution)/shard_map/reduce_scatter | solution.py:202
  122.9 6.5 %all-gather = f32[128,1024]{1,0:T(8,128)S(1)} all-gather(f32[64,1024]{1,0:T(8,128)} %reduce-scatter.2.cloned.1.call-done), channel_id=2, replica_groups=mesh['y'=8,'x'=4,'z'=8,'core'=2] {'core'}, dimensions={0}, use_global_device_ids=true | all-gather | bytes 786432 | tf_op jit(solution)/shard_map/all_gather | solution.py:208
  129.4 0.0 all-to-all-done.3
  129.4 0.6 shard_map.47
  130.0 23.9 %all_to_all.27.parts_ref = f32[32,16,256]{2,1,0:T(8,128)S(1)} all-to-all(f32[32,16,256]{2,1,0:T(8,128)S(1)} %bitcast.19), channel_id=1, replica_groups=mesh['y'=8,'x'=4,'z'=8,'core'=2] {'x','z'}, dimensions={0} | all-to-all | bytes 1048576 | tf_op jit(solution)/shard_map/all_to_all | solution.py:210
  153.8 0.7 shard_map.48
  (9 shorter events, 0.1 us)
Async XLA Ops:
  6.5 0.7 copy-start
  6.5 39.7 %copy-start.2 = (f32[2048,16]{0,1:T(8,128)S(1)}, f32[2048,16]{0,1:T(8,128)}, u32[]{:S(2)}) copy-start(f32[2048,16]{0,1:T(8,128)} %param.5) | copy-start | bytes 393220
  6.5 67.2 %all-gather.3.cloned.1.call-start = ((), (), s32[]{:S(2)}) async-start(), calls=%async_computation.6 | async-start | bytes 3538944 | tf_op jit(solution)/shard_map/all_gather | solution.py:193
  8.4 54.5 %copy-start.8 = (s32[16,2]{0,1:T(2,128)S(1)}, s32[16,2]{0,1:T(2,128)}, u32[]{:S(2)}) copy-start(s32[16,2]{0,1:T(2,128)} %param.6) | copy-start | bytes 388
  19.5 53.4 %collective-permute-start.4 = (f32[2,2048,256]{2,1,0:T(8,128)}, f32[2,2048,256]{2,1,0:T(8,128)}, u32[]{:S(2)}, u32[]{:S(2)}) collective-permute-start(f32[2,2048,256]{2,1,0:T(8,128)} %own_hbm.1), channel_id=1, source_target_pairs={{0,1},{1,0},{2,3},{3,2},{4,5},{5,4},{6,7},{7,6},{8,9},{9,8},{10,11... | collective-permute-start | bytes 12582920 | tf_op jit(solution)/shard_map/ppermute | solution.py:21
  46.2 27.6 %copy-start.1 = (f32[8,16,512]{2,1,0:T(8,128)}, f32[8,16,512]{2,1,0:T(8,128)S(1)}, u32[]{:S(2)}) copy-start(f32[8,16,512]{2,1,0:T(8,128)S(1)} %all_to_all.26.rest_0) | copy-start | bytes 786436
  47.3 37.5 %all-to-all-start.1 = ((f32[8,16,2048]{2,1,0:T(8,128)}), f32[8,16,2048]{2,1,0:T(8,128)S(1)}, u32[]{:S(2)}, u32[]{:S(2)}) async-start(f32[8,16,2048]{2,1,0:T(8,128)} %broadcast_in_dim.12), calls=%async_computation.1 | async-start | bytes 2097152 | tf_op jit(solution)/shard_map/all_to_all | solution.py:26
  54.4 68.4 %reduce-scatter.2.cloned.1.call-start = ((), (), s32[]{:S(2)}) async-start(), calls=%async_computation.7 | async-start | bytes 2359296 | tf_op jit(solution)/shard_map/reduce_scatter | solution.py:202
  54.5 12.8 %collective-permute-start.1 = (f32[8,16,512]{2,1,0:T(8,128)S(1)}, f32[8,16,512]{2,1,0:T(8,128)S(1)}, u32[]{:S(2)}, u32[]{:S(2)}) collective-permute-start(f32[8,16,512]{2,1,0:T(8,128)S(1)} %all_to_all.26.rest_0), channel_id=1, source_target_pairs={{0,16},{16,32},{32,48},{48,0},{1,17},{17,33},{33,49},{49,1},{2,18}... | collective-permute-start | bytes 786440 | tf_op jit(solution)/shard_map/ppermute | solution.py:31
  56.4 13.2 %collective-permute-start.2 = (f32[8,16,512]{2,1,0:T(8,128)S(1)}, f32[8,16,512]{2,1,0:T(8,128)S(1)}, u32[]{:S(2)}, u32[]{:S(2)}) collective-permute-start(f32[8,16,512]{2,1,0:T(8,128)S(1)} %all_to_all.26.rest_0), channel_id=1, source_target_pairs={{0,32},{16,48},{32,0},{48,16},{1,33},{17,49},{33,1},{49,17},{2,34}... | collective-permute-start | bytes 786440 | tf_op jit(solution)/shard_map/ppermute | solution.py:31
  60.3 12.6 %collective-permute-start.3 = (f32[8,16,512]{2,1,0:T(8,128)S(1)}, f32[8,16,512]{2,1,0:T(8,128)S(1)}, u32[]{:S(2)}, u32[]{:S(2)}) collective-permute-start(f32[8,16,512]{2,1,0:T(8,128)S(1)} %all_to_all.26.rest_0), channel_id=1, source_target_pairs={{0,48},{16,0},{32,16},{48,32},{1,49},{17,1},{33,17},{49,33},{2,50}... | collective-permute-start | bytes 786440 | tf_op jit(solution)/shard_map/ppermute | solution.py:31
  63.0 10.8 %copy-start.6 = (s32[16,2]{1,0:T(8,128)}, s32[16,2]{1,0:T(8,128)S(1)}, u32[]{:S(2)}) copy-start(s32[16,2]{1,0:T(8,128)S(1)} %copy.8.own_screen) | copy-start | bytes 388
  63.0 4.3 %collective-permute-start = (s32[16,2]{1,0:T(8,128)S(1)}, s32[16,2]{1,0:T(8,128)S(1)}, u32[]{:S(2)}, u32[]{:S(2)}) collective-permute-start(s32[16,2]{1,0:T(8,128)S(1)} %copy.8.own_screen), channel_id=1, source_target_pairs={{0,1},{1,0},{2,3},{3,2},{4,5},{5,4},{6,7},{7,6},{8,9},{9,8},{10,11... | collective-permute-start | bytes 392 | tf_op jit(solution)/shard_map/ppermute | solution.py:21
  67.3 6.5 %copy-start.7 = (s32[16,2]{1,0:T(8,128)}, s32[16,2]{1,0:T(8,128)S(1)}, u32[]{:S(2)}) copy-start(s32[16,2]{1,0:T(8,128)S(1)} %collective-permute-done.other_screen) | copy-start | bytes 388
  67.3 6.5 %copy-start.3 = (f32[8,16,512]{2,1,0:T(8,128)}, f32[8,16,512]{2,1,0:T(8,128)S(1)}, u32[]{:S(2)}) copy-start(f32[8,16,512]{2,1,0:T(8,128)S(1)} %collective-permute-done.1.rest_1) | copy-start | bytes 786436
  69.6 4.2 %copy-start.4 = (f32[8,16,512]{2,1,0:T(8,128)}, f32[8,16,512]{2,1,0:T(8,128)S(1)}, u32[]{:S(2)}) copy-start(f32[8,16,512]{2,1,0:T(8,128)S(1)} %collective-permute-done.2.rest_2) | copy-start | bytes 786436
  72.9 0.9 copy-start.5
  86.9 42.5 %all-to-all-start.3 = ((f32[32,16,512]{2,1,0:T(8,128)}), f32[32,16,512]{2,1,0:T(8,128)S(1)}, u32[]{:S(2)}, u32[]{:S(2)}) async-start(f32[32,16,512]{2,1,0:T(8,128)} %broadcast_add_fusion), calls=%async_computation.3 | async-start | bytes 2097152 | tf_op jit(solution)/shard_map/all_to_all | solution.py:207
Sparse Core Ops, SparseCore 0:
  19.6 54.1 all-gather.2
  85.0 37.8 reduce-scatter.1

commit v16 on v15

--- a/solution.py
+++ b/solution.py
@@ -7,7 +7,8 @@
 
 TILE = 128
 NX, NZ = 4, 8
-REST, CHUNK = 512, 256
+REST = 512
+STARTS = 0, 256, 768
 BF16 = jnp.bfloat16
 F32 = jnp.float32
 
@@ -39,7 +40,7 @@
     rests = rest_0, rest_1, rest_2, rest_3
     aux, full_depth, width = own.shape
     most = coef.shape[1]
-    starts = [*range(0, most, CHUNK), most]
+    starts = [*STARTS, most]
     ends = [*starts[1:], full_depth]
 
     def copies(step):
@@ -104,7 +105,7 @@
 def first(own_x, own_screen, other_screen, coef, rests, own, other):
     occ, most = coef.shape
     aux, full_depth, half_width = own.shape
-    steps = -(-most // CHUNK) + 1
+    steps = len(STARTS) + 1
     width = 2 * aux * half_width
     away, scalars = pl.BlockSpec(memory_space=pl.ANY), pl.BlockSpec(memory_space=pltpu.SMEM)
     sems = pltpu.SemaphoreType.DMA((steps,))

time: 164 us -> 164 us (level)
  no operation moved by 1% of the time
where the time goes in v16:
time: 164 us; the launch traced here: 161 us
  blocking collectives  59.8 us (36%)
  waiting for transfers between devices  37.4 us (23%)
  starting transfers between devices  33.1 us (20%)
  between operations  13.6 us (8%)
  Pallas kernels  12.3 us (8%)
  other arithmetic  3.05 us (2%)
  local copies, waits for them, and re-layouts  2.1 us (1%)
    reduce_scatter x1, waiting for transfers between devices, shards(): half = lax.psum_scatter(products, 'y', scatter_dimension=0, tiled=True)  30.1 us
    all_to_all x2, blocking collectives, gather(): return lax.all_to_all(copies, axis, 0, 0, tiled=True)  29.4 us
    all_to_all x1, blocking collectives, shards(): pairs = lax.all_to_all(pairs, ('x', 'z'), 0, 0, tiled=True)  23.9 us
    ppermute x2, starting transfers between devices, swap(): return lax.ppermute(value, 'core', [(0, 1), (1, 0)])  11.8 us
    pallas_call x1, Pallas kernels, first(): pl.pallas_call(first_kernel, out_shape=jax.ShapeDtypeStruct((occ, width),...  11 us
    ppermute x3, starting transfers between devices, shifts(): lax.ppermute(value, axis, [(i, (i + step) % count) for i in range(count)])  8.41 us
    all_to_all x1, starting transfers between devices, gather(): return lax.all_to_all(copies, axis, 0, 0, tiled=True)  7.1 us
    all_gather x1, blocking collectives, shards(): lax.all_gather(half, 'core')  6.47 us
  transfers between devices with their start and end apart: 9, of which 5 were waited for; matrix products, arithmetic and copies ran while one was open for 2% of the time, Pallas kernels for 7%

profile of v16, /device:TPU:1, one launch (start us, length us, event | category | flops | bytes accessed | tf_op | source)
XLA Modules:
  0.0 161.3 jit_solution(9620916078386965519)
XLA Ops:
  6.5 0.0 copy-start
  6.5 0.0 copy-start.2
  6.5 0.0 all-gather.3.cloned.1.call-start
  6.6 0.7 copy-done
  7.2 0.2 compare_reduce_fusion
  7.4 0.1 broadcast_bitcast_fusion
  7.5 0.9 multiply_bitcast_fusion
  8.4 0.0 copy-start.8
  8.5 11.0 %all_to_all.25 = f32[4,16,1536]{2,1,0:T(8,128)} all-to-all(f32[4,16,1536]{2,1,0:T(8,128)S(1)} %broadcast_in_dim.14), channel_id=1, replica_groups=mesh['y'=8,'x'=4,'z'=8,'core'=2] {'x'}, dimensions={0} | all-to-all | bytes 786432 | tf_op jit(solution)/shard_map/all_to_all | solution.py:27
  19.5 0.0 all-gather.3.cloned.1.call-update
  19.5 8.3 %collective-permute-start.4 = (f32[2,2048,256]{2,1,0:T(8,128)}, f32[2,2048,256]{2,1,0:T(8,128)}, u32[]{:S(2)}, u32[]{:S(2)}) collective-permute-start(f32[2,2048,256]{2,1,0:T(8,128)} %own_hbm.1), channel_id=1, source_target_pairs={{0,1},{1,0},{2,3},{3,2},{4,5},{5,4},{6,7},{7,6},{8,9},{9,8},{10,11... | collective-permute-start | bytes 12582920 | tf_op jit(solution)/shard_map/ppermute | solution.py:22
  27.8 18.4 %all_to_all.26.rest_0 = f32[8,16,512]{2,1,0:T(8,128)S(1)} all-to-all(f32[8,16,512]{2,1,0:T(8,128)S(1)} %broadcast_in_dim.11), channel_id=1, replica_groups=mesh['y'=8,'x'=4,'z'=8,'core'=2] {'z'}, dimensions={0} | all-to-all | bytes 524288 | tf_op jit(solution)/shard_map/all_to_all | solution.py:27
  46.2 0.0 copy-start.1
  46.2 0.0 copy-done.2
  46.2 1.1 broadcast_in_dim.12
  47.3 7.1 %all-to-all-start.1 = ((f32[8,16,2048]{2,1,0:T(8,128)}), f32[8,16,2048]{2,1,0:T(8,128)S(1)}, u32[]{:S(2)}, u32[]{:S(2)}) async-start(f32[8,16,2048]{2,1,0:T(8,128)} %broadcast_in_dim.12), calls=%async_computation.1 | async-start | bytes 2097152 | tf_op jit(solution)/shard_map/all_to_all | solution.py:27
  54.4 0.0 reduce-scatter.2.cloned.1.call-start
  54.5 1.9 %collective-permute-start.1 = (f32[8,16,512]{2,1,0:T(8,128)S(1)}, f32[8,16,512]{2,1,0:T(8,128)S(1)}, u32[]{:S(2)}, u32[]{:S(2)}) collective-permute-start(f32[8,16,512]{2,1,0:T(8,128)S(1)} %all_to_all.26.rest_0), channel_id=1, source_target_pairs={{0,16},{16,32},{32,48},{48,0},{1,17},{17,33},{33,49},{49,1},{2,18}... | collective-permute-start | bytes 786440 | tf_op jit(solution)/shard_map/ppermute | solution.py:32
  56.4 3.9 %collective-permute-start.2 = (f32[8,16,512]{2,1,0:T(8,128)S(1)}, f32[8,16,512]{2,1,0:T(8,128)S(1)}, u32[]{:S(2)}, u32[]{:S(2)}) collective-permute-start(f32[8,16,512]{2,1,0:T(8,128)S(1)} %all_to_all.26.rest_0), channel_id=1, source_target_pairs={{0,32},{16,48},{32,0},{48,16},{1,33},{17,49},{33,1},{49,17},{2,34}... | collective-permute-start | bytes 786440 | tf_op jit(solution)/shard_map/ppermute | solution.py:32
  60.3 2.6 %collective-permute-start.3 = (f32[8,16,512]{2,1,0:T(8,128)S(1)}, f32[8,16,512]{2,1,0:T(8,128)S(1)}, u32[]{:S(2)}, u32[]{:S(2)}) collective-permute-start(f32[8,16,512]{2,1,0:T(8,128)S(1)} %all_to_all.26.rest_0), channel_id=1, source_target_pairs={{0,48},{16,0},{32,16},{48,32},{1,49},{17,1},{33,17},{49,33},{2,50}... | collective-permute-start | bytes 786440 | tf_op jit(solution)/shard_map/ppermute | solution.py:32
  62.9 0.0 copy-done.8
  62.9 0.1 copy.8.own_screen
  63.0 0.0 copy-start.6
  63.0 3.5 %collective-permute-start = (s32[16,2]{1,0:T(8,128)S(1)}, s32[16,2]{1,0:T(8,128)S(1)}, u32[]{:S(2)}, u32[]{:S(2)}) collective-permute-start(s32[16,2]{1,0:T(8,128)S(1)} %copy.8.own_screen), channel_id=1, source_target_pairs={{0,1},{1,0},{2,3},{3,2},{4,5},{5,4},{6,7},{7,6},{8,9},{9,8},{10,11... | collective-permute-start | bytes 392 | tf_op jit(solution)/shard_map/ppermute | solution.py:22
  66.5 0.8 collective-permute-done.other_screen
  67.3 0.0 copy-start.7
  67.3 0.0 collective-permute-done.1.rest_1
  67.3 0.0 copy-start.3
  67.3 2.3 %collective-permute-done.2.rest_2 = f32[8,16,512]{2,1,0:T(8,128)S(1)} collective-permute-done((f32[8,16,512]{2,1,0:T(8,128)S(1)}, f32[8,16,512]{2,1,0:T(8,128)S(1)}, u32[]{:S(2)}, u32[]{:S(2)}) %collective-permute-start.2) | collective-permute-done | bytes 262176 | tf_op jit(solution)/shard_map/ppermute | solution.py:32
  69.6 0.0 copy-start.4
  69.6 3.3 %collective-permute-done.3.rest_3 = f32[8,16,512]{2,1,0:T(8,128)S(1)} collective-permute-done((f32[8,16,512]{2,1,0:T(8,128)S(1)}, f32[8,16,512]{2,1,0:T(8,128)S(1)}, u32[]{:S(2)}, u32[]{:S(2)}) %collective-permute-start.3) | collective-permute-done | bytes 262176 | tf_op jit(solution)/shard_map/ppermute | solution.py:32
  72.9 0.0 copy-start.5
  72.9 0.0 collective-permute-done.4.other_hbm
  72.9 0.9 all-gather.3.cloned.1.call-done.coef_hbm
  73.8 0.0 copy-done.1
  73.8 0.0 copy-done.6
  73.8 0.0 copy-done.7
  73.8 0.0 copy-done.3
  73.8 0.0 copy-done.4
  73.8 0.0 copy-done.5
  73.8 11.0 %shard_map.46 = f32[512,1024]{1,0:T(8,128)} custom-call(s32[1]{0:T(128)} %bitcast.5.own_x, s32[16,2]{1,0:T(8,128)} %copy-done.6, s32[16,2]{1,0:T(8,128)} %copy-done.7, f32[512,1536]{1,0:T(8,128)} %all-gather.3.cloned.1.call-done.coef_hbm, f32[8,16,512]{2,1,0:T(8,128)} %copy-done.1, f32[8,16,512]{2,1,0:T(8,128)} %copy-done.3, f32[8,16,512]{2,1,0:T(8,128)} %copy-done.4, ...), custom_call_target="tpu_custom_call" | custom-call | tf_op jit(solution)/shard_map/pallas_call | solution.py:112
  84.8 0.0 reduce-scatter.2.cloned.1.call-update
  84.8 0.0 all-to-all-done.1
  84.8 0.1 fusion
  84.9 0.1 pad_maximum_fusion
  85.0 0.8 slice_multiply_fusion
  85.8 1.1 broadcast_add_fusion
  86.9 5.8 %all-to-all-start.3 = ((f32[32,16,512]{2,1,0:T(8,128)}), f32[32,16,512]{2,1,0:T(8,128)S(1)}, u32[]{:S(2)}, u32[]{:S(2)}) async-start(f32[32,16,512]{2,1,0:T(8,128)} %broadcast_add_fusion), calls=%async_computation.3 | async-start | bytes 2097152 | tf_op jit(solution)/shard_map/all_to_all | solution.py:208
  92.7 30.1 %reduce-scatter.2.cloned.1.call-done = f32[64,1024]{1,0:T(8,128)} async-done(((f32[512,1024]{1,0:T(8,128)}), f32[64,1024]{1,0:T(8,128)}) %reduce-scatter.2.cloned.1.call-update) | async-done | bytes 262160 | tf_op jit(solution)/shard_map/reduce_scatter | solution.py:203
  122.8 6.5 %all-gather = f32[128,1024]{1,0:T(8,128)S(1)} all-gather(f32[64,1024]{1,0:T(8,128)} %reduce-scatter.2.cloned.1.call-done), channel_id=2, replica_groups=mesh['y'=8,'x'=4,'z'=8,'core'=2] {'core'}, dimensions={0}, use_global_device_ids=true | all-gather | bytes 786432 | tf_op jit(solution)/shard_map/all_gather | solution.py:209
  129.3 0.0 all-to-all-done.3
  129.3 0.6 shard_map.47
  129.9 23.9 %all_to_all.27.parts_ref = f32[32,16,256]{2,1,0:T(8,128)S(1)} all-to-all(f32[32,16,256]{2,1,0:T(8,128)S(1)} %bitcast.19), channel_id=1, replica_groups=mesh['y'=8,'x'=4,'z'=8,'core'=2] {'x','z'}, dimensions={0} | all-to-all | bytes 1048576 | tf_op jit(solution)/shard_map/all_to_all | solution.py:211
  153.8 0.7 shard_map.48
  (9 shorter events, 0.1 us)
Async XLA Ops:
  6.5 0.7 copy-start
  6.5 39.7 %copy-start.2 = (f32[2048,16]{0,1:T(8,128)S(1)}, f32[2048,16]{0,1:T(8,128)}, u32[]{:S(2)}) copy-start(f32[2048,16]{0,1:T(8,128)} %param.5) | copy-start | bytes 393220
  6.5 67.2 %all-gather.3.cloned.1.call-start = ((), (), s32[]{:S(2)}) async-start(), calls=%async_computation.6 | async-start | bytes 3538944 | tf_op jit(solution)/shard_map/all_gather | solution.py:194
  8.4 54.5 %copy-start.8 = (s32[16,2]{0,1:T(2,128)S(1)}, s32[16,2]{0,1:T(2,128)}, u32[]{:S(2)}) copy-start(s32[16,2]{0,1:T(2,128)} %param.6) | copy-start | bytes 388
  19.5 53.4 %collective-permute-start.4 = (f32[2,2048,256]{2,1,0:T(8,128)}, f32[2,2048,256]{2,1,0:T(8,128)}, u32[]{:S(2)}, u32[]{:S(2)}) collective-permute-start(f32[2,2048,256]{2,1,0:T(8,128)} %own_hbm.1), channel_id=1, source_target_pairs={{0,1},{1,0},{2,3},{3,2},{4,5},{5,4},{6,7},{7,6},{8,9},{9,8},{10,11... | collective-permute-start | bytes 12582920 | tf_op jit(solution)/shard_map/ppermute | solution.py:22
  46.2 27.6 %copy-start.1 = (f32[8,16,512]{2,1,0:T(8,128)}, f32[8,16,512]{2,1,0:T(8,128)S(1)}, u32[]{:S(2)}) copy-start(f32[8,16,512]{2,1,0:T(8,128)S(1)} %all_to_all.26.rest_0) | copy-start | bytes 786436
  47.3 37.5 %all-to-all-start.1 = ((f32[8,16,2048]{2,1,0:T(8,128)}), f32[8,16,2048]{2,1,0:T(8,128)S(1)}, u32[]{:S(2)}, u32[]{:S(2)}) async-start(f32[8,16,2048]{2,1,0:T(8,128)} %broadcast_in_dim.12), calls=%async_computation.1 | async-start | bytes 2097152 | tf_op jit(solution)/shard_map/all_to_all | solution.py:27
  54.4 68.4 %reduce-scatter.2.cloned.1.call-start = ((), (), s32[]{:S(2)}) async-start(), calls=%async_computation.7 | async-start | bytes 2359296 | tf_op jit(solution)/shard_map/reduce_scatter | solution.py:203
  54.5 12.8 %collective-permute-start.1 = (f32[8,16,512]{2,1,0:T(8,128)S(1)}, f32[8,16,512]{2,1,0:T(8,128)S(1)}, u32[]{:S(2)}, u32[]{:S(2)}) collective-permute-start(f32[8,16,512]{2,1,0:T(8,128)S(1)} %all_to_all.26.rest_0), channel_id=1, source_target_pairs={{0,16},{16,32},{32,48},{48,0},{1,17},{17,33},{33,49},{49,1},{2,18}... | collective-permute-start | bytes 786440 | tf_op jit(solution)/shard_map/ppermute | solution.py:32
  56.4 13.2 %collective-permute-start.2 = (f32[8,16,512]{2,1,0:T(8,128)S(1)}, f32[8,16,512]{2,1,0:T(8,128)S(1)}, u32[]{:S(2)}, u32[]{:S(2)}) collective-permute-start(f32[8,16,512]{2,1,0:T(8,128)S(1)} %all_to_all.26.rest_0), channel_id=1, source_target_pairs={{0,32},{16,48},{32,0},{48,16},{1,33},{17,49},{33,1},{49,17},{2,34}... | collective-permute-start | bytes 786440 | tf_op jit(solution)/shard_map/ppermute | solution.py:32
  60.3 12.6 %collective-permute-start.3 = (f32[8,16,512]{2,1,0:T(8,128)S(1)}, f32[8,16,512]{2,1,0:T(8,128)S(1)}, u32[]{:S(2)}, u32[]{:S(2)}) collective-permute-start(f32[8,16,512]{2,1,0:T(8,128)S(1)} %all_to_all.26.rest_0), channel_id=1, source_target_pairs={{0,48},{16,0},{32,16},{48,32},{1,49},{17,1},{33,17},{49,33},{2,50}... | collective-permute-start | bytes 786440 | tf_op jit(solution)/shard_map/ppermute | solution.py:32
  63.0 10.8 %copy-start.6 = (s32[16,2]{1,0:T(8,128)}, s32[16,2]{1,0:T(8,128)S(1)}, u32[]{:S(2)}) copy-start(s32[16,2]{1,0:T(8,128)S(1)} %copy.8.own_screen) | copy-start | bytes 388
  63.0 4.3 %collective-permute-start = (s32[16,2]{1,0:T(8,128)S(1)}, s32[16,2]{1,0:T(8,128)S(1)}, u32[]{:S(2)}, u32[]{:S(2)}) collective-permute-start(s32[16,2]{1,0:T(8,128)S(1)} %copy.8.own_screen), channel_id=1, source_target_pairs={{0,1},{1,0},{2,3},{3,2},{4,5},{5,4},{6,7},{7,6},{8,9},{9,8},{10,11... | collective-permute-start | bytes 392 | tf_op jit(solution)/shard_map/ppermute | solution.py:22
  67.3 6.5 %copy-start.7 = (s32[16,2]{1,0:T(8,128)}, s32[16,2]{1,0:T(8,128)S(1)}, u32[]{:S(2)}) copy-start(s32[16,2]{1,0:T(8,128)S(1)} %collective-permute-done.other_screen) | copy-start | bytes 388
  67.3 6.5 %copy-start.3 = (f32[8,16,512]{2,1,0:T(8,128)}, f32[8,16,512]{2,1,0:T(8,128)S(1)}, u32[]{:S(2)}) copy-start(f32[8,16,512]{2,1,0:T(8,128)S(1)} %collective-permute-done.1.rest_1) | copy-start | bytes 786436
  69.6 4.2 %copy-start.4 = (f32[8,16,512]{2,1,0:T(8,128)}, f32[8,16,512]{2,1,0:T(8,128)S(1)}, u32[]{:S(2)}) copy-start(f32[8,16,512]{2,1,0:T(8,128)S(1)} %collective-permute-done.2.rest_2) | copy-start | bytes 786436
  72.9 0.9 copy-start.5
  86.9 42.4 %all-to-all-start.3 = ((f32[32,16,512]{2,1,0:T(8,128)}), f32[32,16,512]{2,1,0:T(8,128)S(1)}, u32[]{:S(2)}, u32[]{:S(2)}) async-start(f32[32,16,512]{2,1,0:T(8,128)} %broadcast_add_fusion), calls=%async_computation.3 | async-start | bytes 2097152 | tf_op jit(solution)/shard_map/all_to_all | solution.py:208
Sparse Core Ops, SparseCore 0:
  19.6 54.1 all-gather.2
  84.9 37.8 reduce-scatter.1

commit v17 on v16

--- a/solution.py
+++ b/solution.py
@@ -7,7 +7,7 @@
 
 TILE = 128
 NX, NZ = 4, 8
-REST = 512
+REST = 384
 STARTS = 0, 256, 768
 BF16 = jnp.bfloat16
 F32 = jnp.float32

time: 164 us -> 168 us (1.024)
  waiting for transfers between devices: 37.4 us -> 39.8 us
    all_gather x1, waiting for transfers between devices: 0.86 us -> 7.3 us  [shards(): lax.all_gather(along_x.reshape(NX * occ, most), 'z', axis=0, tiled=True)]
    ppermute x3, waiting for transfers between devices: 5.58 us -> 1.6 us  [shifts(): lax.ppermute(value, axis, [(i, (i + step) % count) for i in range(count)])]
  transfers between devices with their start and end apart: 9 -> 9, of which waited for: 5 -> 4; matrix products, arithmetic and copies ran while one was open for 2% -> 3% of each run, Pallas kernels for 7% -> 7%
where the time goes in v17:
time: 168 us; the launch traced here: 165 us
  blocking collectives  58.8 us (35%)
  waiting for transfers between devices  39.8 us (24%)
  starting transfers between devices  33.5 us (20%)
  between operations  13.6 us (8%)
  Pallas kernels  13 us (8%)
  other arithmetic  4.03 us (2%)
  local copies, waits for them, and re-layouts  2.11 us (1%)
    reduce_scatter x1, waiting for transfers between devices, shards(): half = lax.psum_scatter(products, 'y', scatter_dimension=0, tiled=True)  30.1 us
    all_to_all x2, blocking collectives, gather(): return lax.all_to_all(copies, axis, 0, 0, tiled=True)  28.4 us
    all_to_all x1, blocking collectives, shards(): pairs = lax.all_to_all(pairs, ('x', 'z'), 0, 0, tiled=True)  23.9 us
    ppermute x2, starting transfers between devices, swap(): return lax.ppermute(value, 'core', [(0, 1), (1, 0)])  11.9 us
    pallas_call x1, Pallas kernels, first(): pl.pallas_call(first_kernel, out_shape=jax.ShapeDtypeStruct((occ, width),...  11.7 us
    ppermute x3, starting transfers between devices, shifts(): lax.ppermute(value, axis, [(i, (i + step) % count) for i in range(count)])  8.78 us
    all_gather x1, waiting for transfers between devices, shards(): lax.all_gather(along_x.reshape(NX * occ, most), 'z', axis=0, tiled=True)  7.3 us
    all_to_all x1, starting transfers between devices, gather(): return lax.all_to_all(copies, axis, 0, 0, tiled=True)  6.64 us
  transfers between devices with their start and end apart: 9, of which 4 were waited for; matrix products, arithmetic and copies ran while one was open for 3% of the time, Pallas kernels for 7%

profile of v17, /device:TPU:1, one launch (start us, length us, event | category | flops | bytes accessed | tf_op | source)
XLA Modules:
  0.0 164.9 jit_solution(1524491914040216055)
XLA Ops:
  6.5 0.0 copy-start
  6.5 0.0 copy-start.7
  6.5 0.0 all-gather.3.cloned.1.call-start
  6.6 0.7 copy-done
  7.2 0.2 compare_reduce_fusion
  7.4 0.1 broadcast_bitcast_fusion
  7.5 0.9 multiply_bitcast_fusion
  8.5 11.2 %all_to_all.25 = f32[4,16,1664]{2,1,0:T(8,128)} all-to-all(f32[4,16,1664]{2,1,0:T(8,128)S(1)} %broadcast_in_dim.14), channel_id=1, replica_groups=mesh['y'=8,'x'=4,'z'=8,'core'=2] {'x'}, dimensions={0} | all-to-all | bytes 851968 | tf_op jit(solution)/shard_map/all_to_all | solution.py:27
  19.6 0.0 all-gather.3.cloned.1.call-update
  19.7 8.3 %collective-permute-start.4 = (f32[2,2048,256]{2,1,0:T(8,128)}, f32[2,2048,256]{2,1,0:T(8,128)}, u32[]{:S(2)}, u32[]{:S(2)}) collective-permute-start(f32[2,2048,256]{2,1,0:T(8,128)} %own_hbm.1), channel_id=1, source_target_pairs={{0,1},{1,0},{2,3},{3,2},{4,5},{5,4},{6,7},{7,6},{8,9},{9,8},{10,11... | collective-permute-start | bytes 12582920 | tf_op jit(solution)/shard_map/ppermute | solution.py:22
  28.0 17.3 %all_to_all.26.rest_0 = f32[8,16,384]{2,1,0:T(8,128)S(1)} all-to-all(f32[8,16,384]{2,1,0:T(8,128)S(1)} %broadcast_in_dim.11), channel_id=1, replica_groups=mesh['y'=8,'x'=4,'z'=8,'core'=2] {'z'}, dimensions={0} | all-to-all | bytes 393216 | tf_op jit(solution)/shard_map/all_to_all | solution.py:27
  45.2 0.0 copy-start.1
  45.2 1.0 multiply_add_fusion
  46.2 1.1 broadcast_in_dim.12
  47.3 6.6 %all-to-all-start.1 = ((f32[8,16,2048]{2,1,0:T(8,128)}), f32[8,16,2048]{2,1,0:T(8,128)S(1)}, u32[]{:S(2)}, u32[]{:S(2)}) async-start(f32[8,16,2048]{2,1,0:T(8,128)} %broadcast_in_dim.12), calls=%async_computation.1 | async-start | bytes 2097152 | tf_op jit(solution)/shard_map/all_to_all | solution.py:27
  54.0 0.0 reduce-scatter.2.cloned.1.call-start
  54.0 2.4 %collective-permute-start.1 = (f32[8,16,384]{2,1,0:T(8,128)S(1)}, f32[8,16,384]{2,1,0:T(8,128)S(1)}, u32[]{:S(2)}, u32[]{:S(2)}) collective-permute-start(f32[8,16,384]{2,1,0:T(8,128)S(1)} %all_to_all.26.rest_0), channel_id=1, source_target_pairs={{0,16},{16,32},{32,48},{48,0},{1,17},{17,33},{33,49},{49,1},{2,18}... | collective-permute-start | bytes 589832 | tf_op jit(solution)/shard_map/ppermute | solution.py:32
  56.4 3.7 %collective-permute-start.2 = (f32[8,16,384]{2,1,0:T(8,128)S(1)}, f32[8,16,384]{2,1,0:T(8,128)S(1)}, u32[]{:S(2)}, u32[]{:S(2)}) collective-permute-start(f32[8,16,384]{2,1,0:T(8,128)S(1)} %all_to_all.26.rest_0), channel_id=1, source_target_pairs={{0,32},{16,48},{32,0},{48,16},{1,33},{17,49},{33,1},{49,17},{2,34}... | collective-permute-start | bytes 589832 | tf_op jit(solution)/shard_map/ppermute | solution.py:32
  60.1 2.7 %collective-permute-start.3 = (f32[8,16,384]{2,1,0:T(8,128)S(1)}, f32[8,16,384]{2,1,0:T(8,128)S(1)}, u32[]{:S(2)}, u32[]{:S(2)}) collective-permute-start(f32[8,16,384]{2,1,0:T(8,128)S(1)} %all_to_all.26.rest_0), channel_id=1, source_target_pairs={{0,48},{16,0},{32,16},{48,32},{1,49},{17,1},{33,17},{49,33},{2,50}... | collective-permute-start | bytes 589832 | tf_op jit(solution)/shard_map/ppermute | solution.py:32
  62.8 0.0 copy-done.7
  62.8 0.1 copy.8.own_screen
  62.9 0.0 copy-start.5
  62.9 3.7 %collective-permute-start = (s32[16,2]{1,0:T(8,128)S(1)}, s32[16,2]{1,0:T(8,128)S(1)}, u32[]{:S(2)}, u32[]{:S(2)}) collective-permute-start(s32[16,2]{1,0:T(8,128)S(1)} %copy.8.own_screen), channel_id=1, source_target_pairs={{0,1},{1,0},{2,3},{3,2},{4,5},{5,4},{6,7},{7,6},{8,9},{9,8},{10,11... | collective-permute-start | bytes 392 | tf_op jit(solution)/shard_map/ppermute | solution.py:22
  66.6 0.8 collective-permute-done.other_screen
  67.4 0.0 copy-start.6
  67.4 0.0 collective-permute-done.1.rest_1
  67.4 0.0 copy-start.2
  67.4 0.0 collective-permute-done.2.rest_2
  67.4 0.0 copy-start.3
  67.4 1.6 collective-permute-done.3.rest_3
  69.0 0.0 copy-start.4
  69.0 0.0 collective-permute-done.4.other_hbm
  69.0 7.3 %all-gather.3.cloned.1.call-done.coef_hbm = f32[512,1664]{1,0:T(8,128)} async-done(((f32[64,1664]{1,0:T(8,128)}), f32[512,1664]{1,0:T(8,128)}) %all-gather.3.cloned.1.call-update) | async-done | bytes 3407888 | tf_op jit(solution)/shard_map/all_gather | solution.py:194
  76.3 0.0 copy-done.1
  76.3 0.0 copy-done.5
  76.3 0.0 copy-done.6
  76.3 0.0 copy-done.2
  76.3 0.0 copy-done.3
  76.3 0.0 copy-done.4
  76.3 11.7 %shard_map.46 = f32[512,1024]{1,0:T(8,128)} custom-call(s32[1]{0:T(128)} %bitcast.5.own_x, s32[16,2]{1,0:T(8,128)} %copy-done.5, s32[16,2]{1,0:T(8,128)} %copy-done.6, f32[512,1664]{1,0:T(8,128)} %all-gather.3.cloned.1.call-done.coef_hbm, f32[8,16,384]{2,1,0:T(8,128)} %copy-done.1, f32[8,16,384]{2,1,0:T(8,128)} %copy-done.2, f32[8,16,384]{2,1,0:T(8,128)} %copy-done.3, ...), custom_call_target="tpu_custom_call" | custom-call | tf_op jit(solution)/shard_map/pallas_call | solution.py:112
  88.1 0.0 reduce-scatter.2.cloned.1.call-update
  88.1 0.0 all-to-all-done.1
  88.1 0.1 fusion
  88.2 0.1 pad_maximum_fusion
  88.3 0.8 slice_multiply_fusion
  89.1 1.1 broadcast_add_fusion
  90.2 6.1 %all-to-all-start.3 = ((f32[32,16,512]{2,1,0:T(8,128)}), f32[32,16,512]{2,1,0:T(8,128)S(1)}, u32[]{:S(2)}, u32[]{:S(2)}) async-start(f32[32,16,512]{2,1,0:T(8,128)} %broadcast_add_fusion), calls=%async_computation.3 | async-start | bytes 2097152 | tf_op jit(solution)/shard_map/all_to_all | solution.py:208
  96.3 30.1 %reduce-scatter.2.cloned.1.call-done = f32[64,1024]{1,0:T(8,128)} async-done(((f32[512,1024]{1,0:T(8,128)}), f32[64,1024]{1,0:T(8,128)}) %reduce-scatter.2.cloned.1.call-update) | async-done | bytes 262160 | tf_op jit(solution)/shard_map/reduce_scatter | solution.py:203
  126.4 6.5 %all-gather = f32[128,1024]{1,0:T(8,128)S(1)} all-gather(f32[64,1024]{1,0:T(8,128)} %reduce-scatter.2.cloned.1.call-done), channel_id=2, replica_groups=mesh['y'=8,'x'=4,'z'=8,'core'=2] {'core'}, dimensions={0}, use_global_device_ids=true | all-gather | bytes 786432 | tf_op jit(solution)/shard_map/all_gather | solution.py:209
  132.9 0.0 all-to-all-done.3
  132.9 0.6 shard_map.47
  133.5 23.9 %all_to_all.27.parts_ref = f32[32,16,256]{2,1,0:T(8,128)S(1)} all-to-all(f32[32,16,256]{2,1,0:T(8,128)S(1)} %bitcast.19), channel_id=1, replica_groups=mesh['y'=8,'x'=4,'z'=8,'core'=2] {'x','z'}, dimensions={0} | all-to-all | bytes 1048576 | tf_op jit(solution)/shard_map/all_to_all | solution.py:211
  157.4 0.7 shard_map.48
  (8 shorter events, 0.1 us)
Async XLA Ops:
  6.5 0.7 copy-start
  6.5 56.3 %copy-start.7 = (s32[16,2]{0,1:T(2,128)S(1)}, s32[16,2]{0,1:T(2,128)}, u32[]{:S(2)}) copy-start(s32[16,2]{0,1:T(2,128)} %param.6) | copy-start | bytes 388
  6.5 69.8 %all-gather.3.cloned.1.call-start = ((), (), s32[]{:S(2)}) async-start(), calls=%async_computation.6 | async-start | bytes 3833856 | tf_op jit(solution)/shard_map/all_gather | solution.py:194
  19.7 49.4 %collective-permute-start.4 = (f32[2,2048,256]{2,1,0:T(8,128)}, f32[2,2048,256]{2,1,0:T(8,128)}, u32[]{:S(2)}, u32[]{:S(2)}) collective-permute-start(f32[2,2048,256]{2,1,0:T(8,128)} %own_hbm.1), channel_id=1, source_target_pairs={{0,1},{1,0},{2,3},{3,2},{4,5},{5,4},{6,7},{7,6},{8,9},{9,8},{10,11... | collective-permute-start | bytes 12582920 | tf_op jit(solution)/shard_map/ppermute | solution.py:22
  45.2 31.1 %copy-start.1 = (f32[8,16,384]{2,1,0:T(8,128)}, f32[8,16,384]{2,1,0:T(8,128)S(1)}, u32[]{:S(2)}) copy-start(f32[8,16,384]{2,1,0:T(8,128)S(1)} %all_to_all.26.rest_0) | copy-start | bytes 589828
  47.3 40.8 %all-to-all-start.1 = ((f32[8,16,2048]{2,1,0:T(8,128)}), f32[8,16,2048]{2,1,0:T(8,128)S(1)}, u32[]{:S(2)}, u32[]{:S(2)}) async-start(f32[8,16,2048]{2,1,0:T(8,128)} %broadcast_in_dim.12), calls=%async_computation.1 | async-start | bytes 2097152 | tf_op jit(solution)/shard_map/all_to_all | solution.py:27
  54.0 72.4 %reduce-scatter.2.cloned.1.call-start = ((), (), s32[]{:S(2)}) async-start(), calls=%async_computation.7 | async-start | bytes 2359296 | tf_op jit(solution)/shard_map/reduce_scatter | solution.py:203
  54.0 13.4 %collective-permute-start.1 = (f32[8,16,384]{2,1,0:T(8,128)S(1)}, f32[8,16,384]{2,1,0:T(8,128)S(1)}, u32[]{:S(2)}, u32[]{:S(2)}) collective-permute-start(f32[8,16,384]{2,1,0:T(8,128)S(1)} %all_to_all.26.rest_0), channel_id=1, source_target_pairs={{0,16},{16,32},{32,48},{48,0},{1,17},{17,33},{33,49},{49,1},{2,18}... | collective-permute-start | bytes 589832 | tf_op jit(solution)/shard_map/ppermute | solution.py:32
  56.4 11.0 %collective-permute-start.2 = (f32[8,16,384]{2,1,0:T(8,128)S(1)}, f32[8,16,384]{2,1,0:T(8,128)S(1)}, u32[]{:S(2)}, u32[]{:S(2)}) collective-permute-start(f32[8,16,384]{2,1,0:T(8,128)S(1)} %all_to_all.26.rest_0), channel_id=1, source_target_pairs={{0,32},{16,48},{32,0},{48,16},{1,33},{17,49},{33,1},{49,17},{2,34}... | collective-permute-start | bytes 589832 | tf_op jit(solution)/shard_map/ppermute | solution.py:32
  60.1 8.9 %collective-permute-start.3 = (f32[8,16,384]{2,1,0:T(8,128)S(1)}, f32[8,16,384]{2,1,0:T(8,128)S(1)}, u32[]{:S(2)}, u32[]{:S(2)}) collective-permute-start(f32[8,16,384]{2,1,0:T(8,128)S(1)} %all_to_all.26.rest_0), channel_id=1, source_target_pairs={{0,48},{16,0},{32,16},{48,32},{1,49},{17,1},{33,17},{49,33},{2,50}... | collective-permute-start | bytes 589832 | tf_op jit(solution)/shard_map/ppermute | solution.py:32
  62.9 13.4 %copy-start.5 = (s32[16,2]{1,0:T(8,128)}, s32[16,2]{1,0:T(8,128)S(1)}, u32[]{:S(2)}) copy-start(s32[16,2]{1,0:T(8,128)S(1)} %copy.8.own_screen) | copy-start | bytes 388
  62.9 4.5 %collective-permute-start = (s32[16,2]{1,0:T(8,128)S(1)}, s32[16,2]{1,0:T(8,128)S(1)}, u32[]{:S(2)}, u32[]{:S(2)}) collective-permute-start(s32[16,2]{1,0:T(8,128)S(1)} %copy.8.own_screen), channel_id=1, source_target_pairs={{0,1},{1,0},{2,3},{3,2},{4,5},{5,4},{6,7},{7,6},{8,9},{9,8},{10,11... | collective-permute-start | bytes 392 | tf_op jit(solution)/shard_map/ppermute | solution.py:22
  67.4 8.9 %copy-start.6 = (s32[16,2]{1,0:T(8,128)}, s32[16,2]{1,0:T(8,128)S(1)}, u32[]{:S(2)}) copy-start(s32[16,2]{1,0:T(8,128)S(1)} %collective-permute-done.other_screen) | copy-start | bytes 388
  67.4 8.9 %copy-start.2 = (f32[8,16,384]{2,1,0:T(8,128)}, f32[8,16,384]{2,1,0:T(8,128)S(1)}, u32[]{:S(2)}) copy-start(f32[8,16,384]{2,1,0:T(8,128)S(1)} %collective-permute-done.1.rest_1) | copy-start | bytes 589828
  67.4 8.9 %copy-start.3 = (f32[8,16,384]{2,1,0:T(8,128)}, f32[8,16,384]{2,1,0:T(8,128)S(1)}, u32[]{:S(2)}) copy-start(f32[8,16,384]{2,1,0:T(8,128)S(1)} %collective-permute-done.2.rest_2) | copy-start | bytes 589828
  69.0 7.3 %copy-start.4 = (f32[8,16,384]{2,1,0:T(8,128)}, f32[8,16,384]{2,1,0:T(8,128)S(1)}, u32[]{:S(2)}) copy-start(f32[8,16,384]{2,1,0:T(8,128)S(1)} %collective-permute-done.3.rest_3) | copy-start | bytes 589828
  90.2 42.7 %all-to-all-start.3 = ((f32[32,16,512]{2,1,0:T(8,128)}), f32[32,16,512]{2,1,0:T(8,128)S(1)}, u32[]{:S(2)}, u32[]{:S(2)}) async-start(f32[32,16,512]{2,1,0:T(8,128)} %broadcast_add_fusion), calls=%async_computation.3 | async-start | bytes 2097152 | tf_op jit(solution)/shard_map/all_to_all | solution.py:208
Sparse Core Ops, SparseCore 0:
  19.8 56.4 all-gather.2
  88.2 38.0 reduce-scatter.1
